TPU v7x, 128 devices: a whole 4x4x4 slice. The times are simulated.
128 devices in a mesh: rep: 4 (over x), fsdp: 32 (over y, z, core).
Axes of the slice: x: 4, y: 4, z: 4, core: 2. Of those that a mesh axis runs over, the one named last changes fastest.
Arguments:
- tokens: bfloat16 [131072, 8192], P(('rep', 'fsdp')), may hold values from -6 to 6
- weight: bfloat16 [8192, 1024], P('fsdp'), may hold values from -0.0625 to 0.0625
- momentum: float32 [4, 8192, 1024], P('rep', 'fsdp'), may hold values from -6 to 6
- grad: float32 [4, 8192, 1024], P('rep', 'fsdp'), may hold values from -6 to 6
- selection: int32 [4, 128, 16, 64], replicated, may hold values from 0 to 4095, as said below
Outputs:
- keys: bfloat16 [131072, 1024], P(('rep', 'fsdp'))
- new_weight: bfloat16 [8192, 1024], P('fsdp')
- new_momentum: float32 [4, 8192, 1024], P('rep', 'fsdp')
Inputs may be any that keep to these rules, and one draw needn't show every extreme that they name: `selection`: within each replica's block the 64 indices are distinct.
All inputs are finite; a program needn't handle non-finite values.
Results may differ from a plain program's by a relative error of at most 0.0049.
Values may be sent and summed in bfloat16 or wider, within the bound.
No kernel may reach another device: no remote copies, remote signals or barrier semaphores. Data moves between devices by JAX's collectives and lax.ppermute only.
A program may use at most 384 MiB of HBM per device.

v0:
```python
import jax
import jax.numpy as jnp
from jax import lax
from jax.sharding import PartitionSpec as P

GROUP = 64
KEEP = 64


beta_decay = 0.999
step_rate = 0.05


def dct_matrix():
    freq = jnp.arange(GROUP, dtype=jnp.float32)[:, None]
    place = jnp.arange(GROUP, dtype=jnp.float32)[None, :]
    scale = jnp.where(freq == 0, jnp.sqrt(1.0 / GROUP), jnp.sqrt(2.0 / GROUP))
    return scale * jnp.cos(jnp.pi * (2.0 * place + 1.0) * freq / (2.0 * GROUP))


def to_groups(matrix):
    rows, cols = matrix.shape
    return matrix.reshape(rows // GROUP, GROUP, cols // GROUP, GROUP).transpose(0, 2, 1, 3)


def from_groups(blocks):
    nrow, ncol = (blocks.shape[0], blocks.shape[1])
    return blocks.transpose(0, 2, 1, 3).reshape(nrow * GROUP, ncol * GROUP)


def forward_dct(blocks, basis):
    inner = jnp.einsum("ij,abjk->abik", basis, blocks, precision=lax.Precision.HIGHEST)
    return jnp.einsum("abik,lk->abil", inner, basis, precision=lax.Precision.HIGHEST)


def basis_rows(which, basis):
    freqs = jnp.arange(GROUP, dtype=jnp.int32)
    onehot = (which[..., None] == freqs).astype(jnp.float32)
    return jnp.einsum("bkf,fn->bkn", onehot, basis, precision=lax.Precision.HIGHEST)


def decode_sparse(indices, values, basis):

    def one_row(pair):
        idx_row, val_row = pair
        left = basis_rows(idx_row // GROUP, basis)
        right = basis_rows(idx_row % GROUP, basis)
        scaled = right * val_row[..., None]
        return jnp.einsum("bki,bkl->bil", left, scaled, precision=lax.Precision.HIGHEST)

    blocks = lax.map(one_row, (indices, values))
    return from_groups(blocks)


def decode_all(indices, values, basis):
    replicas, nrow, ncol = (indices.shape[0], indices.shape[1], indices.shape[2])
    joint_idx = jnp.moveaxis(indices, 0, 2).reshape(nrow, ncol, replicas * KEEP)
    joint_val = jnp.moveaxis(values, 0, 2).reshape(nrow, ncol, replicas * KEEP)
    return decode_sparse(joint_idx, joint_val, basis)


def on_device(tokens, weight, momentum, grad, selection):
    basis = dct_matrix()
    shard_rows = weight.shape[0]
    block_rows = shard_rows // GROUP
    my_rows = lax.axis_index("fsdp") * block_rows
    own_blocks = lax.dynamic_slice_in_dim(selection, my_rows, block_rows, 1)
    own_sel = lax.dynamic_index_in_dim(own_blocks, lax.axis_index("rep"), 0, keepdims=False)
    moment = beta_decay * momentum[0] + grad[0]
    coeff = forward_dct(to_groups(moment), basis)
    coeff = coeff.reshape(coeff.shape[0], coeff.shape[1], GROUP * GROUP)
    chosen = jnp.take_along_axis(coeff, own_sel, axis=-1)
    own_part = decode_sparse(own_sel, chosen, basis)
    new_momentum = (moment - own_part)[None]
    everyone = lax.all_gather(chosen[None], "rep", axis=0, tiled=True)
    update = decode_all(own_blocks, everyone, basis)
    new_weight = (weight.astype(jnp.float32) - step_rate * update).astype(jnp.bfloat16)
    keys = jnp.dot(
        tokens,
        lax.all_gather(new_weight, "fsdp", axis=0, tiled=True),
        preferred_element_type=jnp.float32,
    )
    return (keys.astype(jnp.bfloat16), new_weight, new_momentum)


def solution(mesh):
    return jax.shard_map(
        on_device,
        mesh=mesh,
        in_specs=(
            P(("rep", "fsdp"), None),
            P("fsdp", None),
            P("rep", "fsdp", None),
            P("rep", "fsdp", None),
            P(),
        ),
        out_specs=(P(("rep", "fsdp"), None), P("fsdp", None), P("rep", "fsdp", None)),
        check_vma=False,
    )
```

profile of v0, /device:TPU:1, one launch (start us, length us, event | category | flops | bytes accessed | tf_op | source)
XLA Modules:
  0.0 217.8 jit_solution(4373254852413871140)
XLA Ops:
  8.8 1.9 dynamic-slice_bitcast_fusion.2
  11.2 1.7 multiply_add_fusion
  13.0 1.9 add.127
  14.9 3.0 %copy.31 = f32[4,64,16,64]{1,3,2,0:T(8,128)} copy(f32[4,64,16,64]{3,2,1,0:T(8,128)} %add.127) | data formatting | bytes 2097152 | tf_op jit(solution)/shard_map/add | solution.py:69
  17.9 3.6 %fusion.39 = f32[4,16,64,64]{3,2,1,0:T(8,128)S(1)} fusion(f32[4,64,16,64]{1,3,2,0:T(8,128)} %copy.31, f32[64]{0:T(128)S(1)} %get-tuple-element.356, f32[64]{0:T(128)S(1)} %get-tuple-element.357), kind=kOutput, calls=%fused_computation.65 | convolution fusion | flops 201338880 | bytes 2097664 | tf_op jit(solution)/shard_map/ij,abjk->abik/dot_general | solution.py:32
  21.5 4.9 %fusion.37 = f32[4,16,64,64]{3,2,1,0:T(8,128)} fusion(f32[4,16,64,64]{3,2,1,0:T(8,128)S(1)} %fusion.39, f32[64]{0:T(128)S(1)} %get-tuple-element.356, f32[64]{0:T(128)S(1)} %get-tuple-element.357), kind=kOutput, calls=%fused_computation.63 | convolution fusion | flops 201338880 | bytes 2097664 | tf_op jit(solution)/shard_map/abik,lk->abil/dot_general | solution.py:33
  26.4 2.1 reshape.186
  28.5 40.6 %gather_fusion = f32[4096]{0:T(1024)S(1)} fusion(f32[4,16,4096]{2,1,0:T(8,128)S(1)} %reshape.186, s32[4096]{0:T(1024)S(1)} %reshape.189), kind=kCustom, calls=%fused_computation | custom fusion | bytes 81920 | tf_op jit(solution)/shard_map/jit(take_along_axis)/gather | solution.py:72
  69.2 10.5 %all_gather.6 = f32[4,4,16,64]{3,2,1,0:T(8,128)S(1)} all-gather(f32[1,4,16,64]{3,2,1,0:T(8,128)S(1)} %and_select_fusion.1), channel_id=1, replica_groups=mesh['rep'=4,'fsdp'=32] {'rep'}, dimensions={0}, use_global_device_ids=true | all-gather | bytes 81920 | tf_op jit(solution)/shard_map/all_gather | solution.py:75
  80.0 2.3 %copy.29 = s32[4,16,4,64]{3,2,1,0:T(4,128)S(1)} copy(s32[4,16,4,64]{0,3,1,2:T(8,128)} %dynamic-slice_bitcast_fusion.2) | data formatting | bytes 131072 | tf_op jit(solution)/shard_map/transpose | solution.py:57
  84.0 14.3 %while.28 = (s32[]{:T(128)}, f32[4,16,64,64]{3,2,1,0:T(8,128)}, s32[4,16,256]{2,1,0:T(8,128)S(1)}, f32[4,16,256]{2,1,0:T(8,128)S(1)}, f32[64]{0:T(128)S(1)}, /*index=5*/f32[64]{0:T(128)S(1)}, s32[]{:T(128)}) while((s32[]{:T(128)}, f32[4,16,64,64]{3,2,1,0:T(8,128)}, s32[4,16,256]{2,1,0:T(8,128)S(1)}, ...), condition=%wide.region_1.2_spmd.clone.clone, body=%wide.region_0.1_spmd.clone.clone.sunk | while | flops 604893184 | bytes 4875865 | solution.py:51
  85.6 1.9 fusion.77
  89.2 1.9 fusion.77
  92.8 1.9 fusion.77
  96.4 1.9 fusion.77
  98.3 1.8 multiply_bitcast_fusion
  100.1 2.5 %copy.34 = f32[4,64,16,64]{3,2,1,0:T(8,128)} copy(f32[4,64,16,64]{3,1,2,0:T(8,128)S(1)} %multiply_bitcast_fusion) | data formatting | bytes 2097152 | tf_op jit(solution)/shard_map/mul | solution.py:77
  102.6 2.1 mul.190
  107.3 12.2 %while.29 = (s32[]{:T(128)}, f32[4,16,64,64]{3,2,1,0:T(8,128)}, s32[4,16,64]{2,1,0:T(8,128)S(1)}, f32[4,16,64]{2,1,0:T(8,128)S(1)}, f32[64]{0:T(128)S(1)}, /*index=5*/f32[64]{0:T(128)S(1)}, s32[]{:T(128)}) while((s32[]{:T(128)}, f32[4,16,64,64]{3,2,1,0:T(8,128)}, s32[4,16,64]{2,1,0:T(8,128)S(1)}, ...), condition=%wide.region_3.4_spmd.clone.clone, body=%wide.region_2.3_spmd.clone.clone.sunk | while | flops 151241728 | bytes 1613401 | solution.py:51
  119.5 4.3 %copy.35 = f32[4,64,16,64]{3,2,1,0:T(8,128)} copy(f32[4,64,16,64]{3,1,2,0:T(8,128)} %bitcast.133) | data formatting | bytes 2097152 | tf_op jit(solution)/shard_map/transpose | solution.py:28
  123.8 2.0 reshape.188
  127.0 56.5 %all-gather.2.cloned.1.call-done = bf16[8192,1024]{1,0:T(8,128)(2,1)} async-done(((bf16[256,1024]{1,0:T(8,128)(2,1)}), bf16[8192,1024]{1,0:T(8,128)(2,1)}) %all-gather.2.cloned.1.call-update) | async-done | bytes 16777232 | tf_op jit(solution)/shard_map/all_gather | solution.py:80
  183.5 23.6 %convert_bitcast_fusion = bf16[1024,1024]{0,1:T(8,128)(2,1)} fusion(bf16[8192,1024]{1,0:T(8,128)(2,1)} %all-gather.2.cloned.1.call-done, bf16[1024,8192]{1,0:T(8,128)(2,1)} %param.9), kind=kOutput, calls=%fused_computation.67 | convolution fusion | flops 17180917760 | bytes 35651584 | tf_op jit(solution)/shard_map/dot_general | solution.py:78
  207.1 3.9 %copy.36 = bf16[1024,1024]{1,0:T(8,128)(2,1)} copy(bf16[1024,1024]{0,1:T(8,128)(2,1)} %convert_bitcast_fusion) | data formatting | bytes 4194304
  (68 shorter events, 26.5 us)
Async XLA Ops:
  7.2 1.6 copy-start
  7.2 176.3 %all-gather.2.cloned.1.call-start = ((), (), s32[]{:S(2)}) async-start(), calls=%async_computation | async-start | bytes 17301504 | tf_op jit(solution)/shard_map/all_gather | solution.py:80
  102.6 2.1 copy-start.2
  183.5 27.5 %copy-start.1 = (s32[4,128,16,64]{1,3,2,0:T(8,128)S(1)}, s32[4,128,16,64]{1,3,2,0:T(8,128)}, u32[]{:S(2)}) copy-start(s32[4,128,16,64]{1,3,2,0:T(8,128)} %param.13) | copy-start | bytes 6291460
Sparse Core Ops, SparseCore 0:
  105.8 77.6 all-gather.1
where the time goes:
time: 218 us
  local copies, waits for them, and re-layouts  72.5 us (33%)
  matrix products  58 us (27%)
  waiting for transfers between devices  56.5 us (26%)
  between operations  14.1 us (6%)
  blocking collectives  10.5 us (5%)
  other arithmetic  5.94 us (3%)
    all_gather x1, waiting for transfers between devices, on_device(): lax.all_gather(new_weight, 'fsdp', axis=0, tiled=True)  56.5 us
    gather x4, local copies, waits for them, and re-layouts, on_device(): chosen = jnp.take_along_axis(coeff, own_sel, axis=-1)  40.9 us
    dot_general x1, matrix products, on_device(): jnp.dot(tokens, lax.all_gather(new_weight, 'fsdp', axis=0, tiled=True), p...  23.6 us
    dot_general x8, matrix products, one_row(): jnp.einsum('bki,bkl->bil', left, scaled, precision=lax.Precision.HIGHEST)  13.4 us
    dot_general x16, matrix products, basis_rows(): jnp.einsum('bkf,fn->bkn', onehot, basis, precision=lax.Precision.HIGHEST)  12.5 us
    all_gather x1, blocking collectives, on_device(): everyone = lax.all_gather(chosen[None], 'rep', axis=0, tiled=True)  10.5 us
    unnamed x8, local copies, waits for them, and re-layouts  5.67 us
    add x2, local copies, waits for them, and re-layouts, on_device(): moment = beta_decay * momentum[0] + grad[0]  4.93 us
  transfers between devices with their start and end apart: 1, of which 1 were waited for; matrix products, arithmetic and copies ran while one was open for 10% of the time, Pallas kernels for 0%

commit v1 on v0

v1 whole, which is shorter than its diff:
```python
import functools

import jax
import jax.numpy as jnp
import numpy as np
from jax import lax
from jax.experimental import pallas as pl
from jax.experimental.pallas import tpu as pltpu
from jax.sharding import Mesh, PartitionSpec as P

GROUP = 64
KEEP = 64
REPS = 4
PAIR = 2 * GROUP

beta_decay = 0.999
step_rate = 0.05

HIGHEST = lax.Precision.HIGHEST
NT = (((1,), (1,)), ((), ()))


def dct_blocks(size):
    freq = np.arange(GROUP, dtype=np.float64)[:, None]
    place = np.arange(GROUP, dtype=np.float64)[None, :]
    scale = np.where(freq == 0, np.sqrt(1.0 / GROUP), np.sqrt(2.0 / GROUP))
    basis = scale * np.cos(np.pi * (2.0 * place + 1.0) * freq / (2.0 * GROUP))
    return np.kron(np.eye(size // GROUP), basis).astype(np.float32)


def halves(value):
    high = value.astype(jnp.bfloat16)
    return high, (value - high.astype(jnp.float32)).astype(jnp.bfloat16)


def targets(idx):
    lane = lax.broadcasted_iota(jnp.int32, idx.shape, 1)
    stacked = jnp.bitwise_and(jnp.right_shift(lane, 6), 3)
    return jnp.right_shift(idx, 6) + stacked * GROUP, jnp.bitwise_and(idx, GROUP - 1)


def is_row(target, rows):
    return lax.broadcasted_iota(jnp.int32, (rows, target.shape[1]), 0) == target


def coeff_kernel(momentum, grad, selection, basis, coeff, chosen, indices, held, sem):
    blocks = held.shape[1]
    first = ((lax.axis_index("y") * 4 + lax.axis_index("z")) * 2 + lax.axis_index("core")) * blocks
    copy = pltpu.make_async_copy(selection.at[:, pl.ds(first, blocks)], held, sem)
    copy.start()
    moment = beta_decay * momentum[0] + grad[0]
    inner = jnp.dot(basis[...], moment, precision=HIGHEST, preferred_element_type=jnp.float32)
    width = basis.shape[0]
    for c in range(0, moment.shape[1], width):
        coeff[:, c : c + width] = lax.dot_general(
            inner[:, c : c + width], basis[...], NT, precision=HIGHEST, preferred_element_type=jnp.float32
        )
    copy.wait()
    for r in range(REPS):
        indices[r] = jnp.concatenate([held[r, a] for a in range(blocks)], axis=1)
    row, col = targets(indices[lax.axis_index("x")])
    for p in range(coeff.shape[1] // PAIR):
        high, low = halves(coeff[:, p * PAIR : (p + 1) * PAIR])
        left = jnp.concatenate([high, low], axis=1)
        for b in range(2):
            k = 2 * p + b
            pick = jnp.where(is_row(col[k : k + 1] + b * GROUP, PAIR), 1.0, 0.0).astype(jnp.bfloat16)
            picked = jnp.dot(left, jnp.concatenate([pick, pick], axis=0), preferred_element_type=jnp.float32)
            mine = jnp.where(is_row(row[k : k + 1], picked.shape[0]), picked, 0.0)
            chosen[k : k + 1, :] = jnp.sum(mine, axis=0, keepdims=True)


def weight_kernel(weight, values, indices, basis, new_weight, dense):
    rows = weight.shape[0]
    for p in range(weight.shape[1] // PAIR):
        lefts, highs, lows = [], [], []
        for b in range(2):
            k = 2 * p + b
            for r in range(REPS):
                row, col = targets(indices[r, k : k + 1, :])
                lefts.append(jnp.where(is_row(row, rows), 1.0, 0.0).astype(jnp.bfloat16))
                here = is_row(col + b * GROUP, PAIR)
                high, low = halves(values[r, k : k + 1, :])
                highs.append(jnp.where(here, high.astype(jnp.float32), 0.0).astype(jnp.bfloat16))
                lows.append(jnp.where(here, low.astype(jnp.float32), 0.0).astype(jnp.bfloat16))
        right = jnp.concatenate([jnp.concatenate(highs, axis=1), jnp.concatenate(lows, axis=1)], axis=0)
        both = lax.dot_general(jnp.concatenate(lefts, axis=1), right, NT, preferred_element_type=jnp.float32)
        dense[:, p * PAIR : (p + 1) * PAIR] = both[:, :PAIR] + both[:, PAIR:]
    width = basis.shape[0]
    inner = jnp.dot(basis[...].T, dense[...], precision=HIGHEST, preferred_element_type=jnp.float32)
    for c in range(0, weight.shape[1], width):
        update = jnp.dot(inner[:, c : c + width], basis[...], precision=HIGHEST, preferred_element_type=jnp.float32)
        old = weight[:, c : c + width].astype(jnp.float32)
        new_weight[:, c : c + width] = (old - step_rate * update).astype(jnp.bfloat16)


def momentum_kernel(momentum, grad, coeff, indices, basis, new_momentum, dense):
    rows = coeff.shape[0]
    row, col = targets(indices[lax.axis_index("x")])
    for p in range(coeff.shape[1] // PAIR):
        lefts, rights = [], []
        for b in range(2):
            k = 2 * p + b
            lefts.append(jnp.where(is_row(row[k : k + 1], rows), 1.0, 0.0).astype(jnp.bfloat16))
            rights.append(jnp.where(is_row(col[k : k + 1] + b * GROUP, PAIR), 1.0, 0.0).astype(jnp.bfloat16))
        kept = lax.dot_general(
            jnp.concatenate(lefts, axis=1), jnp.concatenate(rights, axis=1), NT, preferred_element_type=jnp.float32
        )
        dense[:, p * PAIR : (p + 1) * PAIR] = jnp.where(kept > 0.5, coeff[:, p * PAIR : (p + 1) * PAIR], 0.0)
    width = basis.shape[0]
    inner = jnp.dot(basis[...].T, dense[...], precision=HIGHEST, preferred_element_type=jnp.float32)
    for c in range(0, coeff.shape[1], width):
        own = jnp.dot(inner[:, c : c + width], basis[...], precision=HIGHEST, preferred_element_type=jnp.float32)
        moment = beta_decay * momentum[0, :, c : c + width] + grad[0, :, c : c + width]
        new_momentum[0, :, c : c + width] = moment - own


VM = pl.BlockSpec(memory_space=pltpu.VMEM)
HBM = pl.BlockSpec(memory_space=pl.ANY)
PARAMS = pltpu.CompilerParams(vmem_limit_bytes=48 * 2**20)


def on_device(tokens, weight, momentum, grad, selection):
    rows, cols = weight.shape
    blocks = rows // GROUP
    basis = jnp.asarray(dct_blocks(rows))
    coeff, chosen, indices = pl.pallas_call(
        coeff_kernel,
        out_shape=(
            jax.ShapeDtypeStruct((rows, cols), jnp.float32),
            jax.ShapeDtypeStruct((cols // GROUP, blocks * KEEP), jnp.float32),
            jax.ShapeDtypeStruct((REPS, cols // GROUP, blocks * KEEP), jnp.int32),
        ),
        in_specs=[VM, VM, HBM, VM],
        out_specs=(VM, VM, VM),
        scratch_shapes=[pltpu.VMEM((REPS, blocks, cols // GROUP, KEEP), jnp.int32), pltpu.SemaphoreType.DMA],
        compiler_params=PARAMS,
    )(momentum, grad, selection, basis)
    everyone = lax.all_gather(chosen, "x", axis=0)
    new_weight = pl.pallas_call(
        weight_kernel,
        out_shape=jax.ShapeDtypeStruct((rows, cols), jnp.bfloat16),
        in_specs=[VM] * 4,
        out_specs=VM,
        scratch_shapes=[pltpu.VMEM((rows, cols), jnp.float32)],
        compiler_params=PARAMS,
    )(weight, everyone, indices, basis)
    new_momentum = pl.pallas_call(
        momentum_kernel,
        out_shape=jax.ShapeDtypeStruct(momentum.shape, jnp.float32),
        in_specs=[VM] * 5,
        out_specs=VM,
        scratch_shapes=[pltpu.VMEM((rows, cols), jnp.float32)],
        compiler_params=PARAMS,
    )(momentum, grad, coeff, indices, basis)
    keys = jnp.dot(
        tokens,
        lax.all_gather(new_weight, ("y", "z", "core"), axis=0, tiled=True),
        preferred_element_type=jnp.float32,
    )
    return (keys.astype(jnp.bfloat16), new_weight, new_momentum)


def solution(mesh):
    chips = Mesh(mesh.devices.reshape(4, 4, 4, 2), ("x", "y", "z", "core"))
    plane = ("y", "z", "core")
    return jax.shard_map(
        on_device,
        mesh=chips,
        in_specs=(
            P(("x",) + plane, None),
            P(plane, None),
            P("x", plane, None),
            P("x", plane, None),
            P(),
        ),
        out_specs=(P(("x",) + plane, None), P(plane, None), P("x", plane, None)),
        check_vma=False,
    )
```

time: 218 us -> 145 us (0.67)
  local copies, waits for them, and re-layouts: 72.5 us -> 14.4 us
  matrix products: 58 us -> 22.1 us
  waiting for transfers between devices: 56.5 us -> 70.9 us
  Pallas kernels: 0 us -> 12.8 us
  other arithmetic: 5.94 us -> 0 us
    gather x4 -> x0, local copies, waits for them, and re-layouts: 40.9 us -> none  [on_device(): chosen = jnp.take_along_axis(coeff, own_sel, axis=-1)]
    dot_general x27 -> x1, matrix products: 58 us -> 22.1 us  [on_device(): jnp.dot(tokens, lax.all_gather(new_weight, ('y', 'z', 'core'), axis=0, ti...]
    all_gather x1, waiting for transfers between devices: 56.5 us -> 70.8 us  [on_device(): lax.all_gather(new_weight, ('y', 'z', 'core'), axis=0, tiled=True)]
    pallas_call x0 -> x3, Pallas kernels: none -> 12.8 us  [the longest x1 5.76 us: on_device(): pl.pallas_call(weight_kernel, out_shape=jax.ShapeDtypeStruct((rows, cols)...]
    unnamed x8 -> x16, local copies, waits for them, and re-layouts: 5.67 us -> 14.4 us
    transpose x4 -> x0, local copies, waits for them, and re-layouts: 8.6 us -> none  [the longest x1 4.29 us: from_groups(): return blocks.transpose(0, 2, 1, 3).reshape(nrow * GROUP, ncol * GROUP)]
    add x2 -> x0, local copies, waits for them, and re-layouts: 4.93 us -> none  [on_device(): moment = beta_decay * momentum[0] + grad[0]]
    mul x10 -> x0, local copies, waits for them, and re-layouts: 4.67 us -> none  [the longest x2 4.6 us: on_device(): step_rate * update]
  transfers between devices with their start and end apart: 1 -> 1, of which waited for: 1 -> 1; matrix products, arithmetic and copies ran while one was open for 10% -> 0% of each run, Pallas kernels for 0% -> 2%
where the time goes in v1:
time: 145 us; the launch traced here: 144 us
  waiting for transfers between devices  70.9 us (49%)
  matrix products  22.1 us (15%)
  local copies, waits for them, and re-layouts  14.4 us (10%)
  between operations  14.1 us (10%)
  Pallas kernels  12.8 us (9%)
  blocking collectives  10.2 us (7%)
    all_gather x1, waiting for transfers between devices, on_device(): lax.all_gather(new_weight, ('y', 'z', 'core'), axis=0, tiled=True)  70.8 us
    dot_general x1, matrix products, on_device(): jnp.dot(tokens, lax.all_gather(new_weight, ('y', 'z', 'core'), axis=0, ti...  22.1 us
    unnamed x16, local copies, waits for them, and re-layouts  14.4 us
    all_gather x1, blocking collectives, on_device(): everyone = lax.all_gather(chosen, 'x', axis=0)  10.2 us
    pallas_call x1, Pallas kernels, on_device(): pl.pallas_call(weight_kernel, out_shape=jax.ShapeDtypeStruct((rows, cols)...  5.76 us
    pallas_call x1, Pallas kernels, on_device(): pl.pallas_call(momentum_kernel, out_shape=jax.ShapeDtypeStruct(momentum.s...  3.59 us
    pallas_call x1, Pallas kernels, on_device(): pl.pallas_call(coeff_kernel, out_shape=(jax.ShapeDtypeStruct((rows, cols)...  3.48 us
  transfers between devices with their start and end apart: 1, of which 1 were waited for; matrix products, arithmetic and copies ran while one was open for 0% of the time, Pallas kernels for 2%

profile of v1, /device:TPU:1, one launch (start us, length us, event | category | flops | bytes accessed | tf_op | source)
XLA Modules:
  0.0 144.5 jit_solution(3080586274741847554)
XLA Ops:
  7.2 0.0 all-gather.3.cloned.1.call-start
  7.2 4.0 %copy.9.selection = s32[4,128,16,64]{3,2,1,0:T(8,128)} copy(s32[4,128,16,64]{1,3,2,0:T(8,128)} %param.10) | data formatting | bytes 4194304 | tf_op args[4]
  11.2 0.0 copy-start
  11.2 1.2 copy-done
  12.5 0.0 copy-start.2
  12.5 1.2 copy-done.2
  13.7 0.0 copy-start.4
  13.7 0.9 copy-done.4
  14.6 3.5 %shard_map.85 = (f32[256,1024]{1,0:T(8,128)S(1)}, f32[16,256]{1,0:T(8,128)S(1)}, s32[4,16,256]{2,1,0:T(8,128)S(1)}) custom-call(f32[1,256,1024]{2,1,0:T(8,128)S(1)} %copy-done, f32[1,256,1024]{2,1,0:T(8,128)S(1)} %copy-done.2, s32[4,128,16,64]{3,2,1,0:T(8,128)} %copy.9.selection, f32[256,256]{1,0:T(8,128)S(1)} %copy-done.4), custom_call_target="tpu_custom_call" | custom-call | tf_op jit(solution)/shard_map/pallas_call | solution.py:127
  18.1 10.2 %all-gather = f32[64,256]{1,0:T(8,128)S(1)} all-gather(f32[16,256]{1,0:T(8,128)S(1)} %get-tuple-element.6), channel_id=2, replica_groups=mesh['x'=4,'y'=4,'z'=4,'core'=2] {'x'}, dimensions={0}, use_global_device_ids=true | all-gather | bytes 81920 | tf_op jit(solution)/shard_map/all_gather | solution.py:139
  28.3 0.0 copy-start.6
  28.3 1.0 copy-done.6
  29.3 5.8 %shard_map.86 = bf16[256,1024]{1,0:T(8,128)(2,1)} custom-call(bf16[256,1024]{1,0:T(8,128)(2,1)S(1)} %copy-done.6, f32[4,16,256]{2,1,0:T(8,128)S(1)} %bitcast.5, s32[4,16,256]{2,1,0:T(8,128)S(1)} %get-tuple-element.7.indices, f32[256,256]{1,0:T(8,128)S(1)} %copy-done.4), custom_call_target="tpu_custom_call" | custom-call | tf_op jit(solution)/shard_map/pallas_call | solution.py:140
  35.1 0.0 all-gather.3.cloned.1.call-update
  35.1 0.0 copy-start.1
  35.1 1.2 copy-done.1
  36.3 0.0 copy-start.3
  36.3 1.2 copy-done.3
  37.6 0.0 copy-start.5
  37.6 0.9 copy-done.5
  38.5 3.6 %shard_map.87 = f32[1,256,1024]{2,1,0:T(8,128)} custom-call(f32[1,256,1024]{2,1,0:T(8,128)S(1)} %copy-done.1, f32[1,256,1024]{2,1,0:T(8,128)S(1)} %copy-done.3, f32[256,1024]{1,0:T(8,128)S(1)} %get-tuple-element.8.coeff, s32[4,16,256]{2,1,0:T(8,128)S(1)} %get-tuple-element.7.indices, f32[256,256]{1,0:T(8,128)S(1)} %copy-done.5), custom_call_target="tpu_custom_call" | custom-call | tf_op jit(solution)/shard_map/pallas_call | solution.py:148
  42.1 70.8 %all-gather.3.cloned.1.call-done = bf16[8192,1024]{1,0:T(8,128)(2,1)} async-done(((bf16[256,1024]{1,0:T(8,128)(2,1)}), bf16[8192,1024]{1,0:T(8,128)(2,1)}) %all-gather.3.cloned.1.call-update) | async-done | bytes 16777232 | tf_op jit(solution)/shard_map/all_gather | solution.py:158
  112.9 22.1 %convert_bitcast_fusion = bf16[1024,1024]{0,1:T(8,128)(2,1)S(1)} fusion(bf16[8192,1024]{1,0:T(8,128)(2,1)} %all-gather.3.cloned.1.call-done, bf16[1024,8192]{1,0:T(8,128)(2,1)} %param.6), kind=kOutput, calls=%fused_computation | convolution fusion | flops 17180917760 | bytes 35651584 | tf_op jit(solution)/shard_map/dot_general | solution.py:156
  135.1 2.6 %copy.10 = bf16[1024,1024]{1,0:T(8,128)(2,1)} copy(bf16[1024,1024]{0,1:T(8,128)(2,1)S(1)} %convert_bitcast_fusion) | data formatting | bytes 4194304
Async XLA Ops:
  7.2 105.8 %all-gather.3.cloned.1.call-start = ((), (), s32[]{:S(2)}) async-start(), calls=%async_computation | async-start | bytes 17301504 | tf_op jit(solution)/shard_map/all_gather | solution.py:158
  11.2 1.2 copy-start
  12.5 1.2 copy-start.2
  13.7 0.9 copy-start.4
  28.3 1.0 copy-start.6
  35.1 1.2 copy-start.1
  36.3 1.2 copy-start.3
  37.6 0.9 copy-start.5
Sparse Core Ops, SparseCore 0:
  35.2 77.6 all-gather.2

commit v2 on v0

v2 whole, which is shorter than its diff:
```python
import jax
import jax.numpy as jnp
import numpy as np
from jax import lax
from jax.experimental import pallas as pl
from jax.experimental.pallas import tpu as pltpu
from jax.sharding import Mesh, PartitionSpec as P

GROUP = 64
KEEP = 64
REPS = 4
SIDE = 4
PAIR = 2 * GROUP
PLANE = ("y", "z", "core")

beta_decay = 0.999
step_rate = 0.05

HIGHEST = lax.Precision.HIGHEST
NT = (((1,), (1,)), ((), ()))
TN = (((0,), (0,)), ((), ()))
VM = pl.BlockSpec(memory_space=pltpu.VMEM)
HBM = pl.BlockSpec(memory_space=pltpu.HBM)
PARAMS = pltpu.CompilerParams(vmem_limit_bytes=32 * 2**20)
ALONE = pltpu.CompilerParams(vmem_limit_bytes=60 * 2**20)
FLOPS, BYTES = 1000, 1000


def dct_blocks(size):
    freq = np.arange(GROUP, dtype=np.float64)[:, None]
    place = np.arange(GROUP, dtype=np.float64)[None, :]
    scale = np.where(freq == 0, np.sqrt(1.0 / GROUP), np.sqrt(2.0 / GROUP))
    basis = scale * np.cos(np.pi * (2.0 * place + 1.0) * freq / (2.0 * GROUP))
    return np.kron(np.eye(size // GROUP), basis).astype(np.float32)


def halves(value):
    high = value.astype(jnp.bfloat16)
    return high, (value - high.astype(jnp.float32)).astype(jnp.bfloat16)


def dot3(left, right, dims):
    total = None
    for a, b in ((0, 0), (0, 1), (1, 0)):
        part = lax.dot_general(left[a], right[b], dims, preferred_element_type=jnp.float32)
        total = part if total is None else total + part
    return total


def plain(contract):
    return (contract, ((), ()))


def is_row(target, rows):
    return lax.broadcasted_iota(jnp.int32, (rows, target.shape[1]), 0) == target


def one_hot(target, rows):
    return jnp.where(is_row(target, rows), 1.0, 0.0).astype(jnp.bfloat16)


def coeff_kernel(momentum, grad, selection, basis, chosen, where, mom, gra, sel, sems):
    blocks = mom.shape[0] // GROUP
    copies = [
        pltpu.make_async_copy(selection, sel, sems.at[0]),
        pltpu.make_async_copy(momentum.at[0], mom, sems.at[1]),
        pltpu.make_async_copy(grad.at[0], gra, sems.at[2]),
    ]
    for copy in copies:
        copy.start()
    base = basis[...]
    base = halves(base)
    first = ((lax.axis_index("y") * SIDE + lax.axis_index("z")) * 2 + lax.axis_index("core")) * blocks
    lanes = sel.shape[3]
    cols = sel.shape[1] * KEEP
    sub = lax.broadcasted_iota(jnp.int32, (16, 2 * lanes), 0)
    lane = lax.broadcasted_iota(jnp.int32, (16, 2 * lanes), 1)
    mine = jnp.where(sub < 8, first + sub, lanes + first + sub - 8)
    pick = jnp.where((lane == mine) & (jnp.bitwise_and(sub, 7) < blocks), 1.0, 0.0).astype(jnp.bfloat16)
    copies[0].wait()
    shift = jnp.bitwise_and(lax.broadcasted_iota(jnp.int32, (8, cols), 1), GROUP)
    for r in range(REPS):
        flat = sel[r].reshape(cols, lanes)
        row = jnp.right_shift(flat, 6).astype(jnp.float32).astype(jnp.bfloat16)
        col = jnp.bitwise_and(flat, GROUP - 1).astype(jnp.float32).astype(jnp.bfloat16)
        both = lax.dot_general(pick, jnp.concatenate([row, col], axis=1), NT, preferred_element_type=jnp.float32)
        both = both.astype(jnp.int32)
        where[0, r] = both[:8]
        where[1, r] = both[8:] + shift
    copies[1].wait()
    copies[2].wait()
    moment = halves(beta_decay * mom[...] + gra[...])
    inner = halves(dot3(base, moment, plain(((1,), (0,)))))
    own = lax.axis_index("x")
    width = base[0].shape[0]
    for c in range(0, mom.shape[1], width):
        coeff = dot3([part[:, c : c + width] for part in inner], base, NT)
        high, low = halves(coeff)
        for p in range(c, c + width, PAIR):
            span = slice(p - c, p - c + PAIR)
            for a in range(blocks):
                rows = slice(a * GROUP, (a + 1) * GROUP)
                left = jnp.concatenate([high[rows, span], low[rows, span]], axis=1)
                right = one_hot(where[1, own, a : a + 1, p : p + PAIR], PAIR)
                found = jnp.dot(left, jnp.concatenate([right, right], axis=0), preferred_element_type=jnp.float32)
                kept = jnp.where(is_row(where[0, own, a : a + 1, p : p + PAIR], GROUP), found, 0.0)
                chosen[a : a + 1, p : p + PAIR] = jnp.sum(kept, axis=0, keepdims=True)


def weight_kernel(weight, chosen0, chosen1, chosen2, chosen3, where, basis, new_weight, dense):
    rows, cols = weight.shape
    here = lax.axis_index("x")
    base = halves(basis[...])
    values = []
    for k, chosen in enumerate((chosen0, chosen1, chosen2, chosen3)):
        high, low = halves(chosen[...])
        values.append((lax.rem(here - k + REPS, REPS), high.astype(jnp.float32), low.astype(jnp.float32)))
    for p in range(0, cols, PAIR):
        for a in range(rows // GROUP):
            lefts, highs, lows = [], [], []
            for r, high, low in values:
                lefts.append(one_hot(where[0, r, a : a + 1, p : p + PAIR], GROUP))
                hit = is_row(where[1, r, a : a + 1, p : p + PAIR], PAIR)
                highs.append(jnp.where(hit, high[a : a + 1, p : p + PAIR], 0.0).astype(jnp.bfloat16))
                lows.append(jnp.where(hit, low[a : a + 1, p : p + PAIR], 0.0).astype(jnp.bfloat16))
            right = jnp.concatenate([jnp.concatenate(highs, axis=1), jnp.concatenate(lows, axis=1)], axis=0)
            both = lax.dot_general(jnp.concatenate(lefts, axis=1), right, NT, preferred_element_type=jnp.float32)
            dense[a * GROUP : (a + 1) * GROUP, p : p + PAIR] = both[:, :PAIR] + both[:, PAIR:]
    inner = halves(dot3(base, halves(dense[...]), TN))
    width = rows
    for c in range(0, cols, width):
        update = dot3([part[:, c : c + width] for part in inner], base, plain(((1,), (0,))))
        old = weight[:, c : c + width].astype(jnp.float32)
        new_weight[:, c : c + width] = (old - step_rate * update).astype(jnp.bfloat16)


def momentum_kernel(momentum, grad, where, basis, new_momentum, dense):
    rows, cols = dense.shape
    own = lax.axis_index("x")
    base = basis[...]
    moment = beta_decay * momentum[0] + grad[0]
    inner = jnp.dot(base, moment, precision=HIGHEST, preferred_element_type=jnp.float32)
    width = rows
    for c in range(0, cols, width):
        coeff = lax.dot_general(inner[:, c : c + width], base, NT, precision=HIGHEST, preferred_element_type=jnp.float32)
        for p in range(c, c + width, PAIR):
            for a in range(rows // GROUP):
                left = one_hot(where[0, own, a : a + 1, p : p + PAIR], GROUP)
                right = one_hot(where[1, own, a : a + 1, p : p + PAIR], PAIR)
                kept = lax.dot_general(left, right, NT, preferred_element_type=jnp.float32)
                span = slice(a * GROUP, (a + 1) * GROUP)
                dense[span, p : p + PAIR] = jnp.where(kept > 0.5, coeff[span, p - c : p - c + PAIR], 0.0)
    inner = lax.dot_general(base, dense[...], TN, precision=HIGHEST, preferred_element_type=jnp.float32)
    for c in range(0, cols, width):
        own_part = jnp.dot(inner[:, c : c + width], base, precision=HIGHEST, preferred_element_type=jnp.float32)
        moment = beta_decay * momentum[0, :, c : c + width] + grad[0, :, c : c + width]
        new_momentum[0, :, c : c + width] = moment - own_part


def ring(axis, step):
    pairs = []
    for y in range(SIDE):
        for z in range(SIDE):
            for c in range(2):
                if (c == 0) == (axis == "u"):
                    to = ((y + step) % SIDE, z)
                else:
                    to = (y, (z + step) % SIDE)
                pairs.append(((y * SIDE + z) * 2 + c, (to[0] * SIDE + to[1]) * 2 + c))
    return pairs


def send(value, axis, step):
    return lax.ppermute(value, PLANE, ring(axis, step))


def sibling(value):
    return lax.ppermute(value, "core", [(0, 1), (1, 0)])


def shard_at(u, v, other=False):
    y, z, c = lax.axis_index("y"), lax.axis_index("z"), lax.axis_index("core")
    if other:
        c = 1 - c
    along = lambda at, step: lax.rem(at + step + SIDE, SIDE)
    even = along(y, u) * SIDE + along(z, v)
    odd = along(y, v) * SIDE + along(z, u)
    return 2 * jnp.where(c == 0, even, odd) + c


def multiply(jobs, shards, pieces, dtypes, after=None, chunks=((0, 1024),)):
    cols = pieces[0].shape[1]
    depth, tile = 256, 256
    count = len(shards)
    rows = jobs[0][0].shape[0]
    after = jnp.zeros((8, 128), jnp.float32) if after is None else after
    adds = [x for _, some in jobs for x in some]
    n_jobs, n_pieces, n_adds = len(jobs), len(pieces), len(adds)
    aliases, at = {}, 2 + n_jobs + n_pieces
    for n, (_, some) in enumerate(jobs):
        if some and some[0].dtype == dtypes[n]:
            aliases[at] = n
        at += len(some)

    def kernel(ids, _, *refs):
        toks, refs = refs[:n_jobs], refs[n_jobs:]
        ws, refs = refs[:n_pieces], refs[n_pieces:]
        adds, refs = refs[:n_adds], refs[n_adds:]
        outs, (ran, left, right, sems, piece_sems) = refs[:n_jobs], refs[n_jobs:]
        ran[...] = jnp.zeros_like(ran)
        loads, at = [], 0
        for k, w in enumerate(ws):
            deep = w.shape[0]
            loads.append(pltpu.make_async_copy(w, right.at[pl.ds(at, deep)], piece_sems.at[k]))
            loads[-1].start()
            at += deep
        plan = [(n, at, size) for n in range(n_jobs) for at, size in chunks]
        copies = {}

        def issue(q):
            n, at, size = plan[q]
            for k in range(count):
                copies[q, k] = pltpu.make_async_copy(
                    toks[n].at[pl.ds(at, size), pl.ds(pl.multiple_of(ids[k] * depth, depth), depth)],
                    left.at[n, pl.ds(at, size), pl.ds(k * depth, depth)],
                    sems.at[q, k],
                )
                copies[q, k].start()

        issue(0)
        for load in loads:
            load.wait()
        for q, (n, at, size) in enumerate(plan):
            for k in range(count):
                copies[q, k].wait()
            if q + 1 < len(plan):
                issue(q + 1)
            first = sum(len(some) for _, some in jobs[:n])
            mine = adds[first : first + len(jobs[n][1])]
            for i in range(at, at + size, tile):
                span = slice(i, i + tile)
                result = jnp.dot(left[n, span, :], right[...], preferred_element_type=jnp.float32)
                for add in mine:
                    result = result + add[span, :].astype(jnp.float32)
                outs[n][span, :] = result.astype(outs[n].dtype)

    def result(dtype):
        shape = (rows, cols)
        return pltpu.VMEM(shape, dtype) if dtype == jnp.float32 else jax.ShapeDtypeStruct(shape, dtype)

    return pl.pallas_call(
        kernel,
        in_specs=[pl.BlockSpec(memory_space=pltpu.SMEM)] + [HBM] * (1 + n_jobs + n_pieces) + [VM] * n_adds,
        out_specs=[VM] * (n_jobs + 1),
        out_shape=[result(dtype) for dtype in dtypes] + [jax.ShapeDtypeStruct((8, 128), jnp.float32)],
        scratch_shapes=[
            pltpu.VMEM((n_jobs, rows, count * depth), jnp.bfloat16),
            pltpu.VMEM((count * depth, cols), jnp.bfloat16),
            pltpu.SemaphoreType.DMA((n_jobs * len(chunks), count)),
            pltpu.SemaphoreType.DMA((n_pieces,)),
        ],
        compiler_params=pltpu.CompilerParams(vmem_limit_bytes=24 * 2**20),
        cost_estimate=pl.CostEstimate(flops=FLOPS, bytes_accessed=BYTES, transcendentals=0),
        input_output_aliases=aliases,
    )(jnp.stack(shards).astype(jnp.int32), after, *[in_hbm(t) for t, _ in jobs], *[in_hbm(p) for p in pieces], *adds)


def in_hbm(value):
    return pltpu.with_memory_space_constraint(value, pltpu.HBM)


def on_device(tokens, weight, momentum, grad, selection):
    rows, cols = weight.shape
    blocks = rows // GROUP
    basis = jnp.asarray(dct_blocks(rows))
    lanes = selection.transpose(0, 2, 3, 1)
    chosen, where = pl.pallas_call(
        coeff_kernel,
        out_shape=(
            jax.ShapeDtypeStruct((blocks, cols), jnp.float32),
            jax.ShapeDtypeStruct((2, REPS, 8, cols), jnp.int32),
        ),
        in_specs=[HBM, HBM, HBM, VM],
        out_specs=(VM, VM),
        scratch_shapes=[
            pltpu.VMEM((rows, cols), jnp.float32),
            pltpu.VMEM((rows, cols), jnp.float32),
            pltpu.VMEM(lanes.shape, jnp.int32),
            pltpu.SemaphoreType.DMA((3,)),
        ],
        compiler_params=PARAMS,
    )(in_hbm(momentum), in_hbm(grad), in_hbm(lanes), basis)
    along_x = lambda step: lax.ppermute(chosen, "x", [(i, (i + step) % REPS) for i in range(REPS)])
    others = [along_x(k) for k in range(1, REPS)]
    tokens_too = sibling(tokens)
    shard = pl.pallas_call(
        weight_kernel,
        out_shape=jax.ShapeDtypeStruct((rows, cols), jnp.bfloat16),
        in_specs=[VM] * 7,
        out_specs=VM,
        scratch_shapes=[pltpu.VMEM((rows, cols), jnp.float32)],
        compiler_params=PARAMS,
    )(weight, chosen, *others, where, basis)

    am, ap = send(shard, "u", 1), send(shard, "u", -1)
    new_momentum = pl.pallas_call(
        momentum_kernel,
        out_shape=jax.ShapeDtypeStruct(momentum.shape, jnp.float32),
        in_specs=[VM] * 4,
        out_specs=VM,
        scratch_shapes=[pltpu.VMEM((rows, cols), jnp.float32)],
        compiler_params=PARAMS,
    )(momentum, grad, where, basis)
    am, ap, new_momentum = lax.optimization_barrier((am, ap, new_momentum))
    top, bottom = send(am[: rows // 2], "u", 1), send(ap[rows // 2 :], "u", -1)
    s1 = jnp.concatenate([shard, am], axis=0)
    s2 = jnp.concatenate([ap, top, bottom], axis=0)
    r1p, r2m = send(s1, "v", 1), send(s2, "v", -1)
    r2p, r1m = send(s2, "v", 1), send(s1, "v", -1)
    f32, bf16 = jnp.float32, jnp.bfloat16
    mine, theirs, ran = multiply(
        [(tokens, ()), (tokens_too, ())],
        [shard_at(0, 0), shard_at(-1, 0), shard_at(1, 0), shard_at(2, 0)],
        [s1, s2],
        [f32, f32],
    )
    r1p, r2m, ran = lax.optimization_barrier((r1p, r2m, ran))
    f1, f2 = send(r1p, "v", 1), send(r2m, "v", -1)
    mine, theirs, ran = multiply(
        [(tokens, (mine,)), (tokens_too, (theirs,))],
        [shard_at(0, -1), shard_at(-1, -1), shard_at(1, 1), shard_at(2, 1)],
        [r1p, r2m],
        [f32, f32],
        after=ran,
    )
    mine, theirs, ran = multiply(
        [(tokens, (mine,)), (tokens_too, (theirs,))],
        [shard_at(1, -1), shard_at(2, -1), shard_at(0, 1), shard_at(-1, 1)],
        [r2p, r1m],
        [f32, bf16],
        after=ran,
    )
    theirs = sibling(theirs)
    f1, f2, ran = lax.optimization_barrier((f1, f2, ran))
    g1, g2 = sibling(f1), sibling(f2)
    far = [(0, 2), (-1, 2), (1, 2), (2, 2)]
    split = ((0, 256), (256, 768))
    mine, ran = multiply([(tokens, (mine,))], [shard_at(*at) for at in far], [f1, f2], [f32], ran, split)
    keys, _ = multiply(
        [(tokens, (mine, theirs))], [shard_at(*at, other=True) for at in far], [g1, g2], [bf16], ran, split
    )
    return keys, shard, new_momentum


def solution(mesh):
    chips = Mesh(mesh.devices.reshape(REPS, SIDE, SIDE, 2), ("x",) + PLANE)
    return jax.shard_map(
        on_device,
        mesh=chips,
        in_specs=(
            P(("x",) + PLANE, None),
            P(PLANE, None),
            P("x", PLANE, None),
            P("x", PLANE, None),
            P(),
        ),
        out_specs=(P(("x",) + PLANE, None), P(PLANE, None), P("x", PLANE, None)),
        check_vma=False,
    )
```

time: 218 us -> 103 us (0.47)
  local copies, waits for them, and re-layouts: 72.5 us -> 6.19 us
  matrix products: 58 us -> 0 us
  Pallas kernels: 0 us -> 52.3 us
  waiting for transfers between devices: 56.5 us -> 14.5 us
  starting transfers between devices: 0.04 us -> 27.8 us
  between operations: 14.1 us -> 1.05 us
  blocking collectives: 10.5 us -> 0 us
  other arithmetic: 5.94 us -> 0.45 us
    dot_general x27 -> x0, matrix products: 58 us -> none  [the longest x1 23.6 us: on_device(): jnp.dot(tokens, lax.all_gather(new_weight, 'fsdp', axis=0, tiled=True), p...]
    all_gather x1 -> x0, waiting for transfers between devices: 56.5 us -> none  [on_device(): lax.all_gather(new_weight, 'fsdp', axis=0, tiled=True)]
    pallas_call x0 -> x8, Pallas kernels: none -> 52.3 us  [the longest x5 37.9 us: multiply(): pl.pallas_call(kernel, in_specs=[pl.BlockSpec(memory_space=pltpu.SMEM)] +...]
    gather x4 -> x0, local copies, waits for them, and re-layouts: 40.9 us -> none  [on_device(): chosen = jnp.take_along_axis(coeff, own_sel, axis=-1)]
    ppermute x0 -> x17, starting transfers between devices: none -> 27.8 us  [the longest x10 13.8 us: send(): return lax.ppermute(value, PLANE, ring(axis, step))]
    ppermute x0 -> x17, waiting for transfers between devices: none -> 14.5 us  [the longest x10 11.3 us: send(): return lax.ppermute(value, PLANE, ring(axis, step))]
    all_gather x1 -> x0, blocking collectives: 10.5 us -> none  [on_device(): everyone = lax.all_gather(chosen[None], 'rep', axis=0, tiled=True)]
    transpose x4 -> x0, local copies, waits for them, and re-layouts: 8.6 us -> none  [the longest x1 4.29 us: from_groups(): return blocks.transpose(0, 2, 1, 3).reshape(nrow * GROUP, ncol * GROUP)]
  transfers between devices with their start and end apart: 1 -> 17, of which waited for: 1 -> 7; matrix products, arithmetic and copies ran while one was open for 10% -> 1% of each run, Pallas kernels for 0% -> 44%
where the time goes in v2:
time: 103 us; the launch traced here: 102 us
  Pallas kernels  52.3 us (51%)
  starting transfers between devices  27.8 us (27%)
  waiting for transfers between devices  14.5 us (14%)
  local copies, waits for them, and re-layouts  6.19 us (6%)
  between operations  1.05 us (1%)
    pallas_call x5, Pallas kernels, multiply(): pl.pallas_call(kernel, in_specs=[pl.BlockSpec(memory_space=pltpu.SMEM)] +...  37.9 us
    ppermute x10, starting transfers between devices, send(): return lax.ppermute(value, PLANE, ring(axis, step))  13.8 us
    ppermute x10, waiting for transfers between devices, send(): return lax.ppermute(value, PLANE, ring(axis, step))  11.3 us
    ppermute x4, starting transfers between devices, sibling(): return lax.ppermute(value, 'core', [(0, 1), (1, 0)])  10.2 us
    unnamed x24, local copies, waits for them, and re-layouts  6.13 us
    pallas_call x1, Pallas kernels, on_device(): pl.pallas_call(momentum_kernel, out_shape=jax.ShapeDtypeStruct(momentum.s...  5.17 us
    pallas_call x1, Pallas kernels, on_device(): pl.pallas_call(coeff_kernel, out_shape=(jax.ShapeDtypeStruct((blocks, col...  4.74 us
    pallas_call x1, Pallas kernels, on_device(): pl.pallas_call(weight_kernel, out_shape=jax.ShapeDtypeStruct((rows, cols)...  4.52 us
  transfers between devices with their start and end apart: 17, of which 7 were waited for; matrix products, arithmetic and copies ran while one was open for 1% of the time, Pallas kernels for 44%

profile of v2, /device:TPU:1, one launch (start us, length us, event | category | flops | bytes accessed | tf_op | source)
XLA Modules:
  0.0 102.2 jit_solution(7148559830556072365)
XLA Ops:
  0.7 1.5 %collective-permute-start.9 = (bf16[1024,8192]{1,0:T(8,128)(2,1)}, bf16[1024,8192]{1,0:T(8,128)(2,1)}, u32[]{:S(2)}, u32[]{:S(2)}) collective-permute-start(bf16[1024,8192]{1,0:T(8,128)(2,1)} %refs_0_.9), channel_id=1, source_target_pairs={{0,1},{1,0},{2,3},{3,2},{4,5},{5,4},{6,7},{7,6},{8,9},{9,8},{10,11... | collective-permute-start | bytes 50331656 | tf_op jit(solution)/shard_map/ppermute | solution.py:178
  3.1 4.7 %shard_map.85 = (f32[4,1024]{1,0:T(4,128)S(1)}, s32[2,4,8,1024]{3,2,1,0:T(8,128)S(1)}) custom-call(f32[1,256,1024]{2,1,0:T(8,128)} %momentum.3, f32[1,256,1024]{2,1,0:T(8,128)} %grad.3, s32[4,16,64,128]{3,2,1,0:T(8,128)} %bitcast.21, f32[256,256]{1,0:T(8,128)S(1)} %copy-done.4), custom_call_target="tpu_custom_call" | custom-call | tf_op jit(solution)/shard_map/pallas_call | solution.py:277
  7.8 2.6 %collective-permute-start.2 = (f32[4,1024]{1,0:T(4,128)S(1)}, f32[4,1024]{1,0:T(4,128)S(1)}, u32[]{:S(2)}, u32[]{:S(2)}) collective-permute-start(f32[4,1024]{1,0:T(4,128)S(1)} %get-tuple-element.26.chosen0), channel_id=1, source_target_pairs={{0,96},{32,0},{64,32},{96,64},{1,97},{33,1},{65,33},{97,65},{2,98}... | collective-permute-start | bytes 49160 | tf_op jit(solution)/shard_map/ppermute | solution.py:293
  11.6 3.0 %collective-permute-done.1.chosen2 = f32[4,1024]{1,0:T(4,128)S(1)} collective-permute-done((f32[4,1024]{1,0:T(4,128)S(1)}, f32[4,1024]{1,0:T(4,128)S(1)}, u32[]{:S(2)}, u32[]{:S(2)}) %collective-permute-start.1) | collective-permute-done | bytes 16416 | tf_op jit(solution)/shard_map/ppermute | solution.py:293
  14.8 4.5 %shard_map.86 = bf16[256,1024]{1,0:T(8,128)(2,1)} custom-call(bf16[256,1024]{1,0:T(8,128)(2,1)S(1)} %copy-done.5, f32[4,1024]{1,0:T(4,128)S(1)} %get-tuple-element.26.chosen0, f32[4,1024]{1,0:T(4,128)S(1)} %collective-permute-done.chosen1, f32[4,1024]{1,0:T(4,128)S(1)} %collective-permute-done.1.chosen2, f32[4,1024]{1,0:T(4,128)S(1)} %collective-permute-done.2.chosen3, ...), custom_call_target="tpu_custom_call" | custom-call | tf_op jit(solution)/shard_map/pallas_call | solution.py:296
  19.3 3.8 %collective-permute-start.4 = (bf16[256,1024]{1,0:T(8,128)(2,1)}, bf16[256,1024]{1,0:T(8,128)(2,1)S(1)}, u32[]{:S(2)}, u32[]{:S(2)}) collective-permute-start(bf16[256,1024]{1,0:T(8,128)(2,1)} %shard_map.86), channel_id=1, source_target_pairs={{0,24},{1,7},{2,26},{3,1},{4,28},{5,3},{6,30},{7,5},{8,0},{9,15},{... | collective-permute-start | bytes 1572872 | tf_op jit(solution)/shard_map/ppermute | solution.py:174
  23.1 5.2 %shard_map.87 = f32[1,256,1024]{2,1,0:T(8,128)} custom-call(f32[1,256,1024]{2,1,0:T(8,128)S(1)} %copy-done.2, f32[1,256,1024]{2,1,0:T(8,128)S(1)} %copy-done.3, s32[2,4,8,1024]{3,2,1,0:T(8,128)S(1)} %get-tuple-element.27.where, f32[256,256]{1,0:T(8,128)S(1)} %copy-done.4), custom_call_target="tpu_custom_call" | custom-call | tf_op jit(solution)/shard_map/pallas_call | solution.py:306
  28.3 1.3 %collective-permute-done.4 = bf16[256,1024]{1,0:T(8,128)(2,1)S(1)} collective-permute-done((bf16[256,1024]{1,0:T(8,128)(2,1)}, bf16[256,1024]{1,0:T(8,128)(2,1)S(1)}, u32[]{:S(2)}, u32[]{:S(2)}) %collective-permute-start.4) | collective-permute-done | bytes 524320 | tf_op jit(solution)/shard_map/ppermute | solution.py:174
  29.5 3.3 %collective-permute-done.3 = bf16[256,1024]{1,0:T(8,128)(2,1)S(1)} collective-permute-done((bf16[256,1024]{1,0:T(8,128)(2,1)}, bf16[256,1024]{1,0:T(8,128)(2,1)S(1)}, u32[]{:S(2)}, u32[]{:S(2)}) %collective-permute-start.3) | collective-permute-done | bytes 524320 | tf_op jit(solution)/shard_map/ppermute | solution.py:174
  33.0 1.5 %collective-permute-start.6 = (bf16[128,1024]{1,0:T(8,128)(2,1)S(1)}, bf16[128,1024]{1,0:T(8,128)(2,1)S(1)}, u32[]{:S(2)}, u32[]{:S(2)}) collective-permute-start(bf16[128,1024]{1,0:T(8,128)(2,1)S(1)} %slice.6), channel_id=1, source_target_pairs={{0,8},{1,3},{2,10},{3,5},{4,12},{5,7},{6,14},{7,1},{8,16},{9,11},{... | collective-permute-start | bytes 786440 | tf_op jit(solution)/shard_map/ppermute | solution.py:174
  35.6 4.1 %collective-permute-done.6 = bf16[128,1024]{1,0:T(8,128)(2,1)S(1)} collective-permute-done((bf16[128,1024]{1,0:T(8,128)(2,1)S(1)}, bf16[128,1024]{1,0:T(8,128)(2,1)S(1)}, u32[]{:S(2)}, u32[]{:S(2)}) %collective-permute-start.6) | collective-permute-done | bytes 262176 | tf_op jit(solution)/shard_map/ppermute | solution.py:174
  39.8 2.4 %collective-permute-start.8 = (bf16[512,1024]{1,0:T(8,128)(2,1)S(1)}, bf16[512,1024]{1,0:T(8,128)(2,1)}, u32[]{:S(2)}, u32[]{:S(2)}) collective-permute-start(bf16[512,1024]{1,0:T(8,128)(2,1)S(1)} %constant_dynamic-update-slice_fusion.refs_3_), channel_id=1, source_target_pairs={{0,6},{1,25},{2,0},{3,27},{4,2},{5,29},{6,4},{7,31},{8,14},{9,1},{... | collective-permute-start | bytes 3145736 | tf_op jit(solution)/shard_map/ppermute | solution.py:174
  42.3 1.3 %collective-permute-start.13 = (bf16[512,1024]{1,0:T(8,128)(2,1)S(1)}, bf16[512,1024]{1,0:T(8,128)(2,1)}, u32[]{:S(2)}, u32[]{:S(2)}) collective-permute-start(bf16[512,1024]{1,0:T(8,128)(2,1)S(1)} %pad_maximum_fusion.refs_2_), channel_id=1, source_target_pairs={{0,6},{1,25},{2,0},{3,27},{4,2},{5,29},{6,4},{7,31},{8,14},{9,1},{... | collective-permute-start | bytes 3145736 | tf_op jit(solution)/shard_map/ppermute | solution.py:174
  44.0 7.5 %shard_map.88 = (f32[1024,1024]{1,0:T(8,128)S(1)}, f32[1024,1024]{1,0:T(8,128)S(1)}, f32[8,128]{1,0:T(8,128)S(1)}) custom-call(s32[4]{0:T(128)S(1)} %pad_add_fusion.2.ids, f32[8,128]{1,0:T(8,128)S(1)} %broadcast_in_dim.3._, bf16[1024,8192]{1,0:T(8,128)(2,1)} %refs_0_.9, bf16[1024,8192]{1,0:T(8,128)(2,1)} %collective-permute-done.9.refs_1_, ...), custom_call_target="tpu_custom_call" | custom-call | flops 1000 | bytes 1000 | tf_op jit(solution)/shard_map/pallas_call | solution.py:251
  52.5 1.5 %collective-permute-done.8.refs_3_ = bf16[512,1024]{1,0:T(8,128)(2,1)} collective-permute-done((bf16[512,1024]{1,0:T(8,128)(2,1)S(1)}, bf16[512,1024]{1,0:T(8,128)(2,1)}, u32[]{:S(2)}, u32[]{:S(2)}) %collective-permute-start.8) | collective-permute-done | bytes 1048608 | tf_op jit(solution)/shard_map/ppermute | solution.py:174
  54.0 1.6 %collective-permute-start.10 = (bf16[512,1024]{1,0:T(8,128)(2,1)S(1)}, bf16[512,1024]{1,0:T(8,128)(2,1)}, u32[]{:S(2)}, u32[]{:S(2)}) collective-permute-start(bf16[512,1024]{1,0:T(8,128)(2,1)S(1)} %collective-permute-done.5.refs_2_), channel_id=1, source_target_pairs={{0,2},{1,9},{2,4},{3,11},{4,6},{5,13},{6,0},{7,15},{8,10},{9,17},{... | collective-permute-start | bytes 3145736 | tf_op jit(solution)/shard_map/ppermute | solution.py:174
  55.6 2.0 %collective-permute-start.11 = (bf16[512,1024]{1,0:T(8,128)(2,1)}, bf16[512,1024]{1,0:T(8,128)(2,1)}, u32[]{:S(2)}, u32[]{:S(2)}) collective-permute-start(bf16[512,1024]{1,0:T(8,128)(2,1)} %collective-permute-done.8.refs_3_), channel_id=1, source_target_pairs={{0,6},{1,25},{2,0},{3,27},{4,2},{5,29},{6,4},{7,31},{8,14},{9,1},{... | collective-permute-start | bytes 3145736 | tf_op jit(solution)/shard_map/ppermute | solution.py:174
  57.5 8.3 %shard_map.89 = (f32[1024,1024]{1,0:T(8,128)S(1)}, f32[1024,1024]{1,0:T(8,128)S(1)}, f32[8,128]{1,0:T(8,128)S(1)}) custom-call(s32[4]{0:T(128)S(1)} %pad_add_fusion.4.ids, f32[8,128]{1,0:T(8,128)S(1)} %get-tuple-element.33._, bf16[1024,8192]{1,0:T(8,128)(2,1)} %refs_0_.9, ...), custom_call_target="tpu_custom_call", output_to_operand_aliasing={{0}: (6, {}), {1}: (7, {})} | custom-call | flops 1000 | bytes 1000 | tf_op jit(solution)/shard_map/pallas_call | solution.py:251
  65.8 9.3 %shard_map.90 = (f32[1024,1024]{1,0:T(8,128)S(1)}, bf16[1024,1024]{1,0:T(8,128)(2,1)}, f32[8,128]{1,0:T(8,128)S(1)}) custom-call(s32[4]{0:T(128)S(1)} %pad_add_fusion.3.ids, f32[8,128]{1,0:T(8,128)S(1)} %get-tuple-element.36._, bf16[1024,8192]{1,0:T(8,128)(2,1)} %refs_0_.9, ...), custom_call_target="tpu_custom_call", output_to_operand_aliasing={{0}: (6, {})} | custom-call | flops 1000 | bytes 1000 | tf_op jit(solution)/shard_map/pallas_call | solution.py:251
  75.2 1.9 %copy-done = f32[1024,1024]{1,0:T(8,128)} copy-done((f32[1024,1024]{1,0:T(8,128)}, f32[1024,1024]{1,0:T(8,128)S(1)}, u32[]{:S(2)}) %copy-start) | copy-done | bytes 4194328
  77.1 8.2 %collective-permute-start.16 = (bf16[1024,1024]{1,0:T(8,128)(2,1)}, bf16[1024,1024]{1,0:T(8,128)(2,1)S(1)}, u32[]{:S(2)}, u32[]{:S(2)}) collective-permute-start(bf16[1024,1024]{1,0:T(8,128)(2,1)} %get-tuple-element.46), channel_id=1, source_target_pairs={{0,1},{1,0},{2,3},{3,2},{4,5},{5,4},{6,7},{7,6},{8,9},{9,8},{10,11... | collective-permute-start | bytes 6291464 | tf_op jit(solution)/shard_map/ppermute | solution.py:178
  86.0 2.2 %copy-done.1 = f32[1024,1024]{1,0:T(8,128)S(1)} copy-done((f32[1024,1024]{1,0:T(8,128)S(1)}, f32[1024,1024]{1,0:T(8,128)}, u32[]{:S(2)}) %copy-start.1) | copy-done | bytes 4194328
  88.2 5.8 %shard_map.91 = (f32[1024,1024]{1,0:T(8,128)S(1)}, f32[8,128]{1,0:T(8,128)S(1)}) custom-call(s32[4]{0:T(128)S(1)} %pad_add_fusion.1.ids, f32[8,128]{1,0:T(8,128)S(1)} %get-tuple-element.40._, bf16[1024,8192]{1,0:T(8,128)(2,1)} %refs_0_.9, bf16[512,1024]{1,0:T(8,128)(2,1)} %collective-permute-done.10.refs_1_, ...), custom_call_target="tpu_custom_call", output_to_operand_aliasing={{0}: (5, {})} | custom-call | flops 1000 | bytes 1000 | tf_op jit(solution)/shard_map/pallas_call | solution.py:251
  95.0 7.0 %shard_map.92 = (bf16[1024,1024]{1,0:T(8,128)(2,1)}, f32[8,128]{1,0:T(8,128)}) custom-call(s32[4]{0:T(128)S(1)} %pad_add_fusion.ids, f32[8,128]{1,0:T(8,128)S(1)} %get-tuple-element.44._, bf16[1024,8192]{1,0:T(8,128)(2,1)} %refs_0_.9, bf16[512,1024]{1,0:T(8,128)(2,1)} %copy-done.10, bf16[512,1024]{1,0:T(8,128)(2,1)} %collective-permute-done.15.refs_2_, ...), custom_call_target="tpu_custom_call" | custom-call | flops 1000 | bytes 1000 | tf_op jit(solution)/shard_map/pallas_call | solution.py:251
  (52 shorter events, 6.8 us)
Async XLA Ops:
  0.6 22.5 %copy-start.3 = (f32[1,256,1024]{2,1,0:T(8,128)S(1)}, f32[1,256,1024]{2,1,0:T(8,128)}, u32[]{:S(2)}) copy-start(f32[1,256,1024]{2,1,0:T(8,128)} %grad.3) | copy-start | bytes 3145732
  0.6 22.4 %copy-start.2 = (f32[1,256,1024]{2,1,0:T(8,128)S(1)}, f32[1,256,1024]{2,1,0:T(8,128)}, u32[]{:S(2)}) copy-start(f32[1,256,1024]{2,1,0:T(8,128)} %momentum.3) | copy-start | bytes 3145732
  0.7 43.3 %collective-permute-start.9 = (bf16[1024,8192]{1,0:T(8,128)(2,1)}, bf16[1024,8192]{1,0:T(8,128)(2,1)}, u32[]{:S(2)}, u32[]{:S(2)}) collective-permute-start(bf16[1024,8192]{1,0:T(8,128)(2,1)} %refs_0_.9), channel_id=1, source_target_pairs={{0,1},{1,0},{2,3},{3,2},{4,5},{5,4},{6,7},{7,6},{8,9},{9,8},{10,11... | collective-permute-start | bytes 50331656 | tf_op jit(solution)/shard_map/ppermute | solution.py:178
  3.1 11.7 %copy-start.5 = (bf16[256,1024]{1,0:T(8,128)(2,1)S(1)}, bf16[256,1024]{1,0:T(8,128)(2,1)}, u32[]{:S(2)}) copy-start(bf16[256,1024]{1,0:T(8,128)(2,1)} %weight.1) | copy-start | bytes 1572868
  7.8 3.8 %collective-permute-start.2 = (f32[4,1024]{1,0:T(4,128)S(1)}, f32[4,1024]{1,0:T(4,128)S(1)}, u32[]{:S(2)}, u32[]{:S(2)}) collective-permute-start(f32[4,1024]{1,0:T(4,128)S(1)} %get-tuple-element.26.chosen0), channel_id=1, source_target_pairs={{0,96},{32,0},{64,32},{96,64},{1,97},{33,1},{65,33},{97,65},{2,98}... | collective-permute-start | bytes 49160 | tf_op jit(solution)/shard_map/ppermute | solution.py:293
  10.5 4.1 %collective-permute-start.1 = (f32[4,1024]{1,0:T(4,128)S(1)}, f32[4,1024]{1,0:T(4,128)S(1)}, u32[]{:S(2)}, u32[]{:S(2)}) collective-permute-start(f32[4,1024]{1,0:T(4,128)S(1)} %get-tuple-element.26.chosen0), channel_id=1, source_target_pairs={{0,64},{32,96},{64,0},{96,32},{1,65},{33,97},{65,1},{97,33},{2,66}... | collective-permute-start | bytes 49160 | tf_op jit(solution)/shard_map/ppermute | solution.py:293
  11.0 3.8 %collective-permute-start = (f32[4,1024]{1,0:T(4,128)S(1)}, f32[4,1024]{1,0:T(4,128)S(1)}, u32[]{:S(2)}, u32[]{:S(2)}) collective-permute-start(f32[4,1024]{1,0:T(4,128)S(1)} %get-tuple-element.26.chosen0), channel_id=1, source_target_pairs={{0,32},{32,64},{64,96},{96,0},{1,33},{33,65},{65,97},{97,1},{2,34}... | collective-permute-start | bytes 49160 | tf_op jit(solution)/shard_map/ppermute | solution.py:293
  19.3 15.1 %copy-start.8 = (bf16[256,1024]{1,0:T(8,128)(2,1)S(1)}, bf16[256,1024]{1,0:T(8,128)(2,1)}, u32[]{:S(2)}) copy-start(bf16[256,1024]{1,0:T(8,128)(2,1)} %shard_map.86) | copy-start | bytes 1572868
  19.3 10.2 %collective-permute-start.4 = (bf16[256,1024]{1,0:T(8,128)(2,1)}, bf16[256,1024]{1,0:T(8,128)(2,1)S(1)}, u32[]{:S(2)}, u32[]{:S(2)}) collective-permute-start(bf16[256,1024]{1,0:T(8,128)(2,1)} %shard_map.86), channel_id=1, source_target_pairs={{0,24},{1,7},{2,26},{3,1},{4,28},{5,3},{6,30},{7,5},{8,0},{9,15},{... | collective-permute-start | bytes 1572872 | tf_op jit(solution)/shard_map/ppermute | solution.py:174
  23.1 9.7 %collective-permute-start.3 = (bf16[256,1024]{1,0:T(8,128)(2,1)}, bf16[256,1024]{1,0:T(8,128)(2,1)S(1)}, u32[]{:S(2)}, u32[]{:S(2)}) collective-permute-start(bf16[256,1024]{1,0:T(8,128)(2,1)} %shard_map.86), channel_id=1, source_target_pairs={{0,8},{1,3},{2,10},{3,5},{4,12},{5,7},{6,14},{7,1},{8,16},{9,11},{... | collective-permute-start | bytes 1572872 | tf_op jit(solution)/shard_map/ppermute | solution.py:174
  32.9 6.9 %collective-permute-start.7 = (bf16[128,1024]{1,0:T(8,128)(2,1)S(1)}, bf16[128,1024]{1,0:T(8,128)(2,1)S(1)}, u32[]{:S(2)}, u32[]{:S(2)}) collective-permute-start(bf16[128,1024]{1,0:T(8,128)(2,1)S(1)} %slice.7), channel_id=1, source_target_pairs={{0,24},{1,7},{2,26},{3,1},{4,28},{5,3},{6,30},{7,5},{8,0},{9,15},{... | collective-permute-start | bytes 786440 | tf_op jit(solution)/shard_map/ppermute | solution.py:174
  33.0 6.8 %collective-permute-start.6 = (bf16[128,1024]{1,0:T(8,128)(2,1)S(1)}, bf16[128,1024]{1,0:T(8,128)(2,1)S(1)}, u32[]{:S(2)}, u32[]{:S(2)}) collective-permute-start(bf16[128,1024]{1,0:T(8,128)(2,1)S(1)} %slice.6), channel_id=1, source_target_pairs={{0,8},{1,3},{2,10},{3,5},{4,12},{5,7},{6,14},{7,1},{8,16},{9,11},{... | collective-permute-start | bytes 786440 | tf_op jit(solution)/shard_map/ppermute | solution.py:174
  34.5 9.5 %copy-start.6 = (bf16[512,1024]{1,0:T(8,128)(2,1)}, bf16[512,1024]{1,0:T(8,128)(2,1)S(1)}, u32[]{:S(2)}) copy-start(bf16[512,1024]{1,0:T(8,128)(2,1)S(1)} %pad_maximum_fusion.refs_2_) | copy-start | bytes 3145732
  34.5 18.0 %collective-permute-start.5 = (bf16[512,1024]{1,0:T(8,128)(2,1)S(1)}, bf16[512,1024]{1,0:T(8,128)(2,1)S(1)}, u32[]{:S(2)}, u32[]{:S(2)}) collective-permute-start(bf16[512,1024]{1,0:T(8,128)(2,1)S(1)} %pad_maximum_fusion.refs_2_), channel_id=1, source_target_pairs={{0,2},{1,9},{2,4},{3,11},{4,6},{5,13},{6,0},{7,15},{8,10},{9,17},{... | collective-permute-start | bytes 3145736 | tf_op jit(solution)/shard_map/ppermute | solution.py:174
  39.8 4.2 %copy-start.7 = (bf16[512,1024]{1,0:T(8,128)(2,1)}, bf16[512,1024]{1,0:T(8,128)(2,1)S(1)}, u32[]{:S(2)}) copy-start(bf16[512,1024]{1,0:T(8,128)(2,1)S(1)} %constant_dynamic-update-slice_fusion.refs_3_) | copy-start | bytes 3145732
  39.8 14.2 %collective-permute-start.8 = (bf16[512,1024]{1,0:T(8,128)(2,1)S(1)}, bf16[512,1024]{1,0:T(8,128)(2,1)}, u32[]{:S(2)}, u32[]{:S(2)}) collective-permute-start(bf16[512,1024]{1,0:T(8,128)(2,1)S(1)} %constant_dynamic-update-slice_fusion.refs_3_), channel_id=1, source_target_pairs={{0,6},{1,25},{2,0},{3,27},{4,2},{5,29},{6,4},{7,31},{8,14},{9,1},{... | collective-permute-start | bytes 3145736 | tf_op jit(solution)/shard_map/ppermute | solution.py:174
  42.3 23.6 %collective-permute-start.13 = (bf16[512,1024]{1,0:T(8,128)(2,1)S(1)}, bf16[512,1024]{1,0:T(8,128)(2,1)}, u32[]{:S(2)}, u32[]{:S(2)}) collective-permute-start(bf16[512,1024]{1,0:T(8,128)(2,1)S(1)} %pad_maximum_fusion.refs_2_), channel_id=1, source_target_pairs={{0,6},{1,25},{2,0},{3,27},{4,2},{5,29},{6,4},{7,31},{8,14},{9,1},{... | collective-permute-start | bytes 3145736 | tf_op jit(solution)/shard_map/ppermute | solution.py:174
  43.6 22.3 %collective-permute-start.12 = (bf16[512,1024]{1,0:T(8,128)(2,1)S(1)}, bf16[512,1024]{1,0:T(8,128)(2,1)}, u32[]{:S(2)}, u32[]{:S(2)}) collective-permute-start(bf16[512,1024]{1,0:T(8,128)(2,1)S(1)} %constant_dynamic-update-slice_fusion.refs_3_), channel_id=1, source_target_pairs={{0,2},{1,9},{2,4},{3,11},{4,6},{5,13},{6,0},{7,15},{8,10},{9,17},{... | collective-permute-start | bytes 3145736 | tf_op jit(solution)/shard_map/ppermute | solution.py:174
  52.5 5.0 %copy-start.9 = (bf16[512,1024]{1,0:T(8,128)(2,1)}, bf16[512,1024]{1,0:T(8,128)(2,1)S(1)}, u32[]{:S(2)}) copy-start(bf16[512,1024]{1,0:T(8,128)(2,1)S(1)} %collective-permute-done.5.refs_2_) | copy-start | bytes 3145732
  54.0 31.4 %collective-permute-start.10 = (bf16[512,1024]{1,0:T(8,128)(2,1)S(1)}, bf16[512,1024]{1,0:T(8,128)(2,1)}, u32[]{:S(2)}, u32[]{:S(2)}) collective-permute-start(bf16[512,1024]{1,0:T(8,128)(2,1)S(1)} %collective-permute-done.5.refs_2_), channel_id=1, source_target_pairs={{0,2},{1,9},{2,4},{3,11},{4,6},{5,13},{6,0},{7,15},{8,10},{9,17},{... | collective-permute-start | bytes 3145736 | tf_op jit(solution)/shard_map/ppermute | solution.py:174
  55.6 29.8 %collective-permute-start.11 = (bf16[512,1024]{1,0:T(8,128)(2,1)}, bf16[512,1024]{1,0:T(8,128)(2,1)}, u32[]{:S(2)}, u32[]{:S(2)}) collective-permute-start(bf16[512,1024]{1,0:T(8,128)(2,1)} %collective-permute-done.8.refs_3_), channel_id=1, source_target_pairs={{0,6},{1,25},{2,0},{3,27},{4,2},{5,29},{6,4},{7,31},{8,14},{9,1},{... | collective-permute-start | bytes 3145736 | tf_op jit(solution)/shard_map/ppermute | solution.py:174
  77.1 16.9 %collective-permute-start.16 = (bf16[1024,1024]{1,0:T(8,128)(2,1)}, bf16[1024,1024]{1,0:T(8,128)(2,1)S(1)}, u32[]{:S(2)}, u32[]{:S(2)}) collective-permute-start(bf16[1024,1024]{1,0:T(8,128)(2,1)} %get-tuple-element.46), channel_id=1, source_target_pairs={{0,1},{1,0},{2,3},{3,2},{4,5},{5,4},{6,7},{7,6},{8,9},{9,8},{10,11... | collective-permute-start | bytes 6291464 | tf_op jit(solution)/shard_map/ppermute | solution.py:178
  85.4 8.7 %collective-permute-start.14 = (bf16[512,1024]{1,0:T(8,128)(2,1)}, bf16[512,1024]{1,0:T(8,128)(2,1)S(1)}, u32[]{:S(2)}, u32[]{:S(2)}) collective-permute-start(bf16[512,1024]{1,0:T(8,128)(2,1)} %collective-permute-done.10.refs_1_), channel_id=1, source_target_pairs={{0,1},{1,0},{2,3},{3,2},{4,5},{5,4},{6,7},{7,6},{8,9},{9,8},{10,11... | collective-permute-start | bytes 3145736 | tf_op jit(solution)/shard_map/ppermute | solution.py:178
  85.4 8.6 %collective-permute-start.15 = (bf16[512,1024]{1,0:T(8,128)(2,1)}, bf16[512,1024]{1,0:T(8,128)(2,1)}, u32[]{:S(2)}, u32[]{:S(2)}) collective-permute-start(bf16[512,1024]{1,0:T(8,128)(2,1)} %collective-permute-done.11.refs_2_), channel_id=1, source_target_pairs={{0,1},{1,0},{2,3},{3,2},{4,5},{5,4},{6,7},{7,6},{8,9},{9,8},{10,11... | collective-permute-start | bytes 3145736 | tf_op jit(solution)/shard_map/ppermute | solution.py:178
  (4 other events, 6.1 us)

commit v3 on v2

--- a/solution.py
+++ b/solution.py
@@ -20,10 +20,10 @@
 NT = (((1,), (1,)), ((), ()))
 TN = (((0,), (0,)), ((), ()))
 VM = pl.BlockSpec(memory_space=pltpu.VMEM)
-HBM = pl.BlockSpec(memory_space=pltpu.HBM)
+ANY = pl.BlockSpec(memory_space=pl.ANY)
 PARAMS = pltpu.CompilerParams(vmem_limit_bytes=32 * 2**20)
 ALONE = pltpu.CompilerParams(vmem_limit_bytes=60 * 2**20)
-FLOPS, BYTES = 1000, 1000
+SMALL = pl.CostEstimate(flops=1000, bytes_accessed=1000, transcendentals=0)
 
 
 def dct_blocks(size):
@@ -59,17 +59,16 @@
     return jnp.where(is_row(target, rows), 1.0, 0.0).astype(jnp.bfloat16)
 
 
-def coeff_kernel(momentum, grad, selection, basis, chosen, where, mom, gra, sel, sems):
+def coeff_kernel(momentum, grad, selection, basis, chosen, where, mom, gra, sel, dct, sems):
     blocks = mom.shape[0] // GROUP
     copies = [
         pltpu.make_async_copy(selection, sel, sems.at[0]),
         pltpu.make_async_copy(momentum.at[0], mom, sems.at[1]),
         pltpu.make_async_copy(grad.at[0], gra, sems.at[2]),
+        pltpu.make_async_copy(basis, dct, sems.at[3]),
     ]
     for copy in copies:
         copy.start()
-    base = basis[...]
-    base = halves(base)
     first = ((lax.axis_index("y") * SIDE + lax.axis_index("z")) * 2 + lax.axis_index("core")) * blocks
     lanes = sel.shape[3]
     cols = sel.shape[1] * KEEP
@@ -87,8 +86,9 @@
         both = both.astype(jnp.int32)
         where[0, r] = both[:8]
         where[1, r] = both[8:] + shift
-    copies[1].wait()
-    copies[2].wait()
+    for copy in copies[1:]:
+        copy.wait()
+    base = halves(dct[...])
     moment = halves(beta_decay * mom[...] + gra[...])
     inner = halves(dot3(base, moment, plain(((1,), (0,)))))
     own = lax.axis_index("x")
@@ -178,17 +178,21 @@
     return lax.ppermute(value, "core", [(0, 1), (1, 0)])
 
 
-def shard_at(u, v, other=False):
+def shard_places():
     y, z, c = lax.axis_index("y"), lax.axis_index("z"), lax.axis_index("core")
-    if other:
-        c = 1 - c
-    along = lambda at, step: lax.rem(at + step + SIDE, SIDE)
-    even = along(y, u) * SIDE + along(z, v)
-    odd = along(y, v) * SIDE + along(z, u)
-    return 2 * jnp.where(c == 0, even, odd) + c
-
-
-def multiply(jobs, shards, pieces, dtypes, after=None, chunks=((0, 1024),)):
+    k = np.arange(2 * SIDE * SIDE)
+    u, v = jnp.asarray(k // SIDE % SIDE, jnp.int32), jnp.asarray(k % SIDE, jnp.int32)
+    core = jnp.where(jnp.asarray(k < SIDE * SIDE), c, 1 - c)
+    even = jnp.bitwise_and(y + u, 3) * SIDE + jnp.bitwise_and(z + v, 3)
+    odd = jnp.bitwise_and(y + v, 3) * SIDE + jnp.bitwise_and(z + u, 3)
+    return 2 * jnp.where(core == 0, even, odd) + core
+
+
+def at(*offsets, other=False):
+    return [(u % SIDE) * SIDE + v % SIDE + (SIDE * SIDE if other else 0) for u, v in offsets]
+
+
+def multiply(places, jobs, shards, pieces, dtypes, after=None, chunks=((0, 1024),)):
     cols = pieces[0].shape[1]
     depth, tile = 256, 256
     count = len(shards)
@@ -221,7 +225,7 @@
             n, at, size = plan[q]
             for k in range(count):
                 copies[q, k] = pltpu.make_async_copy(
-                    toks[n].at[pl.ds(at, size), pl.ds(pl.multiple_of(ids[k] * depth, depth), depth)],
+                    toks[n].at[pl.ds(at, size), pl.ds(pl.multiple_of(ids[shards[k]] * depth, depth), depth)],
                     left.at[n, pl.ds(at, size), pl.ds(k * depth, depth)],
                     sems.at[q, k],
                 )
@@ -250,7 +254,7 @@
 
     return pl.pallas_call(
         kernel,
-        in_specs=[pl.BlockSpec(memory_space=pltpu.SMEM)] + [HBM] * (1 + n_jobs + n_pieces) + [VM] * n_adds,
+        in_specs=[pl.BlockSpec(memory_space=pltpu.SMEM)] + [ANY] * (1 + n_jobs + n_pieces) + [VM] * n_adds,
         out_specs=[VM] * (n_jobs + 1),
         out_shape=[result(dtype) for dtype in dtypes] + [jax.ShapeDtypeStruct((8, 128), jnp.float32)],
         scratch_shapes=[
@@ -259,10 +263,10 @@
             pltpu.SemaphoreType.DMA((n_jobs * len(chunks), count)),
             pltpu.SemaphoreType.DMA((n_pieces,)),
         ],
-        compiler_params=pltpu.CompilerParams(vmem_limit_bytes=24 * 2**20),
-        cost_estimate=pl.CostEstimate(flops=FLOPS, bytes_accessed=BYTES, transcendentals=0),
+        compiler_params=pltpu.CompilerParams(vmem_limit_bytes=16 * 2**20),
+        cost_estimate=SMALL,
         input_output_aliases=aliases,
-    )(jnp.stack(shards).astype(jnp.int32), after, *[in_hbm(t) for t, _ in jobs], *[in_hbm(p) for p in pieces], *adds)
+    )(places, after, *[in_hbm(t) for t, _ in jobs], *pieces, *adds)
 
 
 def in_hbm(value):
@@ -280,16 +284,18 @@
             jax.ShapeDtypeStruct((blocks, cols), jnp.float32),
             jax.ShapeDtypeStruct((2, REPS, 8, cols), jnp.int32),
         ),
-        in_specs=[HBM, HBM, HBM, VM],
+        in_specs=[ANY] * 4,
         out_specs=(VM, VM),
         scratch_shapes=[
             pltpu.VMEM((rows, cols), jnp.float32),
             pltpu.VMEM((rows, cols), jnp.float32),
             pltpu.VMEM(lanes.shape, jnp.int32),
-            pltpu.SemaphoreType.DMA((3,)),
+            pltpu.VMEM(basis.shape, jnp.float32),
+            pltpu.SemaphoreType.DMA((4,)),
         ],
         compiler_params=PARAMS,
-    )(in_hbm(momentum), in_hbm(grad), in_hbm(lanes), basis)
+        cost_estimate=SMALL,
+    )(in_hbm(momentum), in_hbm(grad), in_hbm(lanes), in_hbm(basis))
     along_x = lambda step: lax.ppermute(chosen, "x", [(i, (i + step) % REPS) for i in range(REPS)])
     others = [along_x(k) for k in range(1, REPS)]
     tokens_too = sibling(tokens)
@@ -300,8 +306,10 @@
         out_specs=VM,
         scratch_shapes=[pltpu.VMEM((rows, cols), jnp.float32)],
         compiler_params=PARAMS,
+        cost_estimate=SMALL,
     )(weight, chosen, *others, where, basis)
 
+    places = shard_places()
     am, ap = send(shard, "u", 1), send(shard, "u", -1)
     new_momentum = pl.pallas_call(
         momentum_kernel,
@@ -310,44 +318,48 @@
         out_specs=VM,
         scratch_shapes=[pltpu.VMEM((rows, cols), jnp.float32)],
         compiler_params=PARAMS,
+        cost_estimate=SMALL,
     )(momentum, grad, where, basis)
     am, ap, new_momentum = lax.optimization_barrier((am, ap, new_momentum))
     top, bottom = send(am[: rows // 2], "u", 1), send(ap[rows // 2 :], "u", -1)
     s1 = jnp.concatenate([shard, am], axis=0)
-    s2 = jnp.concatenate([ap, top, bottom], axis=0)
-    r1p, r2m = send(s1, "v", 1), send(s2, "v", -1)
-    r2p, r1m = send(s2, "v", 1), send(s1, "v", -1)
+    r1p, r1m = send(s1, "v", 1), send(s1, "v", -1)
     f32, bf16 = jnp.float32, jnp.bfloat16
     mine, theirs, ran = multiply(
-        [(tokens, ()), (tokens_too, ())],
-        [shard_at(0, 0), shard_at(-1, 0), shard_at(1, 0), shard_at(2, 0)],
-        [s1, s2],
+        places, [(tokens, ()), (tokens_too, ())], at((0, 0), (-1, 0)), [s1], [f32, f32]
+    )
+    top, bottom, ran = lax.optimization_barrier((top, bottom, ran))
+    s2 = jnp.concatenate([ap, top, bottom], axis=0)
+    r2p, r2m = send(s2, "v", 1), send(s2, "v", -1)
+    f1 = send(r1p, "v", 1)
+    mine, theirs, ran = multiply(
+        places,
+        [(tokens, (mine,)), (tokens_too, (theirs,))],
+        at((1, 0), (2, 0), (0, -1), (-1, -1), (0, 1), (-1, 1)),
+        [s2, r1p, r1m],
         [f32, f32],
-    )
-    r1p, r2m, ran = lax.optimization_barrier((r1p, r2m, ran))
-    f1, f2 = send(r1p, "v", 1), send(r2m, "v", -1)
+        ran,
+    )
+    r2m, ran = lax.optimization_barrier((r2m, ran))
+    f2 = send(r2m, "v", -1)
     mine, theirs, ran = multiply(
+        places,
         [(tokens, (mine,)), (tokens_too, (theirs,))],
-        [shard_at(0, -1), shard_at(-1, -1), shard_at(1, 1), shard_at(2, 1)],
-        [r1p, r2m],
-        [f32, f32],
-        after=ran,
-    )
-    mine, theirs, ran = multiply(
-        [(tokens, (mine,)), (tokens_too, (theirs,))],
-        [shard_at(1, -1), shard_at(2, -1), shard_at(0, 1), shard_at(-1, 1)],
-        [r2p, r1m],
+        at((1, -1), (2, -1), (1, 1), (2, 1)),
+        [r2p, r2m],
         [f32, bf16],
-        after=ran,
+        ran,
     )
     theirs = sibling(theirs)
-    f1, f2, ran = lax.optimization_barrier((f1, f2, ran))
-    g1, g2 = sibling(f1), sibling(f2)
-    far = [(0, 2), (-1, 2), (1, 2), (2, 2)]
-    split = ((0, 256), (256, 768))
-    mine, ran = multiply([(tokens, (mine,))], [shard_at(*at) for at in far], [f1, f2], [f32], ran, split)
+    f1, ran = lax.optimization_barrier((f1, ran))
+    g1 = sibling(f1)
+    g2 = sibling(f2)
+    near, far = [(0, 2), (-1, 2)], [(1, 2), (2, 2)]
+    mine, ran = multiply(
+        places, [(tokens, (mine,))], at(*near) + at(*near, other=True), [f1, g1], [f32], ran
+    )
     keys, _ = multiply(
-        [(tokens, (mine, theirs))], [shard_at(*at, other=True) for at in far], [g1, g2], [bf16], ran, split
+        places, [(tokens, (mine, theirs))], at(*far) + at(*far, other=True), [f2, g2], [bf16], ran
     )
     return keys, shard, new_momentum
 

time: 103 us -> 90.1 us (0.87)
  local copies, waits for them, and re-layouts: 6.19 us -> 0.15 us
  Pallas kernels: 52.3 us -> 47.7 us
  starting transfers between devices: 27.8 us -> 25.5 us
    unnamed x24 -> x18, local copies, waits for them, and re-layouts: 6.13 us -> 0.09 us
    pallas_call x5, Pallas kernels: 37.9 us -> 33.2 us  [multiply(): pl.pallas_call(kernel, in_specs=[pl.BlockSpec(memory_space=pltpu.SMEM)] +...]
    ppermute x4, starting transfers between devices: 10.2 us -> 6.76 us  [sibling(): return lax.ppermute(value, 'core', [(0, 1), (1, 0)])]
    ppermute x10, waiting for transfers between devices: 11.3 us -> 13.2 us  [send(): return lax.ppermute(value, PLANE, ring(axis, step))]
    ppermute x3, waiting for transfers between devices: 3.19 us -> 1.61 us  [on_device(): lax.ppermute(chosen, 'x', [(i, (i + step) % REPS) for i in range(REPS)])]
    ppermute x3, starting transfers between devices: 3.75 us -> 5.05 us  [on_device(): lax.ppermute(chosen, 'x', [(i, (i + step) % REPS) for i in range(REPS)])]
  transfers between devices with their start and end apart: 17 -> 17, of which waited for: 7 -> 8; matrix products, arithmetic and copies ran while one was open for 1% -> 0% of each run, Pallas kernels for 44% -> 46%
where the time goes in v3:
time: 90.1 us; the launch traced here: 89.8 us
  Pallas kernels  47.7 us (53%)
  starting transfers between devices  25.5 us (28%)
  waiting for transfers between devices  15.4 us (17%)
  between operations  1.01 us (1%)
    pallas_call x5, Pallas kernels, multiply(): pl.pallas_call(kernel, in_specs=[pl.BlockSpec(memory_space=pltpu.SMEM)] +...  33.2 us
    ppermute x10, starting transfers between devices, send(): return lax.ppermute(value, PLANE, ring(axis, step))  13.7 us
    ppermute x10, waiting for transfers between devices, send(): return lax.ppermute(value, PLANE, ring(axis, step))  13.2 us
    ppermute x4, starting transfers between devices, sibling(): return lax.ppermute(value, 'core', [(0, 1), (1, 0)])  6.76 us
    pallas_call x1, Pallas kernels, on_device(): pl.pallas_call(momentum_kernel, out_shape=jax.ShapeDtypeStruct(momentum.s...  5.23 us
    ppermute x3, starting transfers between devices, on_device(): lax.ppermute(chosen, 'x', [(i, (i + step) % REPS) for i in range(REPS)])  5.05 us
    pallas_call x1, Pallas kernels, on_device(): pl.pallas_call(coeff_kernel, out_shape=(jax.ShapeDtypeStruct((blocks, col...  4.73 us
    pallas_call x1, Pallas kernels, on_device(): pl.pallas_call(weight_kernel, out_shape=jax.ShapeDtypeStruct((rows, cols)...  4.54 us
  transfers between devices with their start and end apart: 17, of which 8 were waited for; matrix products, arithmetic and copies ran while one was open for 0% of the time, Pallas kernels for 46%

profile of v3, /device:TPU:1, one launch (start us, length us, event | category | flops | bytes accessed | tf_op | source)
XLA Modules:
  0.0 89.8 jit_solution(6946765757127721807)
XLA Ops:
  0.7 1.5 %collective-permute-start.9 = (bf16[1024,8192]{1,0:T(8,128)(2,1)}, bf16[1024,8192]{1,0:T(8,128)(2,1)}, u32[]{:S(2)}, u32[]{:S(2)}) collective-permute-start(bf16[1024,8192]{1,0:T(8,128)(2,1)} %refs_0_.9), channel_id=1, source_target_pairs={{0,1},{1,0},{2,3},{3,2},{4,5},{5,4},{6,7},{7,6},{8,9},{9,8},{10,11... | collective-permute-start | bytes 50331656 | tf_op jit(solution)/shard_map/ppermute | solution.py:178
  2.2 4.7 %shard_map.112 = (f32[4,1024]{1,0:T(4,128)S(1)}, s32[2,4,8,1024]{3,2,1,0:T(8,128)S(1)}) custom-call(f32[1,256,1024]{2,1,0:T(8,128)} %momentum.3, f32[1,256,1024]{2,1,0:T(8,128)} %grad.3, s32[4,16,64,128]{3,2,1,0:T(8,128)} %bitcast.1, f32[256,256]{1,0:T(8,128)} %constant.31.clone.basis), custom_call_target="tpu_custom_call" | custom-call | flops 1000 | bytes 1000 | tf_op jit(solution)/shard_map/pallas_call | solution.py:281
  6.9 1.5 %collective-permute-start = (f32[4,1024]{1,0:T(4,128)S(1)}, f32[4,1024]{1,0:T(4,128)S(1)}, u32[]{:S(2)}, u32[]{:S(2)}) collective-permute-start(f32[4,1024]{1,0:T(4,128)S(1)} %get-tuple-element.27.chosen0), channel_id=1, source_target_pairs={{0,32},{32,64},{64,96},{96,0},{1,33},{33,65},{65,97},{97,1},{2,34}... | collective-permute-start | bytes 49160 | tf_op jit(solution)/shard_map/ppermute | solution.py:299
  8.4 2.4 %collective-permute-start.1 = (f32[4,1024]{1,0:T(4,128)S(1)}, f32[4,1024]{1,0:T(4,128)S(1)}, u32[]{:S(2)}, u32[]{:S(2)}) collective-permute-start(f32[4,1024]{1,0:T(4,128)S(1)} %get-tuple-element.27.chosen0), channel_id=1, source_target_pairs={{0,64},{32,96},{64,0},{96,32},{1,65},{33,97},{65,1},{97,33},{2,66}... | collective-permute-start | bytes 49160 | tf_op jit(solution)/shard_map/ppermute | solution.py:299
  10.8 1.1 %collective-permute-start.2 = (f32[4,1024]{1,0:T(4,128)S(1)}, f32[4,1024]{1,0:T(4,128)S(1)}, u32[]{:S(2)}, u32[]{:S(2)}) collective-permute-start(f32[4,1024]{1,0:T(4,128)S(1)} %get-tuple-element.27.chosen0), channel_id=1, source_target_pairs={{0,96},{32,0},{64,32},{96,64},{1,97},{33,1},{65,33},{97,65},{2,98}... | collective-permute-start | bytes 49160 | tf_op jit(solution)/shard_map/ppermute | solution.py:299
  13.6 4.5 %shard_map.113 = bf16[256,1024]{1,0:T(8,128)(2,1)} custom-call(bf16[256,1024]{1,0:T(8,128)(2,1)S(1)} %copy-done.3, f32[4,1024]{1,0:T(4,128)S(1)} %get-tuple-element.27.chosen0, f32[4,1024]{1,0:T(4,128)S(1)} %collective-permute-done.chosen1, f32[4,1024]{1,0:T(4,128)S(1)} %collective-permute-done.1.chosen2, f32[4,1024]{1,0:T(4,128)S(1)} %collective-permute-done.2.chosen3, ...), custom_call_target="tpu_custom_call" | custom-call | flops 1000 | bytes 1000 | tf_op jit(solution)/shard_map/pallas_call | solution.py:302
  18.1 1.6 %collective-permute-start.3 = (bf16[256,1024]{1,0:T(8,128)(2,1)}, bf16[256,1024]{1,0:T(8,128)(2,1)S(1)}, u32[]{:S(2)}, u32[]{:S(2)}) collective-permute-start(bf16[256,1024]{1,0:T(8,128)(2,1)} %shard_map.113), channel_id=1, source_target_pairs={{0,8},{1,3},{2,10},{3,5},{4,12},{5,7},{6,14},{7,1},{8,16},{9,11},{... | collective-permute-start | bytes 1572872 | tf_op jit(solution)/shard_map/ppermute | solution.py:174
  19.8 2.1 %collective-permute-start.4 = (bf16[256,1024]{1,0:T(8,128)(2,1)}, bf16[256,1024]{1,0:T(8,128)(2,1)S(1)}, u32[]{:S(2)}, u32[]{:S(2)}) collective-permute-start(bf16[256,1024]{1,0:T(8,128)(2,1)} %shard_map.113), channel_id=1, source_target_pairs={{0,24},{1,7},{2,26},{3,1},{4,28},{5,3},{6,30},{7,5},{8,0},{9,15},{... | collective-permute-start | bytes 1572872 | tf_op jit(solution)/shard_map/ppermute | solution.py:174
  21.9 5.2 %shard_map.114 = f32[1,256,1024]{2,1,0:T(8,128)} custom-call(f32[1,256,1024]{2,1,0:T(8,128)S(1)} %copy-done, f32[1,256,1024]{2,1,0:T(8,128)S(1)} %copy-done.1, s32[2,4,8,1024]{3,2,1,0:T(8,128)S(1)} %get-tuple-element.28.where, f32[256,256]{1,0:T(8,128)S(1)} %copy-done.2), custom_call_target="tpu_custom_call" | custom-call | flops 1000 | bytes 1000 | tf_op jit(solution)/shard_map/pallas_call | solution.py:314
  27.1 1.9 %collective-permute-done.3 = bf16[256,1024]{1,0:T(8,128)(2,1)S(1)} collective-permute-done((bf16[256,1024]{1,0:T(8,128)(2,1)}, bf16[256,1024]{1,0:T(8,128)(2,1)S(1)}, u32[]{:S(2)}, u32[]{:S(2)}) %collective-permute-start.3) | collective-permute-done | bytes 524320 | tf_op jit(solution)/shard_map/ppermute | solution.py:174
  30.1 1.8 %collective-permute-start.8 = (bf16[128,1024]{1,0:T(8,128)(2,1)S(1)}, bf16[128,1024]{1,0:T(8,128)(2,1)S(1)}, u32[]{:S(2)}, u32[]{:S(2)}) collective-permute-start(bf16[128,1024]{1,0:T(8,128)(2,1)S(1)} %slice.7), channel_id=1, source_target_pairs={{0,24},{1,7},{2,26},{3,1},{4,28},{5,3},{6,30},{7,5},{8,0},{9,15},{... | collective-permute-start | bytes 786440 | tf_op jit(solution)/shard_map/ppermute | solution.py:174
  32.0 1.1 %collective-permute-start.5 = (bf16[512,1024]{1,0:T(8,128)(2,1)S(1)}, bf16[512,1024]{1,0:T(8,128)(2,1)S(1)}, u32[]{:S(2)}, u32[]{:S(2)}) collective-permute-start(bf16[512,1024]{1,0:T(8,128)(2,1)S(1)} %pad_maximum_fusion.refs_2_), channel_id=1, source_target_pairs={{0,2},{1,9},{2,4},{3,11},{4,6},{5,13},{6,0},{7,15},{8,10},{9,17},{... | collective-permute-start | bytes 3145736 | tf_op jit(solution)/shard_map/ppermute | solution.py:174
  33.0 1.8 %collective-permute-start.11 = (bf16[512,1024]{1,0:T(8,128)(2,1)S(1)}, bf16[512,1024]{1,0:T(8,128)(2,1)S(1)}, u32[]{:S(2)}, u32[]{:S(2)}) collective-permute-start(bf16[512,1024]{1,0:T(8,128)(2,1)S(1)} %pad_maximum_fusion.refs_2_), channel_id=1, source_target_pairs={{0,6},{1,25},{2,0},{3,27},{4,2},{5,29},{6,4},{7,31},{8,14},{9,1},{... | collective-permute-start | bytes 3145736 | tf_op jit(solution)/shard_map/ppermute | solution.py:174
  34.9 4.4 %shard_map.115 = (f32[1024,1024]{1,0:T(8,128)S(1)}, f32[1024,1024]{1,0:T(8,128)S(1)}, f32[8,128]{1,0:T(8,128)S(1)}) custom-call(s32[32]{0:T(128)S(1)} %select_add_fusion.ids, f32[8,128]{1,0:T(8,128)S(1)} %broadcast_in_dim.13._, bf16[1024,8192]{1,0:T(8,128)(2,1)} %refs_0_.9, bf16[1024,8192]{1,0:T(8,128)(2,1)} %collective-permute-done.9.refs_1_, ...), custom_call_target="tpu_custom_call" | custom-call | flops 1000 | bytes 1000 | tf_op jit(solution)/shard_map/pallas_call | solution.py:255
  39.4 1.5 %collective-permute-start.10 = (bf16[512,1024]{1,0:T(8,128)(2,1)S(1)}, bf16[512,1024]{1,0:T(8,128)(2,1)S(1)}, u32[]{:S(2)}, u32[]{:S(2)}) collective-permute-start(bf16[512,1024]{1,0:T(8,128)(2,1)S(1)} %constant_dynamic-update-slice_fusion.refs_2_), channel_id=1, source_target_pairs={{0,6},{1,25},{2,0},{3,27},{4,2},{5,29},{6,4},{7,31},{8,14},{9,1},{... | collective-permute-start | bytes 3145736 | tf_op jit(solution)/shard_map/ppermute | solution.py:174
  40.9 8.3 %collective-permute-done.5.refs_3_ = bf16[512,1024]{1,0:T(8,128)(2,1)S(1)} collective-permute-done((bf16[512,1024]{1,0:T(8,128)(2,1)S(1)}, bf16[512,1024]{1,0:T(8,128)(2,1)S(1)}, u32[]{:S(2)}, u32[]{:S(2)}) %collective-permute-start.5) | collective-permute-done | bytes 1048608 | tf_op jit(solution)/shard_map/ppermute | solution.py:174
  49.7 10.3 %shard_map.116 = (f32[1024,1024]{1,0:T(8,128)S(1)}, f32[1024,1024]{1,0:T(8,128)S(1)}, f32[8,128]{1,0:T(8,128)S(1)}) custom-call(s32[32]{0:T(128)S(1)} %select_add_fusion.ids, f32[8,128]{1,0:T(8,128)S(1)} %get-tuple-element.34._, bf16[1024,8192]{1,0:T(8,128)(2,1)} %refs_0_.9, ...), custom_call_target="tpu_custom_call", output_to_operand_aliasing={{0}: (7, {}), {1}: (8, {})} | custom-call | flops 1000 | bytes 1000 | tf_op jit(solution)/shard_map/pallas_call | solution.py:255
  60.9 2.6 %collective-permute-start.14 = (bf16[512,1024]{1,0:T(8,128)(2,1)S(1)}, bf16[512,1024]{1,0:T(8,128)(2,1)S(1)}, u32[]{:S(2)}, u32[]{:S(2)}) collective-permute-start(bf16[512,1024]{1,0:T(8,128)(2,1)S(1)} %collective-permute-done.10.refs_3_), channel_id=1, source_target_pairs={{0,6},{1,25},{2,0},{3,27},{4,2},{5,29},{6,4},{7,31},{8,14},{9,1},{... | collective-permute-start | bytes 3145736 | tf_op jit(solution)/shard_map/ppermute | solution.py:174
  63.5 7.5 %shard_map.117 = (f32[1024,1024]{1,0:T(8,128)S(1)}, bf16[1024,1024]{1,0:T(8,128)(2,1)S(1)}, f32[8,128]{1,0:T(8,128)S(1)}) custom-call(s32[32]{0:T(128)S(1)} %select_add_fusion.ids, f32[8,128]{1,0:T(8,128)S(1)} %get-tuple-element.38._, bf16[1024,8192]{1,0:T(8,128)(2,1)} %refs_0_.9, ...), custom_call_target="tpu_custom_call", output_to_operand_aliasing={{0}: (6, {})} | custom-call | flops 1000 | bytes 1000 | tf_op jit(solution)/shard_map/pallas_call | solution.py:255
  71.0 2.2 %collective-permute-start.16 = (bf16[1024,1024]{1,0:T(8,128)(2,1)S(1)}, bf16[1024,1024]{1,0:T(8,128)(2,1)S(1)}, u32[]{:S(2)}, u32[]{:S(2)}) collective-permute-start(bf16[1024,1024]{1,0:T(8,128)(2,1)S(1)} %get-tuple-element.48), channel_id=1, source_target_pairs={{0,1},{1,0},{2,3},{3,2},{4,5},{5,4},{6,7},{7,6},{8,9},{9,8},{10,11... | collective-permute-start | bytes 6291464 | tf_op jit(solution)/shard_map/ppermute | solution.py:178
  73.6 1.7 %collective-permute-done.14.refs_1_ = bf16[512,1024]{1,0:T(8,128)(2,1)S(1)} collective-permute-done((bf16[512,1024]{1,0:T(8,128)(2,1)S(1)}, bf16[512,1024]{1,0:T(8,128)(2,1)S(1)}, u32[]{:S(2)}, u32[]{:S(2)}) %collective-permute-start.14) | collective-permute-done | bytes 1048608 | tf_op jit(solution)/shard_map/ppermute | solution.py:174
  75.3 2.7 %collective-permute-start.15 = (bf16[512,1024]{1,0:T(8,128)(2,1)S(1)}, bf16[512,1024]{1,0:T(8,128)(2,1)S(1)}, u32[]{:S(2)}, u32[]{:S(2)}) collective-permute-start(bf16[512,1024]{1,0:T(8,128)(2,1)S(1)} %collective-permute-done.14.refs_1_), channel_id=1, source_target_pairs={{0,1},{1,0},{2,3},{3,2},{4,5},{5,4},{6,7},{7,6},{8,9},{9,8},{10,11... | collective-permute-start | bytes 3145736 | tf_op jit(solution)/shard_map/ppermute | solution.py:178
  78.5 5.0 %shard_map.118 = (f32[1024,1024]{1,0:T(8,128)S(1)}, f32[8,128]{1,0:T(8,128)S(1)}) custom-call(s32[32]{0:T(128)S(1)} %select_add_fusion.ids, f32[8,128]{1,0:T(8,128)S(1)} %get-tuple-element.43._, bf16[1024,8192]{1,0:T(8,128)(2,1)} %refs_0_.9, bf16[512,1024]{1,0:T(8,128)(2,1)S(1)} %collective-permute-done.6.refs_1_, ...), custom_call_target="tpu_custom_call", output_to_operand_aliasing={{0}: (5, {})} | custom-call | flops 1000 | bytes 1000 | tf_op jit(solution)/shard_map/pallas_call | solution.py:255
  83.5 6.1 %shard_map.119 = (bf16[1024,1024]{1,0:T(8,128)(2,1)}, f32[8,128]{1,0:T(8,128)}) custom-call(s32[32]{0:T(128)S(1)} %select_add_fusion.ids, f32[8,128]{1,0:T(8,128)S(1)} %get-tuple-element.46._, bf16[1024,8192]{1,0:T(8,128)(2,1)} %refs_0_.9, bf16[512,1024]{1,0:T(8,128)(2,1)S(1)} %collective-permute-done.14.refs_1_, ...), custom_call_target="tpu_custom_call" | custom-call | flops 1000 | bytes 1000 | tf_op jit(solution)/shard_map/pallas_call | solution.py:255
  (42 shorter events, 5.2 us)
Async XLA Ops:
  0.6 13.0 %copy-start.2 = (f32[256,256]{1,0:T(8,128)S(1)}, f32[256,256]{1,0:T(8,128)}, u32[]{:S(2)}) copy-start(f32[256,256]{1,0:T(8,128)} %constant.31.clone.basis) | copy-start | bytes 786436
  0.6 21.2 %copy-start = (f32[1,256,1024]{2,1,0:T(8,128)S(1)}, f32[1,256,1024]{2,1,0:T(8,128)}, u32[]{:S(2)}) copy-start(f32[1,256,1024]{2,1,0:T(8,128)} %momentum.3) | copy-start | bytes 3145732
  0.7 21.2 %copy-start.1 = (f32[1,256,1024]{2,1,0:T(8,128)S(1)}, f32[1,256,1024]{2,1,0:T(8,128)}, u32[]{:S(2)}) copy-start(f32[1,256,1024]{2,1,0:T(8,128)} %grad.3) | copy-start | bytes 3145732
  0.7 34.2 %collective-permute-start.9 = (bf16[1024,8192]{1,0:T(8,128)(2,1)}, bf16[1024,8192]{1,0:T(8,128)(2,1)}, u32[]{:S(2)}, u32[]{:S(2)}) collective-permute-start(bf16[1024,8192]{1,0:T(8,128)(2,1)} %refs_0_.9), channel_id=1, source_target_pairs={{0,1},{1,0},{2,3},{3,2},{4,5},{5,4},{6,7},{7,6},{8,9},{9,8},{10,11... | collective-permute-start | bytes 50331656 | tf_op jit(solution)/shard_map/ppermute | solution.py:178
  2.2 24.9 %copy-start.5 = (s32[32]{0:T(128)S(1)}, s32[32]{0:T(128)}, u32[]{:S(2)}) copy-start(s32[32]{0:T(128)} %constant.32.clone) | copy-start | bytes 388
  2.2 24.9 %copy-start.6 = (s32[32]{0:T(128)S(1)}, s32[32]{0:T(128)}, u32[]{:S(2)}) copy-start(s32[32]{0:T(128)} %constant.33.clone) | copy-start | bytes 388
  2.2 24.9 %copy-start.7 = (pred[32]{0:T(512)(128)(4,1)S(1)}, pred[32]{0:T(512)(128)(4,1)}, u32[]{:S(2)}) copy-start(pred[32]{0:T(512)(128)(4,1)} %constant.34.clone) | copy-start | bytes 100
  6.9 5.1 %collective-permute-start = (f32[4,1024]{1,0:T(4,128)S(1)}, f32[4,1024]{1,0:T(4,128)S(1)}, u32[]{:S(2)}, u32[]{:S(2)}) collective-permute-start(f32[4,1024]{1,0:T(4,128)S(1)} %get-tuple-element.27.chosen0), channel_id=1, source_target_pairs={{0,32},{32,64},{64,96},{96,0},{1,33},{33,65},{65,97},{97,1},{2,34}... | collective-permute-start | bytes 49160 | tf_op jit(solution)/shard_map/ppermute | solution.py:299
  8.4 4.2 %collective-permute-start.1 = (f32[4,1024]{1,0:T(4,128)S(1)}, f32[4,1024]{1,0:T(4,128)S(1)}, u32[]{:S(2)}, u32[]{:S(2)}) collective-permute-start(f32[4,1024]{1,0:T(4,128)S(1)} %get-tuple-element.27.chosen0), channel_id=1, source_target_pairs={{0,64},{32,96},{64,0},{96,32},{1,65},{33,97},{65,1},{97,33},{2,66}... | collective-permute-start | bytes 49160 | tf_op jit(solution)/shard_map/ppermute | solution.py:299
  10.8 2.8 %collective-permute-start.2 = (f32[4,1024]{1,0:T(4,128)S(1)}, f32[4,1024]{1,0:T(4,128)S(1)}, u32[]{:S(2)}, u32[]{:S(2)}) collective-permute-start(f32[4,1024]{1,0:T(4,128)S(1)} %get-tuple-element.27.chosen0), channel_id=1, source_target_pairs={{0,96},{32,0},{64,32},{96,64},{1,97},{33,1},{65,33},{97,65},{2,98}... | collective-permute-start | bytes 49160 | tf_op jit(solution)/shard_map/ppermute | solution.py:299
  18.1 13.8 %copy-start.4 = (bf16[256,1024]{1,0:T(8,128)(2,1)S(1)}, bf16[256,1024]{1,0:T(8,128)(2,1)}, u32[]{:S(2)}) copy-start(bf16[256,1024]{1,0:T(8,128)(2,1)} %shard_map.113) | copy-start | bytes 1572868
  18.1 10.9 %collective-permute-start.3 = (bf16[256,1024]{1,0:T(8,128)(2,1)}, bf16[256,1024]{1,0:T(8,128)(2,1)S(1)}, u32[]{:S(2)}, u32[]{:S(2)}) collective-permute-start(bf16[256,1024]{1,0:T(8,128)(2,1)} %shard_map.113), channel_id=1, source_target_pairs={{0,8},{1,3},{2,10},{3,5},{4,12},{5,7},{6,14},{7,1},{8,16},{9,11},{... | collective-permute-start | bytes 1572872 | tf_op jit(solution)/shard_map/ppermute | solution.py:174
  19.8 9.3 %collective-permute-start.4 = (bf16[256,1024]{1,0:T(8,128)(2,1)}, bf16[256,1024]{1,0:T(8,128)(2,1)S(1)}, u32[]{:S(2)}, u32[]{:S(2)}) collective-permute-start(bf16[256,1024]{1,0:T(8,128)(2,1)} %shard_map.113), channel_id=1, source_target_pairs={{0,24},{1,7},{2,26},{3,1},{4,28},{5,3},{6,30},{7,5},{8,0},{9,15},{... | collective-permute-start | bytes 1572872 | tf_op jit(solution)/shard_map/ppermute | solution.py:174
  29.0 10.3 %collective-permute-start.7 = (bf16[128,1024]{1,0:T(8,128)(2,1)S(1)}, bf16[128,1024]{1,0:T(8,128)(2,1)S(1)}, u32[]{:S(2)}, u32[]{:S(2)}) collective-permute-start(bf16[128,1024]{1,0:T(8,128)(2,1)S(1)} %slice.6), channel_id=1, source_target_pairs={{0,8},{1,3},{2,10},{3,5},{4,12},{5,7},{6,14},{7,1},{8,16},{9,11},{... | collective-permute-start | bytes 786440 | tf_op jit(solution)/shard_map/ppermute | solution.py:174
  30.1 9.3 %collective-permute-start.8 = (bf16[128,1024]{1,0:T(8,128)(2,1)S(1)}, bf16[128,1024]{1,0:T(8,128)(2,1)S(1)}, u32[]{:S(2)}, u32[]{:S(2)}) collective-permute-start(bf16[128,1024]{1,0:T(8,128)(2,1)S(1)} %slice.7), channel_id=1, source_target_pairs={{0,24},{1,7},{2,26},{3,1},{4,28},{5,3},{6,30},{7,5},{8,0},{9,15},{... | collective-permute-start | bytes 786440 | tf_op jit(solution)/shard_map/ppermute | solution.py:174
  32.0 17.3 %collective-permute-start.5 = (bf16[512,1024]{1,0:T(8,128)(2,1)S(1)}, bf16[512,1024]{1,0:T(8,128)(2,1)S(1)}, u32[]{:S(2)}, u32[]{:S(2)}) collective-permute-start(bf16[512,1024]{1,0:T(8,128)(2,1)S(1)} %pad_maximum_fusion.refs_2_), channel_id=1, source_target_pairs={{0,2},{1,9},{2,4},{3,11},{4,6},{5,13},{6,0},{7,15},{8,10},{9,17},{... | collective-permute-start | bytes 3145736 | tf_op jit(solution)/shard_map/ppermute | solution.py:174
  33.0 16.6 %collective-permute-start.11 = (bf16[512,1024]{1,0:T(8,128)(2,1)S(1)}, bf16[512,1024]{1,0:T(8,128)(2,1)S(1)}, u32[]{:S(2)}, u32[]{:S(2)}) collective-permute-start(bf16[512,1024]{1,0:T(8,128)(2,1)S(1)} %pad_maximum_fusion.refs_2_), channel_id=1, source_target_pairs={{0,6},{1,25},{2,0},{3,27},{4,2},{5,29},{6,4},{7,31},{8,14},{9,1},{... | collective-permute-start | bytes 3145736 | tf_op jit(solution)/shard_map/ppermute | solution.py:174
  39.4 21.5 %collective-permute-start.10 = (bf16[512,1024]{1,0:T(8,128)(2,1)S(1)}, bf16[512,1024]{1,0:T(8,128)(2,1)S(1)}, u32[]{:S(2)}, u32[]{:S(2)}) collective-permute-start(bf16[512,1024]{1,0:T(8,128)(2,1)S(1)} %constant_dynamic-update-slice_fusion.refs_2_), channel_id=1, source_target_pairs={{0,6},{1,25},{2,0},{3,27},{4,2},{5,29},{6,4},{7,31},{8,14},{9,1},{... | collective-permute-start | bytes 3145736 | tf_op jit(solution)/shard_map/ppermute | solution.py:174
  40.8 22.7 %collective-permute-start.12 = (bf16[512,1024]{1,0:T(8,128)(2,1)S(1)}, bf16[512,1024]{1,0:T(8,128)(2,1)S(1)}, u32[]{:S(2)}, u32[]{:S(2)}) collective-permute-start(bf16[512,1024]{1,0:T(8,128)(2,1)S(1)} %constant_dynamic-update-slice_fusion.refs_2_), channel_id=1, source_target_pairs={{0,2},{1,9},{2,4},{3,11},{4,6},{5,13},{6,0},{7,15},{8,10},{9,17},{... | collective-permute-start | bytes 3145736 | tf_op jit(solution)/shard_map/ppermute | solution.py:174
  49.2 24.0 %collective-permute-start.6 = (bf16[512,1024]{1,0:T(8,128)(2,1)S(1)}, bf16[512,1024]{1,0:T(8,128)(2,1)S(1)}, u32[]{:S(2)}, u32[]{:S(2)}) collective-permute-start(bf16[512,1024]{1,0:T(8,128)(2,1)S(1)} %collective-permute-done.5.refs_3_), channel_id=1, source_target_pairs={{0,2},{1,9},{2,4},{3,11},{4,6},{5,13},{6,0},{7,15},{8,10},{9,17},{... | collective-permute-start | bytes 3145736 | tf_op jit(solution)/shard_map/ppermute | solution.py:174
  60.9 14.3 %collective-permute-start.14 = (bf16[512,1024]{1,0:T(8,128)(2,1)S(1)}, bf16[512,1024]{1,0:T(8,128)(2,1)S(1)}, u32[]{:S(2)}, u32[]{:S(2)}) collective-permute-start(bf16[512,1024]{1,0:T(8,128)(2,1)S(1)} %collective-permute-done.10.refs_3_), channel_id=1, source_target_pairs={{0,6},{1,25},{2,0},{3,27},{4,2},{5,29},{6,4},{7,31},{8,14},{9,1},{... | collective-permute-start | bytes 3145736 | tf_op jit(solution)/shard_map/ppermute | solution.py:174
  71.0 12.5 %collective-permute-start.16 = (bf16[1024,1024]{1,0:T(8,128)(2,1)S(1)}, bf16[1024,1024]{1,0:T(8,128)(2,1)S(1)}, u32[]{:S(2)}, u32[]{:S(2)}) collective-permute-start(bf16[1024,1024]{1,0:T(8,128)(2,1)S(1)} %get-tuple-element.48), channel_id=1, source_target_pairs={{0,1},{1,0},{2,3},{3,2},{4,5},{5,4},{6,7},{7,6},{8,9},{9,8},{10,11... | collective-permute-start | bytes 6291464 | tf_op jit(solution)/shard_map/ppermute | solution.py:178
  73.2 5.3 %collective-permute-start.13 = (bf16[512,1024]{1,0:T(8,128)(2,1)S(1)}, bf16[512,1024]{1,0:T(8,128)(2,1)S(1)}, u32[]{:S(2)}, u32[]{:S(2)}) collective-permute-start(bf16[512,1024]{1,0:T(8,128)(2,1)S(1)} %collective-permute-done.6.refs_1_), channel_id=1, source_target_pairs={{0,1},{1,0},{2,3},{3,2},{4,5},{5,4},{6,7},{7,6},{8,9},{9,8},{10,11... | collective-permute-start | bytes 3145736 | tf_op jit(solution)/shard_map/ppermute | solution.py:178
  75.3 8.3 %collective-permute-start.15 = (bf16[512,1024]{1,0:T(8,128)(2,1)S(1)}, bf16[512,1024]{1,0:T(8,128)(2,1)S(1)}, u32[]{:S(2)}, u32[]{:S(2)}) collective-permute-start(bf16[512,1024]{1,0:T(8,128)(2,1)S(1)} %collective-permute-done.14.refs_1_), channel_id=1, source_target_pairs={{0,1},{1,0},{2,3},{3,2},{4,5},{5,4},{6,7},{7,6},{8,9},{9,8},{10,11... | collective-permute-start | bytes 3145736 | tf_op jit(solution)/shard_map/ppermute | solution.py:178
  (1 other events, 12.9 us)

commit v4 on v3

v4 whole, which is shorter than its diff:
```python
import functools

import jax
import jax.numpy as jnp
import numpy as np
from jax import lax
from jax.experimental import pallas as pl
from jax.experimental.pallas import tpu as pltpu
from jax.sharding import Mesh, PartitionSpec as P

GROUP = 64
KEEP = 64
REPS = 4
SIDE = 4
PAIR = 2 * GROUP
PLANE = ("y", "z", "core")

beta_decay = 0.999
step_rate = 0.05

HIGHEST = lax.Precision.HIGHEST
NT = (((1,), (1,)), ((), ()))
TN = (((0,), (0,)), ((), ()))
VM = pl.BlockSpec(memory_space=pltpu.VMEM)
ANY = pl.BlockSpec(memory_space=pl.ANY)
PARAMS = pltpu.CompilerParams(vmem_limit_bytes=32 * 2**20)
ALONE = pltpu.CompilerParams(vmem_limit_bytes=60 * 2**20)
SMALL = pl.CostEstimate(flops=1000, bytes_accessed=1000, transcendentals=0)


def dct_blocks(size):
    freq = np.arange(GROUP, dtype=np.float64)[:, None]
    place = np.arange(GROUP, dtype=np.float64)[None, :]
    scale = np.where(freq == 0, np.sqrt(1.0 / GROUP), np.sqrt(2.0 / GROUP))
    basis = scale * np.cos(np.pi * (2.0 * place + 1.0) * freq / (2.0 * GROUP))
    return np.kron(np.eye(size // GROUP), basis).astype(np.float32)


def halves(value):
    high = value.astype(jnp.bfloat16)
    return high, (value - high.astype(jnp.float32)).astype(jnp.bfloat16)


def dot3(left, right, dims):
    total = None
    for a, b in ((0, 0), (0, 1), (1, 0)):
        part = lax.dot_general(left[a], right[b], dims, preferred_element_type=jnp.float32)
        total = part if total is None else total + part
    return total


def plain(contract):
    return (contract, ((), ()))


def is_row(target, rows):
    return lax.broadcasted_iota(jnp.int32, (rows, target.shape[1]), 0) == target


def one_hot(target, rows):
    return jnp.where(is_row(target, rows), 1.0, 0.0).astype(jnp.bfloat16)


def picker(blocks, lanes):
    first = ((lax.axis_index("y") * SIDE + lax.axis_index("z")) * 2 + lax.axis_index("core")) * blocks
    sub = lax.broadcasted_iota(jnp.int32, (16, 2 * lanes), 0)
    lane = lax.broadcasted_iota(jnp.int32, (16, 2 * lanes), 1)
    mine = jnp.where(sub < 8, first + sub, lanes + first + sub - 8)
    return jnp.where((lane == mine) & (jnp.bitwise_and(sub, 7) < blocks), 1.0, 0.0).astype(jnp.bfloat16)


def place_of(flat, pick, where, r):
    cols, lanes = flat.shape[0] * flat.shape[1], flat.shape[2]
    flat = flat.reshape(cols, lanes)
    row = jnp.right_shift(flat, 6).astype(jnp.float32).astype(jnp.bfloat16)
    col = jnp.bitwise_and(flat, GROUP - 1).astype(jnp.float32).astype(jnp.bfloat16)
    both = lax.dot_general(pick, jnp.concatenate([row, col], axis=1), NT, preferred_element_type=jnp.float32)
    both = both.astype(jnp.int32)
    where[0, r] = both[:8]
    where[1, r] = both[8:] + jnp.bitwise_and(lax.broadcasted_iota(jnp.int32, (8, cols), 1), GROUP)


def coeff_kernel(momentum, grad, selection, basis, chosen, where, mom, gra, sel, dct, sems):
    blocks = mom.shape[0] // GROUP
    copies = [
        pltpu.make_async_copy(selection.at[lax.axis_index("x")], sel, sems.at[0]),
        pltpu.make_async_copy(momentum.at[0], mom, sems.at[1]),
        pltpu.make_async_copy(grad.at[0], gra, sems.at[2]),
        pltpu.make_async_copy(basis, dct, sems.at[3]),
    ]
    for copy in copies:
        copy.start()
    pick = picker(blocks, sel.shape[2])
    copies[0].wait()
    place_of(sel[...], pick, where, 0)
    for copy in copies[1:]:
        copy.wait()
    base = halves(dct[...])
    moment = halves(beta_decay * mom[...] + gra[...])
    inner = halves(dot3(base, moment, plain(((1,), (0,)))))
    width = base[0].shape[0]
    for c in range(0, mom.shape[1], width):
        coeff = dot3([part[:, c : c + width] for part in inner], base, NT)
        high, low = halves(coeff)
        for p in range(c, c + width, PAIR):
            span = slice(p - c, p - c + PAIR)
            for a in range(blocks):
                rows = slice(a * GROUP, (a + 1) * GROUP)
                left = jnp.concatenate([high[rows, span], low[rows, span]], axis=1)
                right = one_hot(where[1, 0, a : a + 1, p : p + PAIR], PAIR)
                found = jnp.dot(left, jnp.concatenate([right, right], axis=0), preferred_element_type=jnp.float32)
                kept = jnp.where(is_row(where[0, 0, a : a + 1, p : p + PAIR], GROUP), found, 0.0)
                chosen[a : a + 1, p : p + PAIR] = jnp.sum(kept, axis=0, keepdims=True)


def others_kernel(blocks, selection, where, sel, sems):
    copies = []
    for k in range(REPS - 1):
        r = lax.rem(lax.axis_index("x") + REPS - 1 - k, REPS)
        copies.append(pltpu.make_async_copy(selection.at[r], sel.at[k], sems.at[k]))
        copies[-1].start()
    pick = picker(blocks, sel.shape[3])
    for k in range(REPS - 1):
        copies[k].wait()
        place_of(sel[k], pick, where, k)


def weight_kernel(weight, chosen0, chosen1, chosen2, chosen3, where, others, basis, new_weight, dense):
    rows, cols = weight.shape
    base = halves(basis[...])
    values = []
    for k, chosen in enumerate((chosen0, chosen1, chosen2, chosen3)):
        high, low = halves(chosen[...])
        values.append((others if k else where, max(k - 1, 0), high.astype(jnp.float32), low.astype(jnp.float32)))
    for p in range(0, cols, PAIR):
        for a in range(rows // GROUP):
            lefts, highs, lows = [], [], []
            for places, r, high, low in values:
                lefts.append(one_hot(places[0, r, a : a + 1, p : p + PAIR], GROUP))
                hit = is_row(places[1, r, a : a + 1, p : p + PAIR], PAIR)
                highs.append(jnp.where(hit, high[a : a + 1, p : p + PAIR], 0.0).astype(jnp.bfloat16))
                lows.append(jnp.where(hit, low[a : a + 1, p : p + PAIR], 0.0).astype(jnp.bfloat16))
            right = jnp.concatenate([jnp.concatenate(highs, axis=1), jnp.concatenate(lows, axis=1)], axis=0)
            both = lax.dot_general(jnp.concatenate(lefts, axis=1), right, NT, preferred_element_type=jnp.float32)
            dense[a * GROUP : (a + 1) * GROUP, p : p + PAIR] = both[:, :PAIR] + both[:, PAIR:]
    inner = halves(dot3(base, halves(dense[...]), TN))
    width = rows
    for c in range(0, cols, width):
        update = dot3([part[:, c : c + width] for part in inner], base, plain(((1,), (0,))))
        old = weight[:, c : c + width].astype(jnp.float32)
        new_weight[:, c : c + width] = (old - step_rate * update).astype(jnp.bfloat16)


def momentum_kernel(momentum, grad, where, basis, new_momentum, dense):
    rows, cols = dense.shape
    base = basis[...]
    moment = beta_decay * momentum[0] + grad[0]
    inner = jnp.dot(base, moment, precision=HIGHEST, preferred_element_type=jnp.float32)
    width = rows
    for c in range(0, cols, width):
        coeff = lax.dot_general(inner[:, c : c + width], base, NT, precision=HIGHEST, preferred_element_type=jnp.float32)
        for p in range(c, c + width, PAIR):
            for a in range(rows // GROUP):
                left = one_hot(where[0, 0, a : a + 1, p : p + PAIR], GROUP)
                right = one_hot(where[1, 0, a : a + 1, p : p + PAIR], PAIR)
                kept = lax.dot_general(left, right, NT, preferred_element_type=jnp.float32)
                span = slice(a * GROUP, (a + 1) * GROUP)
                dense[span, p : p + PAIR] = jnp.where(kept > 0.5, coeff[span, p - c : p - c + PAIR], 0.0)
    inner = lax.dot_general(base, dense[...], TN, precision=HIGHEST, preferred_element_type=jnp.float32)
    for c in range(0, cols, width):
        own_part = jnp.dot(inner[:, c : c + width], base, precision=HIGHEST, preferred_element_type=jnp.float32)
        moment = beta_decay * momentum[0, :, c : c + width] + grad[0, :, c : c + width]
        new_momentum[0, :, c : c + width] = moment - own_part


def ring(axis, step):
    pairs = []
    for y in range(SIDE):
        for z in range(SIDE):
            for c in range(2):
                if (c == 0) == (axis == "u"):
                    to = ((y + step) % SIDE, z)
                else:
                    to = (y, (z + step) % SIDE)
                pairs.append(((y * SIDE + z) * 2 + c, (to[0] * SIDE + to[1]) * 2 + c))
    return pairs


def send(value, axis, step):
    return lax.ppermute(value, PLANE, ring(axis, step))


def sibling(value):
    return lax.ppermute(value, "core", [(0, 1), (1, 0)])


def shard_places():
    y, z, c = lax.axis_index("y"), lax.axis_index("z"), lax.axis_index("core")
    k = np.arange(2 * SIDE * SIDE)
    u, v = jnp.asarray(k // SIDE % SIDE, jnp.int32), jnp.asarray(k % SIDE, jnp.int32)
    core = jnp.where(jnp.asarray(k < SIDE * SIDE), c, 1 - c)
    even = jnp.bitwise_and(y + u, 3) * SIDE + jnp.bitwise_and(z + v, 3)
    odd = jnp.bitwise_and(y + v, 3) * SIDE + jnp.bitwise_and(z + u, 3)
    return 2 * jnp.where(core == 0, even, odd) + core


def at(*offsets, other=False):
    return [(u % SIDE) * SIDE + v % SIDE + (SIDE * SIDE if other else 0) for u, v in offsets]


def multiply(places, jobs, shards, pieces, after=None, ahead=(), last=False, flops=1000):
    depth, tile = 256, 256
    rows, cols, count = jobs[0][0].shape[0], pieces[0].shape[1], len(shards)
    whole = [tok.shape[1] > count * depth for tok, _, _ in jobs]
    sources = [tok for (tok, _, _), w in zip(jobs, whole) if w] + [tok for tok, _ in ahead]
    laid = [tok for (tok, _, _), w in zip(jobs, whole) if not w]
    adds = [x for _, some, _ in jobs for x in some]
    n_jobs, n_whole = len(jobs), sum(whole)
    wide = max([len(some) for _, some in ahead], default=1)
    after = jnp.zeros((8, 128), jnp.float32) if after is None else after
    aliases, at = {}, 2 + len(sources) + len(pieces) + len(laid)
    for n, (_, some, dtype) in enumerate(jobs):
        if some and some[0].dtype == dtype:
            aliases[at] = n
        at += len(some)

    def kernel(ids, _, *refs):
        refs = list(refs)
        take = lambda n: [refs.pop(0) for _ in range(n)]
        srcs, ws, lefts, adds = take(len(sources)), take(len(pieces)), take(len(laid)), take(len(aliased))
        outs, nexts, (ran, *scratch) = take(n_jobs), take(len(ahead)), refs
        sems, next_sems, *left = scratch
        joined, loads, at = [], [], 0
        if len(ws) > 1:
            joined, piece_sems = [left.pop()], left.pop()
            for k, w in enumerate(ws):
                loads.append(pltpu.make_async_copy(w, joined[0].at[pl.ds(at, w.shape[0])], piece_sems.at[k]))
                loads[-1].start()
                at += w.shape[0]
        held, stores = outs, []
        if last:
            held, out_sems = [left.pop(0)], left.pop(0)
        ran[...] = jnp.zeros_like(ran)
        def columns(src, places, dst, sem):
            return [
                pltpu.make_async_copy(
                    src.at[:, pl.ds(pl.multiple_of(ids[place] * depth, depth), depth)],
                    dst.at[:, pl.ds(k * depth, depth)],
                    sem.at[k],
                )
                for k, place in enumerate(places)
            ]

        copies = {n: columns(srcs[n], shards, left[0].at[n], sems.at[n]) for n in range(n_whole)}
        later = [columns(srcs[n_whole + m], some, nexts[m], next_sems.at[m]) for m, (_, some) in enumerate(ahead)]
        if n_whole:
            for copy in copies[0]:
                copy.start()
        else:
            for copy in sum(later, []):
                copy.start()
        for load in loads:
            load.wait()
        first = 0
        for n, (_, some, _) in enumerate(jobs):
            mine = adds[first : first + len(some)]
            first += len(some)
            if whole[n]:
                for copy in copies[n]:
                    copy.wait()
                for copy in copies[n + 1] if n + 1 < n_whole else sum(later, []):
                    copy.start()
                block = left[0].at[n]
            else:
                block = lefts[n]
            for i in range(0, rows, tile):
                span = slice(i, i + tile)
                right = ws[0] if len(ws) == 1 else joined[0]
                result = jnp.dot(block[span, :], right[...], preferred_element_type=jnp.float32)
                for add in mine:
                    result = result + add[span, :].astype(jnp.float32)
                held[n][span, :] = result.astype(outs[n].dtype)
                if last:
                    stores.append(pltpu.make_async_copy(held[n].at[span], outs[n].at[span], out_sems.at[n, i // tile]))
                    stores[-1].start()
        for copy in sum(later, []) + stores:
            copy.wait()

    def result(dtype):
        shape = (rows, cols)
        return pltpu.VMEM(shape, dtype) if dtype == jnp.float32 else jax.ShapeDtypeStruct(shape, dtype)

    aliased = adds
    out_shape = [result(dtype) for _, _, dtype in jobs]
    out_shape += [pltpu.VMEM((rows, len(some) * depth), jnp.bfloat16) for _, some in ahead]
    out_shape += [jax.ShapeDtypeStruct((8, 128), jnp.float32)]
    scratch = [
        pltpu.SemaphoreType.DMA((max(n_whole, 1), count)),
        pltpu.SemaphoreType.DMA((max(len(ahead), 1), wide)),
    ]
    if last:
        scratch += [pltpu.VMEM((rows, cols), jobs[0][2]), pltpu.SemaphoreType.DMA((1, rows // tile))]
    if n_whole:
        scratch.append(pltpu.VMEM((n_whole, rows, count * depth), jnp.bfloat16))
    if len(pieces) > 1:
        scratch += [pltpu.SemaphoreType.DMA((len(pieces),)), pltpu.VMEM((count * depth, cols), jnp.bfloat16)]
    return pl.pallas_call(
        kernel,
        in_specs=[pl.BlockSpec(memory_space=pltpu.SMEM)]
        + [ANY] * (1 + len(sources))
        + [VM] * (len(pieces) + len(laid) + len(adds)),
        out_specs=[ANY if last else VM] * n_jobs + [VM] * (len(out_shape) - n_jobs),
        out_shape=out_shape,
        scratch_shapes=scratch,
        compiler_params=pltpu.CompilerParams(vmem_limit_bytes=16 * 2**20),
        cost_estimate=pl.CostEstimate(flops=flops, bytes_accessed=1000, transcendentals=0),
        input_output_aliases=aliases,
    )(places, after, *[in_hbm(t) for t in sources], *pieces, *laid, *adds)


def in_hbm(value):
    return pltpu.with_memory_space_constraint(value, pltpu.HBM)


def on_device(tokens, weight, momentum, grad, selection):
    rows, cols = weight.shape
    blocks = rows // GROUP
    basis = jnp.asarray(dct_blocks(rows))
    lanes = selection.transpose(0, 2, 3, 1)
    chosen, where = pl.pallas_call(
        coeff_kernel,
        out_shape=(
            jax.ShapeDtypeStruct((blocks, cols), jnp.float32),
            jax.ShapeDtypeStruct((2, 1, 8, cols), jnp.int32),
        ),
        in_specs=[ANY] * 4,
        out_specs=(VM, VM),
        scratch_shapes=[
            pltpu.VMEM((rows, cols), jnp.float32),
            pltpu.VMEM((rows, cols), jnp.float32),
            pltpu.VMEM(lanes.shape[1:], jnp.int32),
            pltpu.VMEM(basis.shape, jnp.float32),
            pltpu.SemaphoreType.DMA((4,)),
        ],
        compiler_params=PARAMS,
        cost_estimate=SMALL,
    )(in_hbm(momentum), in_hbm(grad), in_hbm(lanes), in_hbm(basis))
    along_x = lambda step: lax.ppermute(chosen, "x", [(i, (i + step) % REPS) for i in range(REPS)])
    others = [along_x(k) for k in range(1, REPS)]
    elsewhere = pl.pallas_call(
        functools.partial(others_kernel, blocks),
        out_shape=jax.ShapeDtypeStruct((2, REPS - 1, 8, cols), jnp.int32),
        in_specs=[ANY],
        out_specs=VM,
        scratch_shapes=[pltpu.VMEM((REPS - 1,) + lanes.shape[1:], jnp.int32), pltpu.SemaphoreType.DMA((REPS - 1,))],
        compiler_params=PARAMS,
        cost_estimate=SMALL,
    )(in_hbm(lanes))
    tokens_too = sibling(tokens)
    shard = pl.pallas_call(
        weight_kernel,
        out_shape=jax.ShapeDtypeStruct((rows, cols), jnp.bfloat16),
        in_specs=[VM] * 8,
        out_specs=VM,
        scratch_shapes=[pltpu.VMEM((rows, cols), jnp.float32)],
        compiler_params=PARAMS,
        cost_estimate=SMALL,
    )(weight, chosen, *others, where, elsewhere, basis)

    places = shard_places()
    am, ap = send(shard, "u", 1), send(shard, "u", -1)
    new_momentum = pl.pallas_call(
        momentum_kernel,
        out_shape=jax.ShapeDtypeStruct(momentum.shape, jnp.float32),
        in_specs=[VM] * 4,
        out_specs=VM,
        scratch_shapes=[pltpu.VMEM((rows, cols), jnp.float32)],
        compiler_params=PARAMS,
        cost_estimate=SMALL,
    )(momentum, grad, where, basis)
    am, ap, new_momentum = lax.optimization_barrier((am, ap, new_momentum))
    top, bottom = send(am[: rows // 2], "u", 1), send(ap[rows // 2 :], "u", -1)
    s1 = jnp.concatenate([shard, am], axis=0)
    r1p, r1m = send(s1, "v", 1), send(s1, "v", -1)
    f32, bf16 = jnp.float32, jnp.bfloat16
    second = at((1, 0), (2, 0), (0, -1), (-1, -1), (0, 1), (-1, 1))
    third = at((1, -1), (2, -1), (1, 1), (2, 1))
    near, far = [(0, 2), (-1, 2)], [(1, 2), (2, 2)]
    fourth, fifth, sixth = at(*near), at(*near, other=True) + at(*far), at(*far, other=True)
    mine, theirs, *laid, ran = multiply(
        places,
        [(tokens, (), f32), (tokens_too, (), f32)],
        at((0, 0), (-1, 0)),
        [s1],
        ahead=[(tokens, second), (tokens_too, second)],
        flops=10**10,
    )
    top, bottom, ran = lax.optimization_barrier((top, bottom, ran))
    s2 = jnp.concatenate([ap, top, bottom], axis=0)
    r2p, r2m = send(s2, "v", 1), send(s2, "v", -1)
    f1 = send(r1p, "v", 1)
    mine, theirs, *laid, ran = multiply(
        places,
        [(laid[0], (mine,), f32), (laid[1], (theirs,), f32)],
        second,
        [s2, r1p, r1m],
        ran,
        ahead=[(tokens, third), (tokens_too, third)],
    )
    r2m, ran = lax.optimization_barrier((r2m, ran))
    f2 = send(r2m, "v", -1)
    mine, theirs, *laid, ran = multiply(
        places,
        [(laid[0], (mine,), f32), (laid[1], (theirs,), bf16)],
        third,
        [r2p, r2m],
        ran,
        ahead=[(tokens, some) for some in (fourth, fifth, sixth)],
    )
    theirs = sibling(theirs)
    f1, ran = lax.optimization_barrier((f1, ran))
    g1 = sibling(f1)
    mine, ran = multiply(places, [(laid[0], (mine,), f32)], fourth, [f1], ran)
    f2, ran = lax.optimization_barrier((f2, ran))
    g2 = sibling(f2)
    mine, ran = multiply(places, [(laid[1], (mine,), f32)], fifth, [g1, f2], ran)
    keys, _ = multiply(places, [(laid[2], (mine, theirs), bf16)], sixth, [g2], ran)
    return keys, shard, new_momentum


def solution(mesh):
    chips = Mesh(mesh.devices.reshape(REPS, SIDE, SIDE, 2), ("x",) + PLANE)
    return jax.shard_map(
        on_device,
        mesh=chips,
        in_specs=(
            P(("x",) + PLANE, None),
            P(PLANE, None),
            P("x", PLANE, None),
            P("x", PLANE, None),
            P(),
        ),
        out_specs=(P(("x",) + PLANE, None), P(PLANE, None), P("x", PLANE, None)),
        check_vma=False,
    )
```

time: 90.1 us -> 84.3 us (0.936)
  waiting for transfers between devices: 15.4 us -> 8.89 us
  starting transfers between devices: 25.5 us -> 28.5 us
  Pallas kernels: 47.7 us -> 45.4 us
    ppermute x10, waiting for transfers between devices: 13.2 us -> 8.87 us  [send(): return lax.ppermute(value, PLANE, ring(axis, step))]
    pallas_call x5 -> x6, Pallas kernels: 33.2 us -> 29.5 us  [multiply(): pl.pallas_call(kernel, in_specs=[pl.BlockSpec(memory_space=pltpu.SMEM)] +...]
    ppermute x4, starting transfers between devices: 6.76 us -> 9.59 us  [sibling(): return lax.ppermute(value, 'core', [(0, 1), (1, 0)])]
    pallas_call x0 -> x1, Pallas kernels: none -> 1.85 us  [on_device(): pl.pallas_call(functools.partial(others_kernel, blocks), out_shape=jax.Sh...]
    ppermute x3, waiting for transfers between devices: 1.61 us -> 0.01 us  [on_device(): lax.ppermute(chosen, 'x', [(i, (i + step) % REPS) for i in range(REPS)])]
  transfers between devices with their start and end apart: 17 -> 17, of which waited for: 8 -> 4; matrix products, arithmetic and copies ran while one was open for 0% -> 0% of each run, Pallas kernels for 46% -> 50%
where the time goes in v4:
time: 84.3 us; the launch traced here: 84.1 us
  Pallas kernels  45.4 us (54%)
  starting transfers between devices  28.5 us (34%)
  waiting for transfers between devices  8.89 us (11%)
  between operations  1.07 us (1%)
    pallas_call x6, Pallas kernels, multiply(): pl.pallas_call(kernel, in_specs=[pl.BlockSpec(memory_space=pltpu.SMEM)] +...  29.5 us
    ppermute x10, starting transfers between devices, send(): return lax.ppermute(value, PLANE, ring(axis, step))  14 us
    ppermute x4, starting transfers between devices, sibling(): return lax.ppermute(value, 'core', [(0, 1), (1, 0)])  9.59 us
    ppermute x10, waiting for transfers between devices, send(): return lax.ppermute(value, PLANE, ring(axis, step))  8.87 us
    pallas_call x1, Pallas kernels, on_device(): pl.pallas_call(momentum_kernel, out_shape=jax.ShapeDtypeStruct(momentum.s...  5.23 us
    ppermute x3, starting transfers between devices, on_device(): lax.ppermute(chosen, 'x', [(i, (i + step) % REPS) for i in range(REPS)])  4.97 us
    pallas_call x1, Pallas kernels, on_device(): pl.pallas_call(weight_kernel, out_shape=jax.ShapeDtypeStruct((rows, cols)...  4.53 us
    pallas_call x1, Pallas kernels, on_device(): pl.pallas_call(coeff_kernel, out_shape=(jax.ShapeDtypeStruct((blocks, col...  4.33 us
  transfers between devices with their start and end apart: 17, of which 4 were waited for; matrix products, arithmetic and copies ran while one was open for 0% of the time, Pallas kernels for 50%

profile of v4, /device:TPU:1, one launch (start us, length us, event | category | flops | bytes accessed | tf_op | source)
XLA Modules:
  0.0 84.1 jit_solution(6126212862004644065)
XLA Ops:
  0.6 1.5 %collective-permute-start.7 = (bf16[1024,8192]{1,0:T(8,128)(2,1)}, bf16[1024,8192]{1,0:T(8,128)(2,1)}, u32[]{:S(2)}, u32[]{:S(2)}) collective-permute-start(bf16[1024,8192]{1,0:T(8,128)(2,1)} %refs_2_.3), channel_id=1, source_target_pairs={{0,1},{1,0},{2,3},{3,2},{4,5},{5,4},{6,7},{7,6},{8,9},{9,8},{10,11... | collective-permute-start | bytes 50331656 | tf_op jit(solution)/shard_map/ppermute | solution.py:194
  2.1 4.3 %shard_map.112 = (f32[4,1024]{1,0:T(4,128)S(1)}, s32[2,1,8,1024]{3,2,1,0:T(8,128)S(1)}) custom-call(f32[1,256,1024]{2,1,0:T(8,128)} %momentum.3, f32[1,256,1024]{2,1,0:T(8,128)} %grad.3, s32[4,16,64,128]{3,2,1,0:T(8,128)} %bitcast.1, f32[256,256]{1,0:T(8,128)} %constant.31.clone.basis), custom_call_target="tpu_custom_call" | custom-call | flops 1000 | bytes 1000 | tf_op jit(solution)/shard_map/pallas_call | solution.py:330
  6.5 1.4 %collective-permute-start = (f32[4,1024]{1,0:T(4,128)S(1)}, f32[4,1024]{1,0:T(4,128)S(1)}, u32[]{:S(2)}, u32[]{:S(2)}) collective-permute-start(f32[4,1024]{1,0:T(4,128)S(1)} %get-tuple-element.38.chosen0), channel_id=1, source_target_pairs={{0,32},{32,64},{64,96},{96,0},{1,33},{33,65},{65,97},{97,1},{2,34}... | collective-permute-start | bytes 49160 | tf_op jit(solution)/shard_map/ppermute | solution.py:348
  7.9 2.4 %collective-permute-start.1 = (f32[4,1024]{1,0:T(4,128)S(1)}, f32[4,1024]{1,0:T(4,128)S(1)}, u32[]{:S(2)}, u32[]{:S(2)}) collective-permute-start(f32[4,1024]{1,0:T(4,128)S(1)} %get-tuple-element.38.chosen0), channel_id=1, source_target_pairs={{0,64},{32,96},{64,0},{96,32},{1,65},{33,97},{65,1},{97,33},{2,66}... | collective-permute-start | bytes 49160 | tf_op jit(solution)/shard_map/ppermute | solution.py:348
  10.3 1.2 %collective-permute-start.2 = (f32[4,1024]{1,0:T(4,128)S(1)}, f32[4,1024]{1,0:T(4,128)S(1)}, u32[]{:S(2)}, u32[]{:S(2)}) collective-permute-start(f32[4,1024]{1,0:T(4,128)S(1)} %get-tuple-element.38.chosen0), channel_id=1, source_target_pairs={{0,96},{32,0},{64,32},{96,64},{1,97},{33,1},{65,33},{97,65},{2,98}... | collective-permute-start | bytes 49160 | tf_op jit(solution)/shard_map/ppermute | solution.py:348
  11.5 1.8 %shard_map.113.others = s32[2,3,8,1024]{3,2,1,0:T(8,128)S(1)} custom-call(s32[4,16,64,128]{3,2,1,0:T(8,128)} %bitcast.2), custom_call_target="tpu_custom_call" | custom-call | flops 1000 | bytes 1000 | tf_op jit(solution)/shard_map/pallas_call | solution.py:350
  13.4 4.5 %shard_map.114 = bf16[256,1024]{1,0:T(8,128)(2,1)} custom-call(bf16[256,1024]{1,0:T(8,128)(2,1)S(1)} %copy-done.3, f32[4,1024]{1,0:T(4,128)S(1)} %get-tuple-element.38.chosen0, f32[4,1024]{1,0:T(4,128)S(1)} %collective-permute-done.chosen1, f32[4,1024]{1,0:T(4,128)S(1)} %collective-permute-done.1.chosen2, f32[4,1024]{1,0:T(4,128)S(1)} %collective-permute-done.2.chosen3, ...), custom_call_target="tpu_custom_call" | custom-call | flops 1000 | bytes 1000 | tf_op jit(solution)/shard_map/pallas_call | solution.py:360
  17.9 1.6 %collective-permute-start.3 = (bf16[256,1024]{1,0:T(8,128)(2,1)}, bf16[256,1024]{1,0:T(8,128)(2,1)S(1)}, u32[]{:S(2)}, u32[]{:S(2)}) collective-permute-start(bf16[256,1024]{1,0:T(8,128)(2,1)} %shard_map.114), channel_id=1, source_target_pairs={{0,8},{1,3},{2,10},{3,5},{4,12},{5,7},{6,14},{7,1},{8,16},{9,11},{... | collective-permute-start | bytes 1572872 | tf_op jit(solution)/shard_map/ppermute | solution.py:190
  19.5 2.1 %collective-permute-start.4 = (bf16[256,1024]{1,0:T(8,128)(2,1)}, bf16[256,1024]{1,0:T(8,128)(2,1)S(1)}, u32[]{:S(2)}, u32[]{:S(2)}) collective-permute-start(bf16[256,1024]{1,0:T(8,128)(2,1)} %shard_map.114), channel_id=1, source_target_pairs={{0,24},{1,7},{2,26},{3,1},{4,28},{5,3},{6,30},{7,5},{8,0},{9,15},{... | collective-permute-start | bytes 1572872 | tf_op jit(solution)/shard_map/ppermute | solution.py:190
  21.7 5.2 %shard_map.115 = f32[1,256,1024]{2,1,0:T(8,128)} custom-call(f32[1,256,1024]{2,1,0:T(8,128)S(1)} %copy-done, f32[1,256,1024]{2,1,0:T(8,128)S(1)} %copy-done.1, s32[2,1,8,1024]{3,2,1,0:T(8,128)S(1)} %get-tuple-element.39.where, f32[256,256]{1,0:T(8,128)S(1)} %copy-done.2), custom_call_target="tpu_custom_call" | custom-call | flops 1000 | bytes 1000 | tf_op jit(solution)/shard_map/pallas_call | solution.py:372
  26.9 1.9 %collective-permute-done.3 = bf16[256,1024]{1,0:T(8,128)(2,1)S(1)} collective-permute-done((bf16[256,1024]{1,0:T(8,128)(2,1)}, bf16[256,1024]{1,0:T(8,128)(2,1)S(1)}, u32[]{:S(2)}, u32[]{:S(2)}) %collective-permute-start.3) | collective-permute-done | bytes 524320 | tf_op jit(solution)/shard_map/ppermute | solution.py:190
  30.0 1.8 %collective-permute-start.10 = (bf16[512,1024]{1,0:T(8,128)(2,1)S(1)}, bf16[512,1024]{1,0:T(8,128)(2,1)S(1)}, u32[]{:S(2)}, u32[]{:S(2)}) collective-permute-start(bf16[512,1024]{1,0:T(8,128)(2,1)S(1)} %pad_maximum_fusion.refs_4_), channel_id=1, source_target_pairs={{0,6},{1,25},{2,0},{3,27},{4,2},{5,29},{6,4},{7,31},{8,14},{9,1},{... | collective-permute-start | bytes 3145736 | tf_op jit(solution)/shard_map/ppermute | solution.py:190
  32.7 1.8 %collective-permute-start.6 = (bf16[128,1024]{1,0:T(8,128)(2,1)S(1)}, bf16[128,1024]{1,0:T(8,128)(2,1)S(1)}, u32[]{:S(2)}, u32[]{:S(2)}) collective-permute-start(bf16[128,1024]{1,0:T(8,128)(2,1)S(1)} %slice.7), channel_id=1, source_target_pairs={{0,24},{1,7},{2,26},{3,1},{4,28},{5,3},{6,30},{7,5},{8,0},{9,15},{... | collective-permute-start | bytes 786440 | tf_op jit(solution)/shard_map/ppermute | solution.py:190
  34.6 6.1 %shard_map.116 = (f32[1024,1024]{1,0:T(8,128)S(1)}, f32[1024,1024]{1,0:T(8,128)S(1)}, bf16[1024,1536]{1,0:T(8,128)(2,1)S(1)}, bf16[1024,1536]{1,0:T(8,128)(2,1)S(1)}, f32[8,128]{1,0:T(8,128)S(1)}) custom-call(s32[32]{0:T(128)S(1)} %select_add_fusion.ids, f32[8,128]{1,0:T(8,128)S(1)} %broadcast_in_dim.13._, bf16[1024,8192]{1,0:T(8,128)(2,1)} %refs_2_.3, ...), custom_call_target="tpu_custom_call" | custom-call | flops 10000000000 | bytes 1000 | tf_op jit(solution)/shard_map/pallas_call | solution.py:307
  42.9 4.1 %collective-permute-done.9.refs_3_ = bf16[512,1024]{1,0:T(8,128)(2,1)S(1)} collective-permute-done((bf16[512,1024]{1,0:T(8,128)(2,1)S(1)}, bf16[512,1024]{1,0:T(8,128)(2,1)S(1)}, u32[]{:S(2)}, u32[]{:S(2)}) %collective-permute-start.9) | collective-permute-done | bytes 1048608 | tf_op jit(solution)/shard_map/ppermute | solution.py:190
  47.0 8.7 %shard_map.117 = (f32[1024,1024]{1,0:T(8,128)S(1)}, f32[1024,1024]{1,0:T(8,128)S(1)}, bf16[1024,1024]{1,0:T(8,128)(2,1)S(1)}, bf16[1024,1024]{1,0:T(8,128)(2,1)S(1)}, f32[8,128]{1,0:T(8,128)S(1)}) custom-call(s32[32]{0:T(128)S(1)} %select_add_fusion.ids, f32[8,128]{1,0:T(8,128)S(1)} %get-tuple-element.45._, ...), custom_call_target="tpu_custom_call", output_to_operand_aliasing={{0}: (9, {}), {1}: (10, {})} | custom-call | flops 1000 | bytes 1000 | tf_op jit(solution)/shard_map/pallas_call | solution.py:307
  55.7 2.3 %collective-permute-done.8.refs_4_ = bf16[512,1024]{1,0:T(8,128)(2,1)S(1)} collective-permute-done((bf16[512,1024]{1,0:T(8,128)(2,1)S(1)}, bf16[512,1024]{1,0:T(8,128)(2,1)S(1)}, u32[]{:S(2)}, u32[]{:S(2)}) %collective-permute-start.8) | collective-permute-done | bytes 1048608 | tf_op jit(solution)/shard_map/ppermute | solution.py:190
  58.0 3.0 %collective-permute-start.11 = (bf16[512,1024]{1,0:T(8,128)(2,1)S(1)}, bf16[512,1024]{1,0:T(8,128)(2,1)S(1)}, u32[]{:S(2)}, u32[]{:S(2)}) collective-permute-start(bf16[512,1024]{1,0:T(8,128)(2,1)S(1)} %collective-permute-done.8.refs_4_), channel_id=1, source_target_pairs={{0,6},{1,25},{2,0},{3,27},{4,2},{5,29},{6,4},{7,31},{8,14},{9,1},{... | collective-permute-start | bytes 3145736 | tf_op jit(solution)/shard_map/ppermute | solution.py:190
  61.0 5.9 %shard_map.118 = (f32[1024,1024]{1,0:T(8,128)S(1)}, bf16[1024,1024]{1,0:T(8,128)(2,1)S(1)}, bf16[1024,512]{1,0:T(8,128)(2,1)S(1)}, bf16[1024,1024]{1,0:T(8,128)(...) custom-call(s32[32]{0:T(128)S(1)} %select_add_fusion.ids, ...), custom_call_target="tpu_custom_call", output_to_operand_aliasing={{0}: (9, {})} | custom-call | flops 1000 | bytes 1000 | tf_op jit(solution)/shard_map/pallas_call | solution.py:307
  66.9 3.5 %collective-permute-start.16 = (bf16[1024,1024]{1,0:T(8,128)(2,1)S(1)}, bf16[1024,1024]{1,0:T(8,128)(2,1)S(1)}, u32[]{:S(2)}, u32[]{:S(2)}) collective-permute-start(bf16[1024,1024]{1,0:T(8,128)(2,1)S(1)} %get-tuple-element.70), channel_id=1, source_target_pairs={{0,1},{1,0},{2,3},{3,2},{4,5},{5,4},{6,7},{7,6},{8,9},{9,8},{10,11... | collective-permute-start | bytes 6291464 | tf_op jit(solution)/shard_map/ppermute | solution.py:194
  70.5 4.2 %collective-permute-start.14 = (bf16[512,1024]{1,0:T(8,128)(2,1)S(1)}, bf16[512,1024]{1,0:T(8,128)(2,1)S(1)}, u32[]{:S(2)}, u32[]{:S(2)}) collective-permute-start(bf16[512,1024]{1,0:T(8,128)(2,1)S(1)} %collective-permute-done.12.refs_0_), channel_id=1, source_target_pairs={{0,1},{1,0},{2,3},{3,2},{4,5},{5,4},{6,7},{7,6},{8,9},{9,8},{10,11... | collective-permute-start | bytes 3145736 | tf_op jit(solution)/shard_map/ppermute | solution.py:194
  74.7 2.1 %shard_map.119 = (f32[1024,1024]{1,0:T(8,128)S(1)}, f32[8,128]{1,0:T(8,128)S(1)}) custom-call(s32[32]{0:T(128)S(1)} %select_add_fusion.ids, f32[8,128]{1,0:T(8,128)S(1)} %get-tuple-element.58._, bf16[512,1024]{1,0:T(8,128)(2,1)S(1)} %collective-permute-done.12.refs_0_, ...), custom_call_target="tpu_custom_call", output_to_operand_aliasing={{0}: (4, {})} | custom-call | flops 1000 | bytes 1000 | tf_op jit(solution)/shard_map/pallas_call | solution.py:307
  77.2 3.5 %shard_map.120 = (f32[1024,1024]{1,0:T(8,128)S(1)}, f32[8,128]{1,0:T(8,128)S(1)}) custom-call(s32[32]{0:T(128)S(1)} %select_add_fusion.ids, f32[8,128]{1,0:T(8,128)S(1)} %get-tuple-element.63._, bf16[512,1024]{1,0:T(8,128)(2,1)S(1)} %collective-permute-done.14.refs_0_, ...), custom_call_target="tpu_custom_call", output_to_operand_aliasing={{0}: (5, {})} | custom-call | flops 1000 | bytes 1000 | tf_op jit(solution)/shard_map/pallas_call | solution.py:307
  80.8 3.2 %shard_map.121 = (bf16[1024,1024]{1,0:T(8,128)(2,1)}, f32[8,128]{1,0:T(8,128)}) custom-call(s32[32]{0:T(128)S(1)} %select_add_fusion.ids, f32[8,128]{1,0:T(8,128)S(1)} %get-tuple-element.67._, bf16[512,1024]{1,0:T(8,128)(2,1)S(1)} %collective-permute-done.15.refs_0_, bf16[1024,512]{1,0:T(8,128)(2,1)S(1)} %get-tuple-element.68.refs_1_, ...), custom_call_target="tpu_custom_call" | custom-call | flops 1000 | bytes 1000 | tf_op jit(solution)/shard_map/pallas_call | solution.py:307
  (44 shorter events, 4.7 us)
Async XLA Ops:
  0.6 34.0 %collective-permute-start.7 = (bf16[1024,8192]{1,0:T(8,128)(2,1)}, bf16[1024,8192]{1,0:T(8,128)(2,1)}, u32[]{:S(2)}, u32[]{:S(2)}) collective-permute-start(bf16[1024,8192]{1,0:T(8,128)(2,1)} %refs_2_.3), channel_id=1, source_target_pairs={{0,1},{1,0},{2,3},{3,2},{4,5},{5,4},{6,7},{7,6},{8,9},{9,8},{10,11... | collective-permute-start | bytes 50331656 | tf_op jit(solution)/shard_map/ppermute | solution.py:194
  2.1 11.2 %copy-start.2 = (f32[256,256]{1,0:T(8,128)S(1)}, f32[256,256]{1,0:T(8,128)}, u32[]{:S(2)}) copy-start(f32[256,256]{1,0:T(8,128)} %constant.31.clone.basis) | copy-start | bytes 786436
  2.1 11.2 %copy-start.3 = (bf16[256,1024]{1,0:T(8,128)(2,1)S(1)}, bf16[256,1024]{1,0:T(8,128)(2,1)}, u32[]{:S(2)}) copy-start(bf16[256,1024]{1,0:T(8,128)(2,1)} %weight.1) | copy-start | bytes 1572868
  2.1 19.5 %copy-start = (f32[1,256,1024]{2,1,0:T(8,128)S(1)}, f32[1,256,1024]{2,1,0:T(8,128)}, u32[]{:S(2)}) copy-start(f32[1,256,1024]{2,1,0:T(8,128)} %momentum.3) | copy-start | bytes 3145732
  2.1 19.5 %copy-start.1 = (f32[1,256,1024]{2,1,0:T(8,128)S(1)}, f32[1,256,1024]{2,1,0:T(8,128)}, u32[]{:S(2)}) copy-start(f32[1,256,1024]{2,1,0:T(8,128)} %grad.3) | copy-start | bytes 3145732
  6.5 20.4 %copy-start.5 = (s32[32]{0:T(128)S(1)}, s32[32]{0:T(128)}, u32[]{:S(2)}) copy-start(s32[32]{0:T(128)} %constant.32.clone) | copy-start | bytes 388
  6.5 20.4 %copy-start.6 = (s32[32]{0:T(128)S(1)}, s32[32]{0:T(128)}, u32[]{:S(2)}) copy-start(s32[32]{0:T(128)} %constant.33.clone) | copy-start | bytes 388
  6.5 20.4 %copy-start.7 = (pred[32]{0:T(512)(128)(4,1)S(1)}, pred[32]{0:T(512)(128)(4,1)}, u32[]{:S(2)}) copy-start(pred[32]{0:T(512)(128)(4,1)} %constant.34.clone) | copy-start | bytes 100
  6.5 6.8 %collective-permute-start = (f32[4,1024]{1,0:T(4,128)S(1)}, f32[4,1024]{1,0:T(4,128)S(1)}, u32[]{:S(2)}, u32[]{:S(2)}) collective-permute-start(f32[4,1024]{1,0:T(4,128)S(1)} %get-tuple-element.38.chosen0), channel_id=1, source_target_pairs={{0,32},{32,64},{64,96},{96,0},{1,33},{33,65},{65,97},{97,1},{2,34}... | collective-permute-start | bytes 49160 | tf_op jit(solution)/shard_map/ppermute | solution.py:348
  7.9 5.5 %collective-permute-start.1 = (f32[4,1024]{1,0:T(4,128)S(1)}, f32[4,1024]{1,0:T(4,128)S(1)}, u32[]{:S(2)}, u32[]{:S(2)}) collective-permute-start(f32[4,1024]{1,0:T(4,128)S(1)} %get-tuple-element.38.chosen0), channel_id=1, source_target_pairs={{0,64},{32,96},{64,0},{96,32},{1,65},{33,97},{65,1},{97,33},{2,66}... | collective-permute-start | bytes 49160 | tf_op jit(solution)/shard_map/ppermute | solution.py:348
  10.3 3.0 %collective-permute-start.2 = (f32[4,1024]{1,0:T(4,128)S(1)}, f32[4,1024]{1,0:T(4,128)S(1)}, u32[]{:S(2)}, u32[]{:S(2)}) collective-permute-start(f32[4,1024]{1,0:T(4,128)S(1)} %get-tuple-element.38.chosen0), channel_id=1, source_target_pairs={{0,96},{32,0},{64,32},{96,64},{1,97},{33,1},{65,33},{97,65},{2,98}... | collective-permute-start | bytes 49160 | tf_op jit(solution)/shard_map/ppermute | solution.py:348
  17.9 10.9 %collective-permute-start.3 = (bf16[256,1024]{1,0:T(8,128)(2,1)}, bf16[256,1024]{1,0:T(8,128)(2,1)S(1)}, u32[]{:S(2)}, u32[]{:S(2)}) collective-permute-start(bf16[256,1024]{1,0:T(8,128)(2,1)} %shard_map.114), channel_id=1, source_target_pairs={{0,8},{1,3},{2,10},{3,5},{4,12},{5,7},{6,14},{7,1},{8,16},{9,11},{... | collective-permute-start | bytes 1572872 | tf_op jit(solution)/shard_map/ppermute | solution.py:190
  19.5 9.3 %collective-permute-start.4 = (bf16[256,1024]{1,0:T(8,128)(2,1)}, bf16[256,1024]{1,0:T(8,128)(2,1)S(1)}, u32[]{:S(2)}, u32[]{:S(2)}) collective-permute-start(bf16[256,1024]{1,0:T(8,128)(2,1)} %shard_map.114), channel_id=1, source_target_pairs={{0,24},{1,7},{2,26},{3,1},{4,28},{5,3},{6,30},{7,5},{8,0},{9,15},{... | collective-permute-start | bytes 1572872 | tf_op jit(solution)/shard_map/ppermute | solution.py:190
  28.9 18.1 %collective-permute-start.9 = (bf16[512,1024]{1,0:T(8,128)(2,1)S(1)}, bf16[512,1024]{1,0:T(8,128)(2,1)S(1)}, u32[]{:S(2)}, u32[]{:S(2)}) collective-permute-start(bf16[512,1024]{1,0:T(8,128)(2,1)S(1)} %pad_maximum_fusion.refs_4_), channel_id=1, source_target_pairs={{0,2},{1,9},{2,4},{3,11},{4,6},{5,13},{6,0},{7,15},{8,10},{9,17},{... | collective-permute-start | bytes 3145736 | tf_op jit(solution)/shard_map/ppermute | solution.py:190
  30.0 17.0 %collective-permute-start.10 = (bf16[512,1024]{1,0:T(8,128)(2,1)S(1)}, bf16[512,1024]{1,0:T(8,128)(2,1)S(1)}, u32[]{:S(2)}, u32[]{:S(2)}) collective-permute-start(bf16[512,1024]{1,0:T(8,128)(2,1)S(1)} %pad_maximum_fusion.refs_4_), channel_id=1, source_target_pairs={{0,6},{1,25},{2,0},{3,27},{4,2},{5,29},{6,4},{7,31},{8,14},{9,1},{... | collective-permute-start | bytes 3145736 | tf_op jit(solution)/shard_map/ppermute | solution.py:190
  31.8 9.5 %collective-permute-start.5 = (bf16[128,1024]{1,0:T(8,128)(2,1)S(1)}, bf16[128,1024]{1,0:T(8,128)(2,1)S(1)}, u32[]{:S(2)}, u32[]{:S(2)}) collective-permute-start(bf16[128,1024]{1,0:T(8,128)(2,1)S(1)} %slice.6), channel_id=1, source_target_pairs={{0,8},{1,3},{2,10},{3,5},{4,12},{5,7},{6,14},{7,1},{8,16},{9,11},{... | collective-permute-start | bytes 786440 | tf_op jit(solution)/shard_map/ppermute | solution.py:190
  32.7 8.6 %collective-permute-start.6 = (bf16[128,1024]{1,0:T(8,128)(2,1)S(1)}, bf16[128,1024]{1,0:T(8,128)(2,1)S(1)}, u32[]{:S(2)}, u32[]{:S(2)}) collective-permute-start(bf16[128,1024]{1,0:T(8,128)(2,1)S(1)} %slice.7), channel_id=1, source_target_pairs={{0,24},{1,7},{2,26},{3,1},{4,28},{5,3},{6,30},{7,5},{8,0},{9,15},{... | collective-permute-start | bytes 786440 | tf_op jit(solution)/shard_map/ppermute | solution.py:190
  41.4 16.6 %collective-permute-start.8 = (bf16[512,1024]{1,0:T(8,128)(2,1)S(1)}, bf16[512,1024]{1,0:T(8,128)(2,1)S(1)}, u32[]{:S(2)}, u32[]{:S(2)}) collective-permute-start(bf16[512,1024]{1,0:T(8,128)(2,1)S(1)} %constant_dynamic-update-slice_fusion.refs_2_), channel_id=1, source_target_pairs={{0,6},{1,25},{2,0},{3,27},{4,2},{5,29},{6,4},{7,31},{8,14},{9,1},{... | collective-permute-start | bytes 3145736 | tf_op jit(solution)/shard_map/ppermute | solution.py:190
  42.3 18.7 %collective-permute-start.13 = (bf16[512,1024]{1,0:T(8,128)(2,1)S(1)}, bf16[512,1024]{1,0:T(8,128)(2,1)S(1)}, u32[]{:S(2)}, u32[]{:S(2)}) collective-permute-start(bf16[512,1024]{1,0:T(8,128)(2,1)S(1)} %constant_dynamic-update-slice_fusion.refs_2_), channel_id=1, source_target_pairs={{0,2},{1,9},{2,4},{3,11},{4,6},{5,13},{6,0},{7,15},{8,10},{9,17},{... | collective-permute-start | bytes 3145736 | tf_op jit(solution)/shard_map/ppermute | solution.py:190
  47.0 23.4 %collective-permute-start.12 = (bf16[512,1024]{1,0:T(8,128)(2,1)S(1)}, bf16[512,1024]{1,0:T(8,128)(2,1)S(1)}, u32[]{:S(2)}, u32[]{:S(2)}) collective-permute-start(bf16[512,1024]{1,0:T(8,128)(2,1)S(1)} %collective-permute-done.9.refs_3_), channel_id=1, source_target_pairs={{0,2},{1,9},{2,4},{3,11},{4,6},{5,13},{6,0},{7,15},{8,10},{9,17},{... | collective-permute-start | bytes 3145736 | tf_op jit(solution)/shard_map/ppermute | solution.py:190
  58.0 18.8 %collective-permute-start.11 = (bf16[512,1024]{1,0:T(8,128)(2,1)S(1)}, bf16[512,1024]{1,0:T(8,128)(2,1)S(1)}, u32[]{:S(2)}, u32[]{:S(2)}) collective-permute-start(bf16[512,1024]{1,0:T(8,128)(2,1)S(1)} %collective-permute-done.8.refs_4_), channel_id=1, source_target_pairs={{0,6},{1,25},{2,0},{3,27},{4,2},{5,29},{6,4},{7,31},{8,14},{9,1},{... | collective-permute-start | bytes 3145736 | tf_op jit(solution)/shard_map/ppermute | solution.py:190
  66.9 13.8 %collective-permute-start.16 = (bf16[1024,1024]{1,0:T(8,128)(2,1)S(1)}, bf16[1024,1024]{1,0:T(8,128)(2,1)S(1)}, u32[]{:S(2)}, u32[]{:S(2)}) collective-permute-start(bf16[1024,1024]{1,0:T(8,128)(2,1)S(1)} %get-tuple-element.70), channel_id=1, source_target_pairs={{0,1},{1,0},{2,3},{3,2},{4,5},{5,4},{6,7},{7,6},{8,9},{9,8},{10,11... | collective-permute-start | bytes 6291464 | tf_op jit(solution)/shard_map/ppermute | solution.py:194
  70.5 6.7 %collective-permute-start.14 = (bf16[512,1024]{1,0:T(8,128)(2,1)S(1)}, bf16[512,1024]{1,0:T(8,128)(2,1)S(1)}, u32[]{:S(2)}, u32[]{:S(2)}) collective-permute-start(bf16[512,1024]{1,0:T(8,128)(2,1)S(1)} %collective-permute-done.12.refs_0_), channel_id=1, source_target_pairs={{0,1},{1,0},{2,3},{3,2},{4,5},{5,4},{6,7},{7,6},{8,9},{9,8},{10,11... | collective-permute-start | bytes 3145736 | tf_op jit(solution)/shard_map/ppermute | solution.py:194
  76.8 3.9 %collective-permute-start.15 = (bf16[512,1024]{1,0:T(8,128)(2,1)S(1)}, bf16[512,1024]{1,0:T(8,128)(2,1)S(1)}, u32[]{:S(2)}, u32[]{:S(2)}) collective-permute-start(bf16[512,1024]{1,0:T(8,128)(2,1)S(1)} %collective-permute-done.11.refs_1_), channel_id=1, source_target_pairs={{0,1},{1,0},{2,3},{3,2},{4,5},{5,4},{6,7},{7,6},{8,9},{9,8},{10,11... | collective-permute-start | bytes 3145736 | tf_op jit(solution)/shard_map/ppermute | solution.py:194
  (1 other events, 10.9 us)

commit v5 on v4

--- a/solution.py
+++ b/solution.py
@@ -128,21 +128,29 @@
 def weight_kernel(weight, chosen0, chosen1, chosen2, chosen3, where, others, basis, new_weight, dense):
     rows, cols = weight.shape
     base = halves(basis[...])
-    values = []
+    blocks = rows // GROUP
+    kinds = [[], [], [], []]
     for k, chosen in enumerate((chosen0, chosen1, chosen2, chosen3)):
+        places, r = (others, k - 1) if k else (where, 0)
         high, low = halves(chosen[...])
-        values.append((others if k else where, max(k - 1, 0), high.astype(jnp.float32), low.astype(jnp.float32)))
+        kinds[0].append(places[0, r][:blocks])
+        kinds[1].append(jnp.bitwise_and(places[1, r][:blocks], GROUP - 1))
+        kinds[2].append(high.astype(jnp.float32))
+        kinds[3].append(low.astype(jnp.float32))
+    lane = lax.broadcasted_iota(jnp.int32, (GROUP, PAIR), 1)
     for p in range(0, cols, PAIR):
-        for a in range(rows // GROUP):
-            lefts, highs, lows = [], [], []
-            for places, r, high, low in values:
-                lefts.append(one_hot(places[0, r, a : a + 1, p : p + PAIR], GROUP))
-                hit = is_row(places[1, r, a : a + 1, p : p + PAIR], PAIR)
-                highs.append(jnp.where(hit, high[a : a + 1, p : p + PAIR], 0.0).astype(jnp.bfloat16))
-                lows.append(jnp.where(hit, low[a : a + 1, p : p + PAIR], 0.0).astype(jnp.bfloat16))
-            right = jnp.concatenate([jnp.concatenate(highs, axis=1), jnp.concatenate(lows, axis=1)], axis=0)
-            both = lax.dot_general(jnp.concatenate(lefts, axis=1), right, NT, preferred_element_type=jnp.float32)
-            dense[a * GROUP : (a + 1) * GROUP, p : p + PAIR] = both[:, :PAIR] + both[:, PAIR:]
+        sides = []
+        for at in (p, p + GROUP):
+            sides.append([jnp.concatenate([x[:, at : at + KEEP] for x in kind], axis=1) for kind in kinds])
+        for a in range(blocks):
+            sums = []
+            for row, col, high, low in sides:
+                left = one_hot(row[a : a + 1], GROUP)
+                hit = is_row(col[a : a + 1], GROUP)
+                right = [jnp.where(hit, x[a : a + 1], 0.0).astype(jnp.bfloat16) for x in (high, low)]
+                both = lax.dot_general(left, jnp.concatenate(right, axis=0), NT, preferred_element_type=jnp.float32)
+                sums.append(both + pltpu.roll(both, GROUP, 1))
+            dense[a * GROUP : (a + 1) * GROUP, p : p + PAIR] = jnp.where(lane < GROUP, *sums)
     inner = halves(dot3(base, halves(dense[...]), TN))
     width = rows
     for c in range(0, cols, width):

time: 84.3 us -> 83 us (0.985)
  Pallas kernels: 45.4 us -> 44.4 us
    pallas_call x1, Pallas kernels: 4.53 us -> 3.54 us  [on_device(): pl.pallas_call(weight_kernel, out_shape=jax.ShapeDtypeStruct((rows, cols)...]
where the time goes in v5:
time: 83 us; the launch traced here: 82.9 us
  Pallas kernels  44.4 us (53%)
  starting transfers between devices  28.5 us (34%)
  waiting for transfers between devices  8.72 us (11%)
  between operations  1.04 us (1%)
    pallas_call x6, Pallas kernels, multiply(): pl.pallas_call(kernel, in_specs=[pl.BlockSpec(memory_space=pltpu.SMEM)] +...  29.5 us
    ppermute x10, starting transfers between devices, send(): return lax.ppermute(value, PLANE, ring(axis, step))  14.3 us
    ppermute x4, starting transfers between devices, sibling(): return lax.ppermute(value, 'core', [(0, 1), (1, 0)])  9.19 us
    ppermute x10, waiting for transfers between devices, send(): return lax.ppermute(value, PLANE, ring(axis, step))  8.69 us
    pallas_call x1, Pallas kernels, on_device(): pl.pallas_call(momentum_kernel, out_shape=jax.ShapeDtypeStruct(momentum.s...  5.23 us
    ppermute x3, starting transfers between devices, on_device(): lax.ppermute(chosen, 'x', [(i, (i + step) % REPS) for i in range(REPS)])  4.97 us
    pallas_call x1, Pallas kernels, on_device(): pl.pallas_call(coeff_kernel, out_shape=(jax.ShapeDtypeStruct((blocks, col...  4.33 us
    pallas_call x1, Pallas kernels, on_device(): pl.pallas_call(weight_kernel, out_shape=jax.ShapeDtypeStruct((rows, cols)...  3.54 us
  transfers between devices with their start and end apart: 17, of which 4 were waited for; matrix products, arithmetic and copies ran while one was open for 0% of the time, Pallas kernels for 50%

profile of v5, /device:TPU:1, one launch (start us, length us, event | category | flops | bytes accessed | tf_op | source)
XLA Modules:
  0.0 82.9 jit_solution(8102931255375865594)
XLA Ops:
  0.6 1.5 %collective-permute-start.7 = (bf16[1024,8192]{1,0:T(8,128)(2,1)}, bf16[1024,8192]{1,0:T(8,128)(2,1)}, u32[]{:S(2)}, u32[]{:S(2)}) collective-permute-start(bf16[1024,8192]{1,0:T(8,128)(2,1)} %refs_2_.3), channel_id=1, source_target_pairs={{0,1},{1,0},{2,3},{3,2},{4,5},{5,4},{6,7},{7,6},{8,9},{9,8},{10,11... | collective-permute-start | bytes 50331656 | tf_op jit(solution)/shard_map/ppermute | solution.py:202
  2.1 4.3 %shard_map.112 = (f32[4,1024]{1,0:T(4,128)S(1)}, s32[2,1,8,1024]{3,2,1,0:T(8,128)S(1)}) custom-call(f32[1,256,1024]{2,1,0:T(8,128)} %momentum.3, f32[1,256,1024]{2,1,0:T(8,128)} %grad.3, s32[4,16,64,128]{3,2,1,0:T(8,128)} %bitcast.1, f32[256,256]{1,0:T(8,128)} %constant.31.clone.basis), custom_call_target="tpu_custom_call" | custom-call | flops 1000 | bytes 1000 | tf_op jit(solution)/shard_map/pallas_call | solution.py:338
  6.5 1.4 %collective-permute-start = (f32[4,1024]{1,0:T(4,128)S(1)}, f32[4,1024]{1,0:T(4,128)S(1)}, u32[]{:S(2)}, u32[]{:S(2)}) collective-permute-start(f32[4,1024]{1,0:T(4,128)S(1)} %get-tuple-element.38.chosen0), channel_id=1, source_target_pairs={{0,32},{32,64},{64,96},{96,0},{1,33},{33,65},{65,97},{97,1},{2,34}... | collective-permute-start | bytes 49160 | tf_op jit(solution)/shard_map/ppermute | solution.py:356
  7.9 2.4 %collective-permute-start.1 = (f32[4,1024]{1,0:T(4,128)S(1)}, f32[4,1024]{1,0:T(4,128)S(1)}, u32[]{:S(2)}, u32[]{:S(2)}) collective-permute-start(f32[4,1024]{1,0:T(4,128)S(1)} %get-tuple-element.38.chosen0), channel_id=1, source_target_pairs={{0,64},{32,96},{64,0},{96,32},{1,65},{33,97},{65,1},{97,33},{2,66}... | collective-permute-start | bytes 49160 | tf_op jit(solution)/shard_map/ppermute | solution.py:356
  10.3 1.2 %collective-permute-start.2 = (f32[4,1024]{1,0:T(4,128)S(1)}, f32[4,1024]{1,0:T(4,128)S(1)}, u32[]{:S(2)}, u32[]{:S(2)}) collective-permute-start(f32[4,1024]{1,0:T(4,128)S(1)} %get-tuple-element.38.chosen0), channel_id=1, source_target_pairs={{0,96},{32,0},{64,32},{96,64},{1,97},{33,1},{65,33},{97,65},{2,98}... | collective-permute-start | bytes 49160 | tf_op jit(solution)/shard_map/ppermute | solution.py:356
  11.5 1.8 %shard_map.113.others = s32[2,3,8,1024]{3,2,1,0:T(8,128)S(1)} custom-call(s32[4,16,64,128]{3,2,1,0:T(8,128)} %bitcast.2), custom_call_target="tpu_custom_call" | custom-call | flops 1000 | bytes 1000 | tf_op jit(solution)/shard_map/pallas_call | solution.py:358
  13.4 3.5 %shard_map.114 = bf16[256,1024]{1,0:T(8,128)(2,1)} custom-call(bf16[256,1024]{1,0:T(8,128)(2,1)S(1)} %copy-done.3, f32[4,1024]{1,0:T(4,128)S(1)} %get-tuple-element.38.chosen0, f32[4,1024]{1,0:T(4,128)S(1)} %collective-permute-done.chosen1, f32[4,1024]{1,0:T(4,128)S(1)} %collective-permute-done.1.chosen2, f32[4,1024]{1,0:T(4,128)S(1)} %collective-permute-done.2.chosen3, ...), custom_call_target="tpu_custom_call" | custom-call | flops 1000 | bytes 1000 | tf_op jit(solution)/shard_map/pallas_call | solution.py:368
  16.9 1.6 %collective-permute-start.3 = (bf16[256,1024]{1,0:T(8,128)(2,1)}, bf16[256,1024]{1,0:T(8,128)(2,1)S(1)}, u32[]{:S(2)}, u32[]{:S(2)}) collective-permute-start(bf16[256,1024]{1,0:T(8,128)(2,1)} %shard_map.114), channel_id=1, source_target_pairs={{0,8},{1,3},{2,10},{3,5},{4,12},{5,7},{6,14},{7,1},{8,16},{9,11},{... | collective-permute-start | bytes 1572872 | tf_op jit(solution)/shard_map/ppermute | solution.py:198
  18.6 2.1 %collective-permute-start.4 = (bf16[256,1024]{1,0:T(8,128)(2,1)}, bf16[256,1024]{1,0:T(8,128)(2,1)S(1)}, u32[]{:S(2)}, u32[]{:S(2)}) collective-permute-start(bf16[256,1024]{1,0:T(8,128)(2,1)} %shard_map.114), channel_id=1, source_target_pairs={{0,24},{1,7},{2,26},{3,1},{4,28},{5,3},{6,30},{7,5},{8,0},{9,15},{... | collective-permute-start | bytes 1572872 | tf_op jit(solution)/shard_map/ppermute | solution.py:198
  20.7 5.2 %shard_map.115 = f32[1,256,1024]{2,1,0:T(8,128)} custom-call(f32[1,256,1024]{2,1,0:T(8,128)S(1)} %copy-done, f32[1,256,1024]{2,1,0:T(8,128)S(1)} %copy-done.1, s32[2,1,8,1024]{3,2,1,0:T(8,128)S(1)} %get-tuple-element.39.where, f32[256,256]{1,0:T(8,128)S(1)} %copy-done.2), custom_call_target="tpu_custom_call" | custom-call | flops 1000 | bytes 1000 | tf_op jit(solution)/shard_map/pallas_call | solution.py:380
  26.0 1.9 %collective-permute-done.3 = bf16[256,1024]{1,0:T(8,128)(2,1)S(1)} collective-permute-done((bf16[256,1024]{1,0:T(8,128)(2,1)}, bf16[256,1024]{1,0:T(8,128)(2,1)S(1)}, u32[]{:S(2)}, u32[]{:S(2)}) %collective-permute-start.3) | collective-permute-done | bytes 524320 | tf_op jit(solution)/shard_map/ppermute | solution.py:198
  29.0 2.0 %collective-permute-start.10 = (bf16[512,1024]{1,0:T(8,128)(2,1)S(1)}, bf16[512,1024]{1,0:T(8,128)(2,1)S(1)}, u32[]{:S(2)}, u32[]{:S(2)}) collective-permute-start(bf16[512,1024]{1,0:T(8,128)(2,1)S(1)} %pad_maximum_fusion.refs_4_), channel_id=1, source_target_pairs={{0,6},{1,25},{2,0},{3,27},{4,2},{5,29},{6,4},{7,31},{8,14},{9,1},{... | collective-permute-start | bytes 3145736 | tf_op jit(solution)/shard_map/ppermute | solution.py:198
  31.9 1.8 %collective-permute-start.6 = (bf16[128,1024]{1,0:T(8,128)(2,1)S(1)}, bf16[128,1024]{1,0:T(8,128)(2,1)S(1)}, u32[]{:S(2)}, u32[]{:S(2)}) collective-permute-start(bf16[128,1024]{1,0:T(8,128)(2,1)S(1)} %slice.7), channel_id=1, source_target_pairs={{0,24},{1,7},{2,26},{3,1},{4,28},{5,3},{6,30},{7,5},{8,0},{9,15},{... | collective-permute-start | bytes 786440 | tf_op jit(solution)/shard_map/ppermute | solution.py:198
  33.8 6.1 %shard_map.116 = (f32[1024,1024]{1,0:T(8,128)S(1)}, f32[1024,1024]{1,0:T(8,128)S(1)}, bf16[1024,1536]{1,0:T(8,128)(2,1)S(1)}, bf16[1024,1536]{1,0:T(8,128)(2,1)S(1)}, f32[8,128]{1,0:T(8,128)S(1)}) custom-call(s32[32]{0:T(128)S(1)} %select_add_fusion.ids, f32[8,128]{1,0:T(8,128)S(1)} %broadcast_in_dim.13._, bf16[1024,8192]{1,0:T(8,128)(2,1)} %refs_2_.3, ...), custom_call_target="tpu_custom_call" | custom-call | flops 10000000000 | bytes 1000 | tf_op jit(solution)/shard_map/pallas_call | solution.py:315
  42.0 4.0 %collective-permute-done.9.refs_3_ = bf16[512,1024]{1,0:T(8,128)(2,1)S(1)} collective-permute-done((bf16[512,1024]{1,0:T(8,128)(2,1)S(1)}, bf16[512,1024]{1,0:T(8,128)(2,1)S(1)}, u32[]{:S(2)}, u32[]{:S(2)}) %collective-permute-start.9) | collective-permute-done | bytes 1048608 | tf_op jit(solution)/shard_map/ppermute | solution.py:198
  46.0 8.7 %shard_map.117 = (f32[1024,1024]{1,0:T(8,128)S(1)}, f32[1024,1024]{1,0:T(8,128)S(1)}, bf16[1024,1024]{1,0:T(8,128)(2,1)S(1)}, bf16[1024,1024]{1,0:T(8,128)(2,1)S(1)}, f32[8,128]{1,0:T(8,128)S(1)}) custom-call(s32[32]{0:T(128)S(1)} %select_add_fusion.ids, f32[8,128]{1,0:T(8,128)S(1)} %get-tuple-element.45._, ...), custom_call_target="tpu_custom_call", output_to_operand_aliasing={{0}: (9, {}), {1}: (10, {})} | custom-call | flops 1000 | bytes 1000 | tf_op jit(solution)/shard_map/pallas_call | solution.py:315
  54.7 2.3 %collective-permute-done.8.refs_4_ = bf16[512,1024]{1,0:T(8,128)(2,1)S(1)} collective-permute-done((bf16[512,1024]{1,0:T(8,128)(2,1)S(1)}, bf16[512,1024]{1,0:T(8,128)(2,1)S(1)}, u32[]{:S(2)}, u32[]{:S(2)}) %collective-permute-start.8) | collective-permute-done | bytes 1048608 | tf_op jit(solution)/shard_map/ppermute | solution.py:198
  57.0 3.2 %collective-permute-start.11 = (bf16[512,1024]{1,0:T(8,128)(2,1)S(1)}, bf16[512,1024]{1,0:T(8,128)(2,1)S(1)}, u32[]{:S(2)}, u32[]{:S(2)}) collective-permute-start(bf16[512,1024]{1,0:T(8,128)(2,1)S(1)} %collective-permute-done.8.refs_4_), channel_id=1, source_target_pairs={{0,6},{1,25},{2,0},{3,27},{4,2},{5,29},{6,4},{7,31},{8,14},{9,1},{... | collective-permute-start | bytes 3145736 | tf_op jit(solution)/shard_map/ppermute | solution.py:198
  60.2 5.9 %shard_map.118 = (f32[1024,1024]{1,0:T(8,128)S(1)}, bf16[1024,1024]{1,0:T(8,128)(2,1)S(1)}, bf16[1024,512]{1,0:T(8,128)(2,1)S(1)}, bf16[1024,1024]{1,0:T(8,128)(...) custom-call(s32[32]{0:T(128)S(1)} %select_add_fusion.ids, ...), custom_call_target="tpu_custom_call", output_to_operand_aliasing={{0}: (9, {})} | custom-call | flops 1000 | bytes 1000 | tf_op jit(solution)/shard_map/pallas_call | solution.py:315
  66.1 3.5 %collective-permute-start.16 = (bf16[1024,1024]{1,0:T(8,128)(2,1)S(1)}, bf16[1024,1024]{1,0:T(8,128)(2,1)S(1)}, u32[]{:S(2)}, u32[]{:S(2)}) collective-permute-start(bf16[1024,1024]{1,0:T(8,128)(2,1)S(1)} %get-tuple-element.70), channel_id=1, source_target_pairs={{0,1},{1,0},{2,3},{3,2},{4,5},{5,4},{6,7},{7,6},{8,9},{9,8},{10,11... | collective-permute-start | bytes 6291464 | tf_op jit(solution)/shard_map/ppermute | solution.py:202
  69.7 4.0 %collective-permute-start.14 = (bf16[512,1024]{1,0:T(8,128)(2,1)S(1)}, bf16[512,1024]{1,0:T(8,128)(2,1)S(1)}, u32[]{:S(2)}, u32[]{:S(2)}) collective-permute-start(bf16[512,1024]{1,0:T(8,128)(2,1)S(1)} %collective-permute-done.12.refs_0_), channel_id=1, source_target_pairs={{0,1},{1,0},{2,3},{3,2},{4,5},{5,4},{6,7},{7,6},{8,9},{9,8},{10,11... | collective-permute-start | bytes 3145736 | tf_op jit(solution)/shard_map/ppermute | solution.py:202
  73.7 2.1 %shard_map.119 = (f32[1024,1024]{1,0:T(8,128)S(1)}, f32[8,128]{1,0:T(8,128)S(1)}) custom-call(s32[32]{0:T(128)S(1)} %select_add_fusion.ids, f32[8,128]{1,0:T(8,128)S(1)} %get-tuple-element.58._, bf16[512,1024]{1,0:T(8,128)(2,1)S(1)} %collective-permute-done.12.refs_0_, ...), custom_call_target="tpu_custom_call", output_to_operand_aliasing={{0}: (4, {})} | custom-call | flops 1000 | bytes 1000 | tf_op jit(solution)/shard_map/pallas_call | solution.py:315
  76.0 3.5 %shard_map.120 = (f32[1024,1024]{1,0:T(8,128)S(1)}, f32[8,128]{1,0:T(8,128)S(1)}) custom-call(s32[32]{0:T(128)S(1)} %select_add_fusion.ids, f32[8,128]{1,0:T(8,128)S(1)} %get-tuple-element.63._, bf16[512,1024]{1,0:T(8,128)(2,1)S(1)} %collective-permute-done.14.refs_0_, ...), custom_call_target="tpu_custom_call", output_to_operand_aliasing={{0}: (5, {})} | custom-call | flops 1000 | bytes 1000 | tf_op jit(solution)/shard_map/pallas_call | solution.py:315
  79.5 3.2 %shard_map.121 = (bf16[1024,1024]{1,0:T(8,128)(2,1)}, f32[8,128]{1,0:T(8,128)}) custom-call(s32[32]{0:T(128)S(1)} %select_add_fusion.ids, f32[8,128]{1,0:T(8,128)S(1)} %get-tuple-element.67._, bf16[512,1024]{1,0:T(8,128)(2,1)S(1)} %collective-permute-done.15.refs_0_, bf16[1024,512]{1,0:T(8,128)(2,1)S(1)} %get-tuple-element.68.refs_1_, ...), custom_call_target="tpu_custom_call" | custom-call | flops 1000 | bytes 1000 | tf_op jit(solution)/shard_map/pallas_call | solution.py:315
  (44 shorter events, 4.4 us)
Async XLA Ops:
  0.6 33.2 %collective-permute-start.7 = (bf16[1024,8192]{1,0:T(8,128)(2,1)}, bf16[1024,8192]{1,0:T(8,128)(2,1)}, u32[]{:S(2)}, u32[]{:S(2)}) collective-permute-start(bf16[1024,8192]{1,0:T(8,128)(2,1)} %refs_2_.3), channel_id=1, source_target_pairs={{0,1},{1,0},{2,3},{3,2},{4,5},{5,4},{6,7},{7,6},{8,9},{9,8},{10,11... | collective-permute-start | bytes 50331656 | tf_op jit(solution)/shard_map/ppermute | solution.py:202
  2.1 11.2 %copy-start.2 = (f32[256,256]{1,0:T(8,128)S(1)}, f32[256,256]{1,0:T(8,128)}, u32[]{:S(2)}) copy-start(f32[256,256]{1,0:T(8,128)} %constant.31.clone.basis) | copy-start | bytes 786436
  2.1 11.2 %copy-start.3 = (bf16[256,1024]{1,0:T(8,128)(2,1)S(1)}, bf16[256,1024]{1,0:T(8,128)(2,1)}, u32[]{:S(2)}) copy-start(bf16[256,1024]{1,0:T(8,128)(2,1)} %weight.1) | copy-start | bytes 1572868
  2.1 18.6 %copy-start = (f32[1,256,1024]{2,1,0:T(8,128)S(1)}, f32[1,256,1024]{2,1,0:T(8,128)}, u32[]{:S(2)}) copy-start(f32[1,256,1024]{2,1,0:T(8,128)} %momentum.3) | copy-start | bytes 3145732
  2.1 18.6 %copy-start.1 = (f32[1,256,1024]{2,1,0:T(8,128)S(1)}, f32[1,256,1024]{2,1,0:T(8,128)}, u32[]{:S(2)}) copy-start(f32[1,256,1024]{2,1,0:T(8,128)} %grad.3) | copy-start | bytes 3145732
  6.5 19.5 %copy-start.5 = (s32[32]{0:T(128)S(1)}, s32[32]{0:T(128)}, u32[]{:S(2)}) copy-start(s32[32]{0:T(128)} %constant.32.clone) | copy-start | bytes 388
  6.5 19.4 %copy-start.6 = (s32[32]{0:T(128)S(1)}, s32[32]{0:T(128)}, u32[]{:S(2)}) copy-start(s32[32]{0:T(128)} %constant.33.clone) | copy-start | bytes 388
  6.5 19.4 %copy-start.7 = (pred[32]{0:T(512)(128)(4,1)S(1)}, pred[32]{0:T(512)(128)(4,1)}, u32[]{:S(2)}) copy-start(pred[32]{0:T(512)(128)(4,1)} %constant.34.clone) | copy-start | bytes 100
  6.5 6.8 %collective-permute-start = (f32[4,1024]{1,0:T(4,128)S(1)}, f32[4,1024]{1,0:T(4,128)S(1)}, u32[]{:S(2)}, u32[]{:S(2)}) collective-permute-start(f32[4,1024]{1,0:T(4,128)S(1)} %get-tuple-element.38.chosen0), channel_id=1, source_target_pairs={{0,32},{32,64},{64,96},{96,0},{1,33},{33,65},{65,97},{97,1},{2,34}... | collective-permute-start | bytes 49160 | tf_op jit(solution)/shard_map/ppermute | solution.py:356
  7.9 5.5 %collective-permute-start.1 = (f32[4,1024]{1,0:T(4,128)S(1)}, f32[4,1024]{1,0:T(4,128)S(1)}, u32[]{:S(2)}, u32[]{:S(2)}) collective-permute-start(f32[4,1024]{1,0:T(4,128)S(1)} %get-tuple-element.38.chosen0), channel_id=1, source_target_pairs={{0,64},{32,96},{64,0},{96,32},{1,65},{33,97},{65,1},{97,33},{2,66}... | collective-permute-start | bytes 49160 | tf_op jit(solution)/shard_map/ppermute | solution.py:356
  10.3 3.0 %collective-permute-start.2 = (f32[4,1024]{1,0:T(4,128)S(1)}, f32[4,1024]{1,0:T(4,128)S(1)}, u32[]{:S(2)}, u32[]{:S(2)}) collective-permute-start(f32[4,1024]{1,0:T(4,128)S(1)} %get-tuple-element.38.chosen0), channel_id=1, source_target_pairs={{0,96},{32,0},{64,32},{96,64},{1,97},{33,1},{65,33},{97,65},{2,98}... | collective-permute-start | bytes 49160 | tf_op jit(solution)/shard_map/ppermute | solution.py:356
  16.9 10.9 %collective-permute-start.3 = (bf16[256,1024]{1,0:T(8,128)(2,1)}, bf16[256,1024]{1,0:T(8,128)(2,1)S(1)}, u32[]{:S(2)}, u32[]{:S(2)}) collective-permute-start(bf16[256,1024]{1,0:T(8,128)(2,1)} %shard_map.114), channel_id=1, source_target_pairs={{0,8},{1,3},{2,10},{3,5},{4,12},{5,7},{6,14},{7,1},{8,16},{9,11},{... | collective-permute-start | bytes 1572872 | tf_op jit(solution)/shard_map/ppermute | solution.py:198
  18.6 9.3 %collective-permute-start.4 = (bf16[256,1024]{1,0:T(8,128)(2,1)}, bf16[256,1024]{1,0:T(8,128)(2,1)S(1)}, u32[]{:S(2)}, u32[]{:S(2)}) collective-permute-start(bf16[256,1024]{1,0:T(8,128)(2,1)} %shard_map.114), channel_id=1, source_target_pairs={{0,24},{1,7},{2,26},{3,1},{4,28},{5,3},{6,30},{7,5},{8,0},{9,15},{... | collective-permute-start | bytes 1572872 | tf_op jit(solution)/shard_map/ppermute | solution.py:198
  27.9 18.1 %collective-permute-start.9 = (bf16[512,1024]{1,0:T(8,128)(2,1)S(1)}, bf16[512,1024]{1,0:T(8,128)(2,1)S(1)}, u32[]{:S(2)}, u32[]{:S(2)}) collective-permute-start(bf16[512,1024]{1,0:T(8,128)(2,1)S(1)} %pad_maximum_fusion.refs_4_), channel_id=1, source_target_pairs={{0,2},{1,9},{2,4},{3,11},{4,6},{5,13},{6,0},{7,15},{8,10},{9,17},{... | collective-permute-start | bytes 3145736 | tf_op jit(solution)/shard_map/ppermute | solution.py:198
  29.0 17.0 %collective-permute-start.10 = (bf16[512,1024]{1,0:T(8,128)(2,1)S(1)}, bf16[512,1024]{1,0:T(8,128)(2,1)S(1)}, u32[]{:S(2)}, u32[]{:S(2)}) collective-permute-start(bf16[512,1024]{1,0:T(8,128)(2,1)S(1)} %pad_maximum_fusion.refs_4_), channel_id=1, source_target_pairs={{0,6},{1,25},{2,0},{3,27},{4,2},{5,29},{6,4},{7,31},{8,14},{9,1},{... | collective-permute-start | bytes 3145736 | tf_op jit(solution)/shard_map/ppermute | solution.py:198
  31.0 9.4 %collective-permute-start.5 = (bf16[128,1024]{1,0:T(8,128)(2,1)S(1)}, bf16[128,1024]{1,0:T(8,128)(2,1)S(1)}, u32[]{:S(2)}, u32[]{:S(2)}) collective-permute-start(bf16[128,1024]{1,0:T(8,128)(2,1)S(1)} %slice.6), channel_id=1, source_target_pairs={{0,8},{1,3},{2,10},{3,5},{4,12},{5,7},{6,14},{7,1},{8,16},{9,11},{... | collective-permute-start | bytes 786440 | tf_op jit(solution)/shard_map/ppermute | solution.py:198
  31.9 8.5 %collective-permute-start.6 = (bf16[128,1024]{1,0:T(8,128)(2,1)S(1)}, bf16[128,1024]{1,0:T(8,128)(2,1)S(1)}, u32[]{:S(2)}, u32[]{:S(2)}) collective-permute-start(bf16[128,1024]{1,0:T(8,128)(2,1)S(1)} %slice.7), channel_id=1, source_target_pairs={{0,24},{1,7},{2,26},{3,1},{4,28},{5,3},{6,30},{7,5},{8,0},{9,15},{... | collective-permute-start | bytes 786440 | tf_op jit(solution)/shard_map/ppermute | solution.py:198
  40.5 16.5 %collective-permute-start.8 = (bf16[512,1024]{1,0:T(8,128)(2,1)S(1)}, bf16[512,1024]{1,0:T(8,128)(2,1)S(1)}, u32[]{:S(2)}, u32[]{:S(2)}) collective-permute-start(bf16[512,1024]{1,0:T(8,128)(2,1)S(1)} %constant_dynamic-update-slice_fusion.refs_2_), channel_id=1, source_target_pairs={{0,6},{1,25},{2,0},{3,27},{4,2},{5,29},{6,4},{7,31},{8,14},{9,1},{... | collective-permute-start | bytes 3145736 | tf_op jit(solution)/shard_map/ppermute | solution.py:198
  41.3 18.9 %collective-permute-start.13 = (bf16[512,1024]{1,0:T(8,128)(2,1)S(1)}, bf16[512,1024]{1,0:T(8,128)(2,1)S(1)}, u32[]{:S(2)}, u32[]{:S(2)}) collective-permute-start(bf16[512,1024]{1,0:T(8,128)(2,1)S(1)} %constant_dynamic-update-slice_fusion.refs_2_), channel_id=1, source_target_pairs={{0,2},{1,9},{2,4},{3,11},{4,6},{5,13},{6,0},{7,15},{8,10},{9,17},{... | collective-permute-start | bytes 3145736 | tf_op jit(solution)/shard_map/ppermute | solution.py:198
  46.0 23.6 %collective-permute-start.12 = (bf16[512,1024]{1,0:T(8,128)(2,1)S(1)}, bf16[512,1024]{1,0:T(8,128)(2,1)S(1)}, u32[]{:S(2)}, u32[]{:S(2)}) collective-permute-start(bf16[512,1024]{1,0:T(8,128)(2,1)S(1)} %collective-permute-done.9.refs_3_), channel_id=1, source_target_pairs={{0,2},{1,9},{2,4},{3,11},{4,6},{5,13},{6,0},{7,15},{8,10},{9,17},{... | collective-permute-start | bytes 3145736 | tf_op jit(solution)/shard_map/ppermute | solution.py:198
  57.0 18.8 %collective-permute-start.11 = (bf16[512,1024]{1,0:T(8,128)(2,1)S(1)}, bf16[512,1024]{1,0:T(8,128)(2,1)S(1)}, u32[]{:S(2)}, u32[]{:S(2)}) collective-permute-start(bf16[512,1024]{1,0:T(8,128)(2,1)S(1)} %collective-permute-done.8.refs_4_), channel_id=1, source_target_pairs={{0,6},{1,25},{2,0},{3,27},{4,2},{5,29},{6,4},{7,31},{8,14},{9,1},{... | collective-permute-start | bytes 3145736 | tf_op jit(solution)/shard_map/ppermute | solution.py:198
  66.1 13.4 %collective-permute-start.16 = (bf16[1024,1024]{1,0:T(8,128)(2,1)S(1)}, bf16[1024,1024]{1,0:T(8,128)(2,1)S(1)}, u32[]{:S(2)}, u32[]{:S(2)}) collective-permute-start(bf16[1024,1024]{1,0:T(8,128)(2,1)S(1)} %get-tuple-element.70), channel_id=1, source_target_pairs={{0,1},{1,0},{2,3},{3,2},{4,5},{5,4},{6,7},{7,6},{8,9},{9,8},{10,11... | collective-permute-start | bytes 6291464 | tf_op jit(solution)/shard_map/ppermute | solution.py:202
  69.7 6.3 %collective-permute-start.14 = (bf16[512,1024]{1,0:T(8,128)(2,1)S(1)}, bf16[512,1024]{1,0:T(8,128)(2,1)S(1)}, u32[]{:S(2)}, u32[]{:S(2)}) collective-permute-start(bf16[512,1024]{1,0:T(8,128)(2,1)S(1)} %collective-permute-done.12.refs_0_), channel_id=1, source_target_pairs={{0,1},{1,0},{2,3},{3,2},{4,5},{5,4},{6,7},{7,6},{8,9},{9,8},{10,11... | collective-permute-start | bytes 3145736 | tf_op jit(solution)/shard_map/ppermute | solution.py:202
  75.8 3.7 %collective-permute-start.15 = (bf16[512,1024]{1,0:T(8,128)(2,1)S(1)}, bf16[512,1024]{1,0:T(8,128)(2,1)S(1)}, u32[]{:S(2)}, u32[]{:S(2)}) collective-permute-start(bf16[512,1024]{1,0:T(8,128)(2,1)S(1)} %collective-permute-done.11.refs_1_), channel_id=1, source_target_pairs={{0,1},{1,0},{2,3},{3,2},{4,5},{5,4},{6,7},{7,6},{8,9},{9,8},{10,11... | collective-permute-start | bytes 3145736 | tf_op jit(solution)/shard_map/ppermute | solution.py:202
  (1 other events, 10.9 us)

commit v6 on v5

--- a/solution.py
+++ b/solution.py
@@ -106,9 +106,10 @@
             span = slice(p - c, p - c + PAIR)
             for a in range(blocks):
                 rows = slice(a * GROUP, (a + 1) * GROUP)
-                left = jnp.concatenate([high[rows, span], low[rows, span]], axis=1)
+                left = jnp.concatenate([high[rows, span], low[rows, span]], axis=0)
                 right = one_hot(where[1, 0, a : a + 1, p : p + PAIR], PAIR)
-                found = jnp.dot(left, jnp.concatenate([right, right], axis=0), preferred_element_type=jnp.float32)
+                found = jnp.dot(left, right, preferred_element_type=jnp.float32)
+                found = found[:GROUP] + found[GROUP:]
                 kept = jnp.where(is_row(where[0, 0, a : a + 1, p : p + PAIR], GROUP), found, 0.0)
                 chosen[a : a + 1, p : p + PAIR] = jnp.sum(kept, axis=0, keepdims=True)
 

time: 83 us -> 83.1 us (level)
  no operation moved by 1% of the time
where the time goes in v6:
time: 83.1 us; the launch traced here: 82.9 us
  Pallas kernels  44.4 us (53%)
  starting transfers between devices  28.5 us (34%)
  waiting for transfers between devices  8.74 us (11%)
  between operations  1.04 us (1%)
    pallas_call x6, Pallas kernels, multiply(): pl.pallas_call(kernel, in_specs=[pl.BlockSpec(memory_space=pltpu.SMEM)] +...  29.5 us
    ppermute x10, starting transfers between devices, send(): return lax.ppermute(value, PLANE, ring(axis, step))  14.3 us
    ppermute x4, starting transfers between devices, sibling(): return lax.ppermute(value, 'core', [(0, 1), (1, 0)])  9.19 us
    ppermute x10, waiting for transfers between devices, send(): return lax.ppermute(value, PLANE, ring(axis, step))  8.7 us
    pallas_call x1, Pallas kernels, on_device(): pl.pallas_call(momentum_kernel, out_shape=jax.ShapeDtypeStruct(momentum.s...  5.23 us
    ppermute x3, starting transfers between devices, on_device(): lax.ppermute(chosen, 'x', [(i, (i + step) % REPS) for i in range(REPS)])  4.97 us
    pallas_call x1, Pallas kernels, on_device(): pl.pallas_call(coeff_kernel, out_shape=(jax.ShapeDtypeStruct((blocks, col...  4.34 us
    pallas_call x1, Pallas kernels, on_device(): pl.pallas_call(weight_kernel, out_shape=jax.ShapeDtypeStruct((rows, cols)...  3.53 us
  transfers between devices with their start and end apart: 17, of which 4 were waited for; matrix products, arithmetic and copies ran while one was open for 0% of the time, Pallas kernels for 50%

profile of v6, /device:TPU:1, one launch (start us, length us, event | category | flops | bytes accessed | tf_op | source)
XLA Modules:
  0.0 82.9 jit_solution(744254495304914632)
XLA Ops:
  0.6 1.5 %collective-permute-start.7 = (bf16[1024,8192]{1,0:T(8,128)(2,1)}, bf16[1024,8192]{1,0:T(8,128)(2,1)}, u32[]{:S(2)}, u32[]{:S(2)}) collective-permute-start(bf16[1024,8192]{1,0:T(8,128)(2,1)} %refs_2_.3), channel_id=1, source_target_pairs={{0,1},{1,0},{2,3},{3,2},{4,5},{5,4},{6,7},{7,6},{8,9},{9,8},{10,11... | collective-permute-start | bytes 50331656 | tf_op jit(solution)/shard_map/ppermute | solution.py:203
  2.1 4.3 %shard_map.112 = (f32[4,1024]{1,0:T(4,128)S(1)}, s32[2,1,8,1024]{3,2,1,0:T(8,128)S(1)}) custom-call(f32[1,256,1024]{2,1,0:T(8,128)} %momentum.3, f32[1,256,1024]{2,1,0:T(8,128)} %grad.3, s32[4,16,64,128]{3,2,1,0:T(8,128)} %bitcast.1, f32[256,256]{1,0:T(8,128)} %constant.31.clone.basis), custom_call_target="tpu_custom_call" | custom-call | flops 1000 | bytes 1000 | tf_op jit(solution)/shard_map/pallas_call | solution.py:339
  6.5 1.4 %collective-permute-start = (f32[4,1024]{1,0:T(4,128)S(1)}, f32[4,1024]{1,0:T(4,128)S(1)}, u32[]{:S(2)}, u32[]{:S(2)}) collective-permute-start(f32[4,1024]{1,0:T(4,128)S(1)} %get-tuple-element.38.chosen0), channel_id=1, source_target_pairs={{0,32},{32,64},{64,96},{96,0},{1,33},{33,65},{65,97},{97,1},{2,34}... | collective-permute-start | bytes 49160 | tf_op jit(solution)/shard_map/ppermute | solution.py:357
  7.9 2.4 %collective-permute-start.1 = (f32[4,1024]{1,0:T(4,128)S(1)}, f32[4,1024]{1,0:T(4,128)S(1)}, u32[]{:S(2)}, u32[]{:S(2)}) collective-permute-start(f32[4,1024]{1,0:T(4,128)S(1)} %get-tuple-element.38.chosen0), channel_id=1, source_target_pairs={{0,64},{32,96},{64,0},{96,32},{1,65},{33,97},{65,1},{97,33},{2,66}... | collective-permute-start | bytes 49160 | tf_op jit(solution)/shard_map/ppermute | solution.py:357
  10.3 1.2 %collective-permute-start.2 = (f32[4,1024]{1,0:T(4,128)S(1)}, f32[4,1024]{1,0:T(4,128)S(1)}, u32[]{:S(2)}, u32[]{:S(2)}) collective-permute-start(f32[4,1024]{1,0:T(4,128)S(1)} %get-tuple-element.38.chosen0), channel_id=1, source_target_pairs={{0,96},{32,0},{64,32},{96,64},{1,97},{33,1},{65,33},{97,65},{2,98}... | collective-permute-start | bytes 49160 | tf_op jit(solution)/shard_map/ppermute | solution.py:357
  11.5 1.8 %shard_map.113.others = s32[2,3,8,1024]{3,2,1,0:T(8,128)S(1)} custom-call(s32[4,16,64,128]{3,2,1,0:T(8,128)} %bitcast.2), custom_call_target="tpu_custom_call" | custom-call | flops 1000 | bytes 1000 | tf_op jit(solution)/shard_map/pallas_call | solution.py:359
  13.4 3.5 %shard_map.114 = bf16[256,1024]{1,0:T(8,128)(2,1)} custom-call(bf16[256,1024]{1,0:T(8,128)(2,1)S(1)} %copy-done.3, f32[4,1024]{1,0:T(4,128)S(1)} %get-tuple-element.38.chosen0, f32[4,1024]{1,0:T(4,128)S(1)} %collective-permute-done.chosen1, f32[4,1024]{1,0:T(4,128)S(1)} %collective-permute-done.1.chosen2, f32[4,1024]{1,0:T(4,128)S(1)} %collective-permute-done.2.chosen3, ...), custom_call_target="tpu_custom_call" | custom-call | flops 1000 | bytes 1000 | tf_op jit(solution)/shard_map/pallas_call | solution.py:369
  16.9 1.6 %collective-permute-start.3 = (bf16[256,1024]{1,0:T(8,128)(2,1)}, bf16[256,1024]{1,0:T(8,128)(2,1)S(1)}, u32[]{:S(2)}, u32[]{:S(2)}) collective-permute-start(bf16[256,1024]{1,0:T(8,128)(2,1)} %shard_map.114), channel_id=1, source_target_pairs={{0,8},{1,3},{2,10},{3,5},{4,12},{5,7},{6,14},{7,1},{8,16},{9,11},{... | collective-permute-start | bytes 1572872 | tf_op jit(solution)/shard_map/ppermute | solution.py:199
  18.6 2.1 %collective-permute-start.4 = (bf16[256,1024]{1,0:T(8,128)(2,1)}, bf16[256,1024]{1,0:T(8,128)(2,1)S(1)}, u32[]{:S(2)}, u32[]{:S(2)}) collective-permute-start(bf16[256,1024]{1,0:T(8,128)(2,1)} %shard_map.114), channel_id=1, source_target_pairs={{0,24},{1,7},{2,26},{3,1},{4,28},{5,3},{6,30},{7,5},{8,0},{9,15},{... | collective-permute-start | bytes 1572872 | tf_op jit(solution)/shard_map/ppermute | solution.py:199
  20.7 5.2 %shard_map.115 = f32[1,256,1024]{2,1,0:T(8,128)} custom-call(f32[1,256,1024]{2,1,0:T(8,128)S(1)} %copy-done, f32[1,256,1024]{2,1,0:T(8,128)S(1)} %copy-done.1, s32[2,1,8,1024]{3,2,1,0:T(8,128)S(1)} %get-tuple-element.39.where, f32[256,256]{1,0:T(8,128)S(1)} %copy-done.2), custom_call_target="tpu_custom_call" | custom-call | flops 1000 | bytes 1000 | tf_op jit(solution)/shard_map/pallas_call | solution.py:381
  26.0 1.9 %collective-permute-done.3 = bf16[256,1024]{1,0:T(8,128)(2,1)S(1)} collective-permute-done((bf16[256,1024]{1,0:T(8,128)(2,1)}, bf16[256,1024]{1,0:T(8,128)(2,1)S(1)}, u32[]{:S(2)}, u32[]{:S(2)}) %collective-permute-start.3) | collective-permute-done | bytes 524320 | tf_op jit(solution)/shard_map/ppermute | solution.py:199
  29.0 2.0 %collective-permute-start.10 = (bf16[512,1024]{1,0:T(8,128)(2,1)S(1)}, bf16[512,1024]{1,0:T(8,128)(2,1)S(1)}, u32[]{:S(2)}, u32[]{:S(2)}) collective-permute-start(bf16[512,1024]{1,0:T(8,128)(2,1)S(1)} %pad_maximum_fusion.refs_4_), channel_id=1, source_target_pairs={{0,6},{1,25},{2,0},{3,27},{4,2},{5,29},{6,4},{7,31},{8,14},{9,1},{... | collective-permute-start | bytes 3145736 | tf_op jit(solution)/shard_map/ppermute | solution.py:199
  32.0 1.8 %collective-permute-start.6 = (bf16[128,1024]{1,0:T(8,128)(2,1)S(1)}, bf16[128,1024]{1,0:T(8,128)(2,1)S(1)}, u32[]{:S(2)}, u32[]{:S(2)}) collective-permute-start(bf16[128,1024]{1,0:T(8,128)(2,1)S(1)} %slice.7), channel_id=1, source_target_pairs={{0,24},{1,7},{2,26},{3,1},{4,28},{5,3},{6,30},{7,5},{8,0},{9,15},{... | collective-permute-start | bytes 786440 | tf_op jit(solution)/shard_map/ppermute | solution.py:199
  33.9 6.1 %shard_map.116 = (f32[1024,1024]{1,0:T(8,128)S(1)}, f32[1024,1024]{1,0:T(8,128)S(1)}, bf16[1024,1536]{1,0:T(8,128)(2,1)S(1)}, bf16[1024,1536]{1,0:T(8,128)(2,1)S(1)}, f32[8,128]{1,0:T(8,128)S(1)}) custom-call(s32[32]{0:T(128)S(1)} %select_add_fusion.ids, f32[8,128]{1,0:T(8,128)S(1)} %broadcast_in_dim.13._, bf16[1024,8192]{1,0:T(8,128)(2,1)} %refs_2_.3, ...), custom_call_target="tpu_custom_call" | custom-call | flops 10000000000 | bytes 1000 | tf_op jit(solution)/shard_map/pallas_call | solution.py:316
  42.1 4.0 %collective-permute-done.9.refs_3_ = bf16[512,1024]{1,0:T(8,128)(2,1)S(1)} collective-permute-done((bf16[512,1024]{1,0:T(8,128)(2,1)S(1)}, bf16[512,1024]{1,0:T(8,128)(2,1)S(1)}, u32[]{:S(2)}, u32[]{:S(2)}) %collective-permute-start.9) | collective-permute-done | bytes 1048608 | tf_op jit(solution)/shard_map/ppermute | solution.py:199
  46.1 8.7 %shard_map.117 = (f32[1024,1024]{1,0:T(8,128)S(1)}, f32[1024,1024]{1,0:T(8,128)S(1)}, bf16[1024,1024]{1,0:T(8,128)(2,1)S(1)}, bf16[1024,1024]{1,0:T(8,128)(2,1)S(1)}, f32[8,128]{1,0:T(8,128)S(1)}) custom-call(s32[32]{0:T(128)S(1)} %select_add_fusion.ids, f32[8,128]{1,0:T(8,128)S(1)} %get-tuple-element.45._, ...), custom_call_target="tpu_custom_call", output_to_operand_aliasing={{0}: (9, {}), {1}: (10, {})} | custom-call | flops 1000 | bytes 1000 | tf_op jit(solution)/shard_map/pallas_call | solution.py:316
  54.7 2.3 %collective-permute-done.8.refs_4_ = bf16[512,1024]{1,0:T(8,128)(2,1)S(1)} collective-permute-done((bf16[512,1024]{1,0:T(8,128)(2,1)S(1)}, bf16[512,1024]{1,0:T(8,128)(2,1)S(1)}, u32[]{:S(2)}, u32[]{:S(2)}) %collective-permute-start.8) | collective-permute-done | bytes 1048608 | tf_op jit(solution)/shard_map/ppermute | solution.py:199
  57.0 3.2 %collective-permute-start.11 = (bf16[512,1024]{1,0:T(8,128)(2,1)S(1)}, bf16[512,1024]{1,0:T(8,128)(2,1)S(1)}, u32[]{:S(2)}, u32[]{:S(2)}) collective-permute-start(bf16[512,1024]{1,0:T(8,128)(2,1)S(1)} %collective-permute-done.8.refs_4_), channel_id=1, source_target_pairs={{0,6},{1,25},{2,0},{3,27},{4,2},{5,29},{6,4},{7,31},{8,14},{9,1},{... | collective-permute-start | bytes 3145736 | tf_op jit(solution)/shard_map/ppermute | solution.py:199
  60.2 5.9 %shard_map.118 = (f32[1024,1024]{1,0:T(8,128)S(1)}, bf16[1024,1024]{1,0:T(8,128)(2,1)S(1)}, bf16[1024,512]{1,0:T(8,128)(2,1)S(1)}, bf16[1024,1024]{1,0:T(8,128)(...) custom-call(s32[32]{0:T(128)S(1)} %select_add_fusion.ids, ...), custom_call_target="tpu_custom_call", output_to_operand_aliasing={{0}: (9, {})} | custom-call | flops 1000 | bytes 1000 | tf_op jit(solution)/shard_map/pallas_call | solution.py:316
  66.2 3.5 %collective-permute-start.16 = (bf16[1024,1024]{1,0:T(8,128)(2,1)S(1)}, bf16[1024,1024]{1,0:T(8,128)(2,1)S(1)}, u32[]{:S(2)}, u32[]{:S(2)}) collective-permute-start(bf16[1024,1024]{1,0:T(8,128)(2,1)S(1)} %get-tuple-element.70), channel_id=1, source_target_pairs={{0,1},{1,0},{2,3},{3,2},{4,5},{5,4},{6,7},{7,6},{8,9},{9,8},{10,11... | collective-permute-start | bytes 6291464 | tf_op jit(solution)/shard_map/ppermute | solution.py:203
  69.7 4.0 %collective-permute-start.14 = (bf16[512,1024]{1,0:T(8,128)(2,1)S(1)}, bf16[512,1024]{1,0:T(8,128)(2,1)S(1)}, u32[]{:S(2)}, u32[]{:S(2)}) collective-permute-start(bf16[512,1024]{1,0:T(8,128)(2,1)S(1)} %collective-permute-done.12.refs_0_), channel_id=1, source_target_pairs={{0,1},{1,0},{2,3},{3,2},{4,5},{5,4},{6,7},{7,6},{8,9},{9,8},{10,11... | collective-permute-start | bytes 3145736 | tf_op jit(solution)/shard_map/ppermute | solution.py:203
  73.7 2.1 %shard_map.119 = (f32[1024,1024]{1,0:T(8,128)S(1)}, f32[8,128]{1,0:T(8,128)S(1)}) custom-call(s32[32]{0:T(128)S(1)} %select_add_fusion.ids, f32[8,128]{1,0:T(8,128)S(1)} %get-tuple-element.58._, bf16[512,1024]{1,0:T(8,128)(2,1)S(1)} %collective-permute-done.12.refs_0_, ...), custom_call_target="tpu_custom_call", output_to_operand_aliasing={{0}: (4, {})} | custom-call | flops 1000 | bytes 1000 | tf_op jit(solution)/shard_map/pallas_call | solution.py:316
  76.0 3.5 %shard_map.120 = (f32[1024,1024]{1,0:T(8,128)S(1)}, f32[8,128]{1,0:T(8,128)S(1)}) custom-call(s32[32]{0:T(128)S(1)} %select_add_fusion.ids, f32[8,128]{1,0:T(8,128)S(1)} %get-tuple-element.63._, bf16[512,1024]{1,0:T(8,128)(2,1)S(1)} %collective-permute-done.14.refs_0_, ...), custom_call_target="tpu_custom_call", output_to_operand_aliasing={{0}: (5, {})} | custom-call | flops 1000 | bytes 1000 | tf_op jit(solution)/shard_map/pallas_call | solution.py:316
  79.6 3.2 %shard_map.121 = (bf16[1024,1024]{1,0:T(8,128)(2,1)}, f32[8,128]{1,0:T(8,128)}) custom-call(s32[32]{0:T(128)S(1)} %select_add_fusion.ids, f32[8,128]{1,0:T(8,128)S(1)} %get-tuple-element.67._, bf16[512,1024]{1,0:T(8,128)(2,1)S(1)} %collective-permute-done.15.refs_0_, bf16[1024,512]{1,0:T(8,128)(2,1)S(1)} %get-tuple-element.68.refs_1_, ...), custom_call_target="tpu_custom_call" | custom-call | flops 1000 | bytes 1000 | tf_op jit(solution)/shard_map/pallas_call | solution.py:316
  (44 shorter events, 4.4 us)
Async XLA Ops:
  0.6 33.2 %collective-permute-start.7 = (bf16[1024,8192]{1,0:T(8,128)(2,1)}, bf16[1024,8192]{1,0:T(8,128)(2,1)}, u32[]{:S(2)}, u32[]{:S(2)}) collective-permute-start(bf16[1024,8192]{1,0:T(8,128)(2,1)} %refs_2_.3), channel_id=1, source_target_pairs={{0,1},{1,0},{2,3},{3,2},{4,5},{5,4},{6,7},{7,6},{8,9},{9,8},{10,11... | collective-permute-start | bytes 50331656 | tf_op jit(solution)/shard_map/ppermute | solution.py:203
  2.1 11.2 %copy-start.2 = (f32[256,256]{1,0:T(8,128)S(1)}, f32[256,256]{1,0:T(8,128)}, u32[]{:S(2)}) copy-start(f32[256,256]{1,0:T(8,128)} %constant.31.clone.basis) | copy-start | bytes 786436
  2.1 11.3 %copy-start.3 = (bf16[256,1024]{1,0:T(8,128)(2,1)S(1)}, bf16[256,1024]{1,0:T(8,128)(2,1)}, u32[]{:S(2)}) copy-start(bf16[256,1024]{1,0:T(8,128)(2,1)} %weight.1) | copy-start | bytes 1572868
  2.1 18.6 %copy-start = (f32[1,256,1024]{2,1,0:T(8,128)S(1)}, f32[1,256,1024]{2,1,0:T(8,128)}, u32[]{:S(2)}) copy-start(f32[1,256,1024]{2,1,0:T(8,128)} %momentum.3) | copy-start | bytes 3145732
  2.1 18.6 %copy-start.1 = (f32[1,256,1024]{2,1,0:T(8,128)S(1)}, f32[1,256,1024]{2,1,0:T(8,128)}, u32[]{:S(2)}) copy-start(f32[1,256,1024]{2,1,0:T(8,128)} %grad.3) | copy-start | bytes 3145732
  6.5 19.4 %copy-start.5 = (s32[32]{0:T(128)S(1)}, s32[32]{0:T(128)}, u32[]{:S(2)}) copy-start(s32[32]{0:T(128)} %constant.32.clone) | copy-start | bytes 388
  6.5 19.4 %copy-start.6 = (s32[32]{0:T(128)S(1)}, s32[32]{0:T(128)}, u32[]{:S(2)}) copy-start(s32[32]{0:T(128)} %constant.33.clone) | copy-start | bytes 388
  6.5 19.4 %copy-start.7 = (pred[32]{0:T(512)(128)(4,1)S(1)}, pred[32]{0:T(512)(128)(4,1)}, u32[]{:S(2)}) copy-start(pred[32]{0:T(512)(128)(4,1)} %constant.34.clone) | copy-start | bytes 100
  6.5 6.8 %collective-permute-start = (f32[4,1024]{1,0:T(4,128)S(1)}, f32[4,1024]{1,0:T(4,128)S(1)}, u32[]{:S(2)}, u32[]{:S(2)}) collective-permute-start(f32[4,1024]{1,0:T(4,128)S(1)} %get-tuple-element.38.chosen0), channel_id=1, source_target_pairs={{0,32},{32,64},{64,96},{96,0},{1,33},{33,65},{65,97},{97,1},{2,34}... | collective-permute-start | bytes 49160 | tf_op jit(solution)/shard_map/ppermute | solution.py:357
  7.9 5.5 %collective-permute-start.1 = (f32[4,1024]{1,0:T(4,128)S(1)}, f32[4,1024]{1,0:T(4,128)S(1)}, u32[]{:S(2)}, u32[]{:S(2)}) collective-permute-start(f32[4,1024]{1,0:T(4,128)S(1)} %get-tuple-element.38.chosen0), channel_id=1, source_target_pairs={{0,64},{32,96},{64,0},{96,32},{1,65},{33,97},{65,1},{97,33},{2,66}... | collective-permute-start | bytes 49160 | tf_op jit(solution)/shard_map/ppermute | solution.py:357
  10.3 3.0 %collective-permute-start.2 = (f32[4,1024]{1,0:T(4,128)S(1)}, f32[4,1024]{1,0:T(4,128)S(1)}, u32[]{:S(2)}, u32[]{:S(2)}) collective-permute-start(f32[4,1024]{1,0:T(4,128)S(1)} %get-tuple-element.38.chosen0), channel_id=1, source_target_pairs={{0,96},{32,0},{64,32},{96,64},{1,97},{33,1},{65,33},{97,65},{2,98}... | collective-permute-start | bytes 49160 | tf_op jit(solution)/shard_map/ppermute | solution.py:357
  16.9 10.9 %collective-permute-start.3 = (bf16[256,1024]{1,0:T(8,128)(2,1)}, bf16[256,1024]{1,0:T(8,128)(2,1)S(1)}, u32[]{:S(2)}, u32[]{:S(2)}) collective-permute-start(bf16[256,1024]{1,0:T(8,128)(2,1)} %shard_map.114), channel_id=1, source_target_pairs={{0,8},{1,3},{2,10},{3,5},{4,12},{5,7},{6,14},{7,1},{8,16},{9,11},{... | collective-permute-start | bytes 1572872 | tf_op jit(solution)/shard_map/ppermute | solution.py:199
  18.6 9.3 %collective-permute-start.4 = (bf16[256,1024]{1,0:T(8,128)(2,1)}, bf16[256,1024]{1,0:T(8,128)(2,1)S(1)}, u32[]{:S(2)}, u32[]{:S(2)}) collective-permute-start(bf16[256,1024]{1,0:T(8,128)(2,1)} %shard_map.114), channel_id=1, source_target_pairs={{0,24},{1,7},{2,26},{3,1},{4,28},{5,3},{6,30},{7,5},{8,0},{9,15},{... | collective-permute-start | bytes 1572872 | tf_op jit(solution)/shard_map/ppermute | solution.py:199
  28.0 18.1 %collective-permute-start.9 = (bf16[512,1024]{1,0:T(8,128)(2,1)S(1)}, bf16[512,1024]{1,0:T(8,128)(2,1)S(1)}, u32[]{:S(2)}, u32[]{:S(2)}) collective-permute-start(bf16[512,1024]{1,0:T(8,128)(2,1)S(1)} %pad_maximum_fusion.refs_4_), channel_id=1, source_target_pairs={{0,2},{1,9},{2,4},{3,11},{4,6},{5,13},{6,0},{7,15},{8,10},{9,17},{... | collective-permute-start | bytes 3145736 | tf_op jit(solution)/shard_map/ppermute | solution.py:199
  29.0 17.0 %collective-permute-start.10 = (bf16[512,1024]{1,0:T(8,128)(2,1)S(1)}, bf16[512,1024]{1,0:T(8,128)(2,1)S(1)}, u32[]{:S(2)}, u32[]{:S(2)}) collective-permute-start(bf16[512,1024]{1,0:T(8,128)(2,1)S(1)} %pad_maximum_fusion.refs_4_), channel_id=1, source_target_pairs={{0,6},{1,25},{2,0},{3,27},{4,2},{5,29},{6,4},{7,31},{8,14},{9,1},{... | collective-permute-start | bytes 3145736 | tf_op jit(solution)/shard_map/ppermute | solution.py:199
  31.0 9.4 %collective-permute-start.5 = (bf16[128,1024]{1,0:T(8,128)(2,1)S(1)}, bf16[128,1024]{1,0:T(8,128)(2,1)S(1)}, u32[]{:S(2)}, u32[]{:S(2)}) collective-permute-start(bf16[128,1024]{1,0:T(8,128)(2,1)S(1)} %slice.6), channel_id=1, source_target_pairs={{0,8},{1,3},{2,10},{3,5},{4,12},{5,7},{6,14},{7,1},{8,16},{9,11},{... | collective-permute-start | bytes 786440 | tf_op jit(solution)/shard_map/ppermute | solution.py:199
  32.0 8.5 %collective-permute-start.6 = (bf16[128,1024]{1,0:T(8,128)(2,1)S(1)}, bf16[128,1024]{1,0:T(8,128)(2,1)S(1)}, u32[]{:S(2)}, u32[]{:S(2)}) collective-permute-start(bf16[128,1024]{1,0:T(8,128)(2,1)S(1)} %slice.7), channel_id=1, source_target_pairs={{0,24},{1,7},{2,26},{3,1},{4,28},{5,3},{6,30},{7,5},{8,0},{9,15},{... | collective-permute-start | bytes 786440 | tf_op jit(solution)/shard_map/ppermute | solution.py:199
  40.5 16.5 %collective-permute-start.8 = (bf16[512,1024]{1,0:T(8,128)(2,1)S(1)}, bf16[512,1024]{1,0:T(8,128)(2,1)S(1)}, u32[]{:S(2)}, u32[]{:S(2)}) collective-permute-start(bf16[512,1024]{1,0:T(8,128)(2,1)S(1)} %constant_dynamic-update-slice_fusion.refs_2_), channel_id=1, source_target_pairs={{0,6},{1,25},{2,0},{3,27},{4,2},{5,29},{6,4},{7,31},{8,14},{9,1},{... | collective-permute-start | bytes 3145736 | tf_op jit(solution)/shard_map/ppermute | solution.py:199
  41.3 18.9 %collective-permute-start.13 = (bf16[512,1024]{1,0:T(8,128)(2,1)S(1)}, bf16[512,1024]{1,0:T(8,128)(2,1)S(1)}, u32[]{:S(2)}, u32[]{:S(2)}) collective-permute-start(bf16[512,1024]{1,0:T(8,128)(2,1)S(1)} %constant_dynamic-update-slice_fusion.refs_2_), channel_id=1, source_target_pairs={{0,2},{1,9},{2,4},{3,11},{4,6},{5,13},{6,0},{7,15},{8,10},{9,17},{... | collective-permute-start | bytes 3145736 | tf_op jit(solution)/shard_map/ppermute | solution.py:199
  46.1 23.6 %collective-permute-start.12 = (bf16[512,1024]{1,0:T(8,128)(2,1)S(1)}, bf16[512,1024]{1,0:T(8,128)(2,1)S(1)}, u32[]{:S(2)}, u32[]{:S(2)}) collective-permute-start(bf16[512,1024]{1,0:T(8,128)(2,1)S(1)} %collective-permute-done.9.refs_3_), channel_id=1, source_target_pairs={{0,2},{1,9},{2,4},{3,11},{4,6},{5,13},{6,0},{7,15},{8,10},{9,17},{... | collective-permute-start | bytes 3145736 | tf_op jit(solution)/shard_map/ppermute | solution.py:199
  57.0 18.8 %collective-permute-start.11 = (bf16[512,1024]{1,0:T(8,128)(2,1)S(1)}, bf16[512,1024]{1,0:T(8,128)(2,1)S(1)}, u32[]{:S(2)}, u32[]{:S(2)}) collective-permute-start(bf16[512,1024]{1,0:T(8,128)(2,1)S(1)} %collective-permute-done.8.refs_4_), channel_id=1, source_target_pairs={{0,6},{1,25},{2,0},{3,27},{4,2},{5,29},{6,4},{7,31},{8,14},{9,1},{... | collective-permute-start | bytes 3145736 | tf_op jit(solution)/shard_map/ppermute | solution.py:199
  66.2 13.4 %collective-permute-start.16 = (bf16[1024,1024]{1,0:T(8,128)(2,1)S(1)}, bf16[1024,1024]{1,0:T(8,128)(2,1)S(1)}, u32[]{:S(2)}, u32[]{:S(2)}) collective-permute-start(bf16[1024,1024]{1,0:T(8,128)(2,1)S(1)} %get-tuple-element.70), channel_id=1, source_target_pairs={{0,1},{1,0},{2,3},{3,2},{4,5},{5,4},{6,7},{7,6},{8,9},{9,8},{10,11... | collective-permute-start | bytes 6291464 | tf_op jit(solution)/shard_map/ppermute | solution.py:203
  69.7 6.3 %collective-permute-start.14 = (bf16[512,1024]{1,0:T(8,128)(2,1)S(1)}, bf16[512,1024]{1,0:T(8,128)(2,1)S(1)}, u32[]{:S(2)}, u32[]{:S(2)}) collective-permute-start(bf16[512,1024]{1,0:T(8,128)(2,1)S(1)} %collective-permute-done.12.refs_0_), channel_id=1, source_target_pairs={{0,1},{1,0},{2,3},{3,2},{4,5},{5,4},{6,7},{7,6},{8,9},{9,8},{10,11... | collective-permute-start | bytes 3145736 | tf_op jit(solution)/shard_map/ppermute | solution.py:203
  75.9 3.7 %collective-permute-start.15 = (bf16[512,1024]{1,0:T(8,128)(2,1)S(1)}, bf16[512,1024]{1,0:T(8,128)(2,1)S(1)}, u32[]{:S(2)}, u32[]{:S(2)}) collective-permute-start(bf16[512,1024]{1,0:T(8,128)(2,1)S(1)} %collective-permute-done.11.refs_1_), channel_id=1, source_target_pairs={{0,1},{1,0},{2,3},{3,2},{4,5},{5,4},{6,7},{7,6},{8,9},{9,8},{10,11... | collective-permute-start | bytes 3145736 | tf_op jit(solution)/shard_map/ppermute | solution.py:203
  (1 other events, 10.9 us)
